TPU v7x, 32 devices: a whole 2x2x4 slice. The times are simulated.
32 devices in a mesh: tm: 4 (over y, x), rows: 8 (over z, core).
Axes of the slice: x: 2, y: 2, z: 4, core: 2. Of those that a mesh axis runs over, the one named last changes fastest.
Arguments:
- queries: bfloat16 [16, 64, 16, 1792], P('tm', 'rows'), may hold values from -60 to 60
- keys: bfloat16 [16, 64, 16, 1792], P('tm', 'rows'), may hold values from -6 to 6
- values: bfloat16 [16, 64, 16, 1792], P('tm', 'rows'), may hold values from -6 to 6
- out_grad: bfloat16 [16, 64, 16, 1792], P('tm', 'rows'), may hold values from -6 to 6
Outputs:
- query_grad: bfloat16 [16, 64, 16, 1792], P('tm', 'rows')
- key_grad: bfloat16 [16, 64, 16, 1792], P('tm', 'rows')
- value_grad: bfloat16 [16, 64, 16, 1792], P('tm', 'rows')
All inputs are finite; a program needn't handle non-finite values.
Results may differ from a plain program's by a relative error of at most 0.012.
Values may be sent and summed in bfloat16 or wider, within the bound.
No kernel may reach another device: no remote copies, remote signals or barrier semaphores. Data moves between devices by JAX's collectives and lax.ppermute only.
A program may use at most 128 MiB of HBM per device.

v0:
```python
import math

import jax
import jax.numpy as jnp
from jax import lax
from jax.sharding import PartitionSpec as P

WW = 8
HEADS = 14
HEAD_DIM = 128


def passed_along(value, axis, by):
    size = lax.axis_size(axis)
    return lax.ppermute(value, axis, [(i, (i + by) % size) for i in range(size)])


def window_grads(query_w, key_w, value_w, grad_w):
    factor = 1.0 / math.sqrt(query_w.shape[-1])
    scores = (
        jnp.einsum("bhqd,bhkd->bhqk", query_w, key_w, preferred_element_type=jnp.float32) * factor
    )
    weights = jax.nn.softmax(scores, axis=-1)
    weights_b = weights.astype(jnp.bfloat16)
    attended = jnp.einsum("bhqk,bhkd->bhqd", weights_b, value_w, preferred_element_type=jnp.float32)
    row_dot = jnp.sum(grad_w.astype(jnp.float32) * attended, axis=-1, keepdims=True)
    weight_grad = jnp.einsum("bhqd,bhkd->bhqk", grad_w, value_w, preferred_element_type=jnp.float32)
    score_grad = (weights * (weight_grad - row_dot) * factor).astype(jnp.bfloat16)
    value_out = jnp.einsum(
        "bhqk,bhqd->bhkd", weights_b, grad_w, preferred_element_type=jnp.float32
    ).astype(jnp.bfloat16)
    query_out = jnp.einsum(
        "bhqk,bhkd->bhqd", score_grad, key_w, preferred_element_type=jnp.float32
    ).astype(jnp.bfloat16)
    key_out = jnp.einsum(
        "bhqk,bhqd->bhkd", score_grad, query_w, preferred_element_type=jnp.float32
    ).astype(jnp.bfloat16)
    return jnp.stack((query_out, key_out, value_out))


def forward_route(stacked):
    half_time = stacked.shape[1] // 2
    half_rows = stacked.shape[2] // 2
    row_slab = passed_along(stacked[:, :, :half_rows], "rows", -1)
    time_slab = passed_along(stacked[:, :half_time, half_rows:], "tm", -1)
    corner = passed_along(row_slab[:, :half_time], "tm", -1)
    top_half = jnp.concatenate(
        (stacked[:, half_time:, half_rows:], row_slab[:, half_time:]), axis=2
    )
    bottom_half = jnp.concatenate((time_slab, corner), axis=2)
    return jnp.concatenate((top_half, bottom_half), axis=1)


def backward_route(grads):
    half_time = grads.shape[1] // 2
    half_rows = grads.shape[2] // 2
    row_slab = passed_along(grads[:, :, half_rows:], "rows", 1)
    time_slab = passed_along(grads[:, half_time:, :half_rows], "tm", 1)
    corner = passed_along(row_slab[:, half_time:], "tm", 1)
    top_half = jnp.concatenate((corner, time_slab), axis=2)
    bottom_half = jnp.concatenate(
        (row_slab[:, :half_time], grads[:, :half_time, :half_rows]), axis=2
    )
    return jnp.concatenate((top_half, bottom_half), axis=1)


def shards(queries, keys, values, out_grad):
    stacked = jnp.stack((queries, keys, values, out_grad))
    shifted = forward_route(stacked)
    rolled = jnp.roll(shifted, -(WW // 2), axis=3)
    groups, frames, rows_here, columns, features = rolled.shape
    window_count = columns // WW
    length = frames * rows_here * WW
    windowed = rolled.reshape(groups, frames, rows_here, window_count, WW, HEADS, HEAD_DIM)
    windowed = windowed.transpose(0, 3, 5, 1, 2, 4, 6).reshape(
        groups, window_count, HEADS, length, HEAD_DIM
    )
    grads = window_grads(windowed[0], windowed[1], windowed[2], windowed[3])
    restored = grads.reshape(3, window_count, HEADS, frames, rows_here, WW, HEAD_DIM)
    restored = restored.transpose(0, 3, 4, 1, 5, 2, 6).reshape(
        3, frames, rows_here, columns, features
    )
    restored = jnp.roll(restored, WW // 2, axis=3)
    unshifted = backward_route(restored)
    return (unshifted[0], unshifted[1], unshifted[2])


def solution(mesh):
    return jax.shard_map(
        shards,
        mesh=mesh,
        in_specs=(
            P("tm", "rows", None, None),
            P("tm", "rows", None, None),
            P("tm", "rows", None, None),
            P("tm", "rows", None, None),
        ),
        out_specs=(
            P("tm", "rows", None, None),
            P("tm", "rows", None, None),
            P("tm", "rows", None, None),
        ),
        check_vma=False,
    )
```

profile of v0, /device:TPU:0, one launch (start us, length us, event | category | flops | bytes accessed | tf_op | source)
XLA Modules:
  0.0 208.0 jit_solution(2484511782098327271)
XLA Ops:
  0.6 4.0 %pad_maximum_fusion.8 = bf16[4,4,8,16,1792]{4,3,2,1,0:T(8,128)(2,1)S(1)} fusion(bf16[1,4,8,16,1792]{4,3,2,1,0:T(8,128)(2,1)} %bitcast.45, bf16[1,4,8,16,1792]{4,3,2,1,0:T(8,128)(2,1)} %bitcast.49, bf16[1,4,8,16,1792]{4,3,2,1,0:T(8,128)(2,1)} %bitcast.53, bf16[1,4,8,16,1792]{4,3,2,1,0:T(8,128)(2,1)} %bitcast.57), kind=kLoop, calls=%fused_computation.14 | loop fusion | flops 11010048 | bytes 14680064 | tf_op jit(solution)/shard_map/stack | solution.py:68
  4.7 0.0 copy-start
  4.7 0.0 copy-start.1
  4.7 0.0 copy-start.2
  4.7 0.0 copy-start.3
  4.7 0.3 slice.92
  5.1 4.5 %collective-permute-start = (bf16[4,4,4,16,1792]{4,3,2,1,0:T(8,128)(2,1)S(1)}, bf16[4,4,4,16,1792]{4,3,2,1,0:T(8,128)(2,1)S(1)}, u32[]{:S(2)}, u32[]{:S(2)}) collective-permute-start(bf16[4,4,4,16,1792]{4,3,2,1,0:T(8,128)(2,1)S(1)} %slice.92), channel_id=1, source_target_pairs={{0,7},{1,0},{2,1},{3,2},{4,3},{5,4},{6,5},{7,6},{8,15},{9,8},{10,9... | collective-permute-start | bytes 11010056 | tf_op jit(solution)/shard_map/ppermute | solution.py:15
  9.6 0.0 copy-done
  9.6 0.0 copy-done.1
  9.6 0.0 copy-done.2
  9.6 0.0 copy-done.3
  9.6 0.2 pad_maximum_fusion.10
  9.9 2.5 %collective-permute-start.1 = (bf16[4,2,4,16,1792]{4,3,2,1,0:T(8,128)(2,1)S(1)}, bf16[4,2,4,16,1792]{4,3,2,1,0:T(8,128)(2,1)S(1)}, u32[]{:S(2)}, u32[]{:S(2)}) collective-permute-start(bf16[4,2,4,16,1792]{4,3,2,1,0:T(8,128)(2,1)S(1)} %pad_maximum_fusion.10), channel_id=1, source_target_pairs={{0,24},{8,0},{16,8},{24,16},{1,25},{9,1},{17,9},{25,17},{2,26},{10... | collective-permute-start | bytes 5505032 | tf_op jit(solution)/shard_map/ppermute | solution.py:15
  12.4 37.7 %collective-permute-done = bf16[4,4,4,16,1792]{4,3,2,1,0:T(8,128)(2,1)S(1)} collective-permute-done((bf16[4,4,4,16,1792]{4,3,2,1,0:T(8,128)(2,1)S(1)}, bf16[4,4,4,16,1792]{4,3,2,1,0:T(8,128)(2,1)S(1)}, u32[]{:S(2)}, u32[]{:S(2)}) %collective-permute-start) | collective-permute-done | bytes 3670048 | tf_op jit(solution)/shard_map/ppermute | solution.py:15
  50.0 0.3 fusion.19
  50.4 2.5 %collective-permute-start.2 = (bf16[4,2,4,16,1792]{4,3,2,1,0:T(8,128)(2,1)S(1)}, bf16[4,2,4,16,1792]{4,3,2,1,0:T(8,128)(2,1)S(1)}, u32[]{:S(2)}, u32[]{:S(2)}) collective-permute-start(bf16[4,2,4,16,1792]{4,3,2,1,0:T(8,128)(2,1)S(1)} %get-tuple-element.11), channel_id=1, source_target_pairs={{0,24},{8,0},{16,8},{24,16},{1,25},{9,1},{17,9},{25,17},{2,26},{10... | collective-permute-start | bytes 5505032 | tf_op jit(solution)/shard_map/ppermute | solution.py:15
  52.9 0.0 collective-permute-done.1
  52.9 38.6 %collective-permute-done.2 = bf16[4,2,4,16,1792]{4,3,2,1,0:T(8,128)(2,1)S(1)} collective-permute-done((bf16[4,2,4,16,1792]{4,3,2,1,0:T(8,128)(2,1)S(1)}, bf16[4,2,4,16,1792]{4,3,2,1,0:T(8,128)(2,1)S(1)}, u32[]{:S(2)}, u32[]{:S(2)}) %collective-permute-start.2) | collective-permute-done | bytes 1835040 | tf_op jit(solution)/shard_map/ppermute | solution.py:15
  91.4 3.7 %fusion.5 = bf16[4,4,8,16,1792]{4,3,2,1,0:T(8,128)(2,1)} fusion(bf16[1,4,8,16,1792]{4,3,2,1,0:T(8,128)(2,1)S(1)} %bitcast.47, bf16[1,4,8,16,1792]{4,3,2,1,0:T(8,128)(2,1)S(1)} %bitcast.51, bf16[1,4,8,16,1792]{4,3,2,1,0:T(8,128)(2,1)S(1)} %bitcast.55, bf16[1,4,8,16,1792]{4,3,2,1,0:T(8,128)(2,1)S(1)} %bitcast.59, ...), kind=kLoop, calls=%fused_computation.11 | loop fusion | flops 22020096 | bytes 20185088 | tf_op jit(solution)/shard_map/concatenate | solution.py:51
  95.2 9.8 %slice.95 = bf16[4,4,8,12,1792]{4,3,2,1,0:T(8,128)(2,1)} slice(bf16[4,4,8,16,1792]{4,3,2,1,0:T(8,128)(2,1)} %fusion.5), slice={[0:4], [0:4], [0:8], [4:16], [0:1792]} | slice | bytes 11010048 | tf_op jit(solution)/shard_map/jit(_roll_static)/slice | solution.py:70
  105.0 7.0 %copy_bitcast_fusion = bf16[4,2,14,4,8,8,128]{6,5,4,3,2,1,0:T(8,128)(2,1)S(1)} fusion(bf16[4,2,4,16,1792]{4,3,2,1,0:T(8,128)(2,1)S(1)} %collective-permute-done.2, bf16[4,2,4,16,1792]{4,3,2,1,0:T(8,128)(2,1)S(1)} %collective-permute-done.1, bf16[4,2,4,16,1792]{4,3,2,1,0:T(8,128)(2,1)S(1)} %get-tuple-element.10, bf16[1,4,8,16,1792]{4,3,2,1,0:T(8,128)(2,1)S(1)} %bitcast.48, ...), kind=kLoop, calls=%fused_computation.15 | loop fusion | flops 58720256 | bytes 25690112 | tf_op jit(solution)/shard_map/transpose | solution.py:75
  112.0 3.4 %fusion.18 = (bf16[1,2,14,4,8,8,128]{6,5,4,3,2,1,0:T(8,128)(2,1)}, bf16[1,2,14,4,8,8,128]{6,5,4,3,2,1,0:T(8,128)(2,1)}, bf16[1,2,14,4,8,8,128]{6,5,4,3,2,1,0:T(8,128)(2,1)S(1)}, bf16[1,2,14,4,8,8,128]{6,5,4,3,2,1,0:T(8,128)(2,1)}) fusion(bf16[4,2,14,4,8,8,128]{6,5,4,3,2,1,0:T(8,128)(2,1)S(1)} %copy_bitcast_fusion), kind=kLoop, calls=%fused_computation.44 | loop fusion | bytes 14680064 | tf_op jit(solution)/shard_map/slice | solution.py:78
  115.3 6.8 %fusion.21 = (f32[2,14,256]{2,1,0:T(8,128)S(1)}, f32[2,14,256,256]{2,3,1,0:T(8,128)}) fusion(bf16[2,14,256,128]{3,2,1,0:T(8,128)(2,1)} %bitcast.63, bf16[2,14,256,128]{3,2,1,0:T(8,128)(2,1)S(1)} %bitcast.61), kind=kOutput, calls=%fused_computation.47 | convolution fusion | flops 475267328 | bytes 11038720 | tf_op jit(solution)/shard_map/sub | solution.py:23
  122.2 4.1 %fusion.12 = bf16[2,14,256,256]{2,3,1,0:T(8,128)(2,1)S(1)} fusion(f32[2,14,256,256]{2,3,1,0:T(8,128)} %get-tuple-element.15, f32[2,14,256]{2,1,0:T(8,128)S(1)} %get-tuple-element.14), kind=kLoop, calls=%fused_computation.32 | loop fusion | flops 3670016 | bytes 11038720 | tf_op jit(solution)/shard_map/convert_element_type | solution.py:24
  126.3 0.0 copy-done.5
  126.3 0.0 copy-start.6
  126.3 0.0 slice-start
  126.3 1.1 convolution_convert_fusion
  127.4 0.4 copy-done.6
  127.8 2.0 multiply_reduce_fusion.1
  129.8 0.4 slice-done.1
  130.2 1.4 multiply_convert_fusion
  131.5 0.1 copy-done.4
  131.7 1.1 convolution_convert_fusion.1
  132.8 1.2 convolution_convert_fusion.2
  134.0 4.1 %copy_bitcast_fusion.1 = bf16[3,4,8,16,1792]{4,3,2,1,0:T(8,128)(2,1)S(1)} fusion(bf16[1,2,14,4,8,8,128]{6,5,4,3,2,1,0:T(8,128)(2,1)S(1)} %bitcast.70, bf16[1,2,14,4,8,8,128]{6,5,4,3,2,1,0:T(8,128)(2,1)S(1)} %bitcast.71, bf16[1,2,14,4,8,8,128]{6,5,4,3,2,1,0:T(8,128)(2,1)S(1)} %bitcast.72), kind=kLoop, calls=%fused_computation.26 | loop fusion | flops 5505024 | bytes 11010048 | tf_op jit(solution)/shard_map/reshape | solution.py:80
  138.1 0.8 slice.100
  138.9 1.2 fusion.13
  140.1 0.1 collective-permute-start.3
  140.2 0.5 fusion.14
  140.7 2.4 %collective-permute-start.5 = (bf16[3,2,4,16,1792]{4,3,2,1,0:T(8,128)(2,1)S(1)}, bf16[3,2,4,16,1792]{4,3,2,1,0:T(8,128)(2,1)S(1)}, u32[]{:S(2)}, u32[]{:S(2)}) collective-permute-start(bf16[3,2,4,16,1792]{4,3,2,1,0:T(8,128)(2,1)S(1)} %fusion.14), channel_id=1, source_target_pairs={{0,8},{8,16},{16,24},{24,0},{1,9},{9,17},{17,25},{25,1},{2,10},{10... | collective-permute-start | bytes 4128776 | tf_op jit(solution)/shard_map/ppermute | solution.py:15
  143.1 31.3 %collective-permute-done.3 = bf16[3,4,4,16,1792]{4,3,2,1,0:T(8,128)(2,1)S(1)} collective-permute-done((bf16[3,4,4,16,1792]{4,3,2,1,0:T(8,128)(2,1)S(1)}, bf16[3,4,4,16,1792]{4,3,2,1,0:T(8,128)(2,1)S(1)}, u32[]{:S(2)}, u32[]{:S(2)}) %collective-permute-start.3) | collective-permute-done | bytes 2752544 | tf_op jit(solution)/shard_map/ppermute | solution.py:15
  174.4 0.2 fusion.20
  174.6 2.4 %collective-permute-start.4 = (bf16[3,2,4,16,1792]{4,3,2,1,0:T(8,128)(2,1)S(1)}, bf16[3,2,4,16,1792]{4,3,2,1,0:T(8,128)(2,1)S(1)}, u32[]{:S(2)}, u32[]{:S(2)}) collective-permute-start(bf16[3,2,4,16,1792]{4,3,2,1,0:T(8,128)(2,1)S(1)} %get-tuple-element.12), channel_id=1, source_target_pairs={{0,8},{8,16},{16,24},{24,0},{1,9},{9,17},{17,25},{25,1},{2,10},{10... | collective-permute-start | bytes 4128776 | tf_op jit(solution)/shard_map/ppermute | solution.py:15
  177.1 0.0 collective-permute-done.5
  177.1 27.0 %collective-permute-done.4 = bf16[3,2,4,16,1792]{4,3,2,1,0:T(8,128)(2,1)S(1)} collective-permute-done((bf16[3,2,4,16,1792]{4,3,2,1,0:T(8,128)(2,1)S(1)}, bf16[3,2,4,16,1792]{4,3,2,1,0:T(8,128)(2,1)S(1)}, u32[]{:S(2)}, u32[]{:S(2)}) %collective-permute-start.4) | collective-permute-done | bytes 1376288 | tf_op jit(solution)/shard_map/ppermute | solution.py:15
  204.1 1.3 fusion.8
  205.4 2.6 %slice_bitcast_fusion = (bf16[4,8,16,1792]{3,2,1,0:T(8,128)(2,1)}, bf16[4,8,16,1792]{3,2,1,0:T(8,128)(2,1)}, bf16[4,8,16,1792]{3,2,1,0:T(8,128)(2,1)}) fusion(bf16[3,4,8,16,1792]{4,3,2,1,0:T(8,128)(2,1)S(1)} %fusion.8), kind=kLoop, calls=%fused_computation.34 | loop fusion | bytes 11010048 | tf_op jit(solution)/shard_map/squeeze | solution.py:85
  (5 shorter events, 0.0 us)
Async XLA Ops:
  4.7 4.9 %copy-start = (bf16[4,8,16,1792]{3,2,1,0:T(8,128)(2,1)S(1)}, bf16[4,8,16,1792]{3,2,1,0:T(8,128)(2,1)}, u32[]{:S(2)}) copy-start(bf16[4,8,16,1792]{3,2,1,0:T(8,128)(2,1)} %param.7) | copy-start | bytes 5505028
  4.7 4.9 %copy-start.1 = (bf16[4,8,16,1792]{3,2,1,0:T(8,128)(2,1)S(1)}, bf16[4,8,16,1792]{3,2,1,0:T(8,128)(2,1)}, u32[]{:S(2)}) copy-start(bf16[4,8,16,1792]{3,2,1,0:T(8,128)(2,1)} %param.6) | copy-start | bytes 5505028
  4.7 4.9 %copy-start.2 = (bf16[4,8,16,1792]{3,2,1,0:T(8,128)(2,1)S(1)}, bf16[4,8,16,1792]{3,2,1,0:T(8,128)(2,1)}, u32[]{:S(2)}) copy-start(bf16[4,8,16,1792]{3,2,1,0:T(8,128)(2,1)} %param.5) | copy-start | bytes 5505028
  4.7 4.9 %copy-start.3 = (bf16[4,8,16,1792]{3,2,1,0:T(8,128)(2,1)S(1)}, bf16[4,8,16,1792]{3,2,1,0:T(8,128)(2,1)}, u32[]{:S(2)}) copy-start(bf16[4,8,16,1792]{3,2,1,0:T(8,128)(2,1)} %param.4) | copy-start | bytes 5505028
  5.1 44.9 %collective-permute-start = (bf16[4,4,4,16,1792]{4,3,2,1,0:T(8,128)(2,1)S(1)}, bf16[4,4,4,16,1792]{4,3,2,1,0:T(8,128)(2,1)S(1)}, u32[]{:S(2)}, u32[]{:S(2)}) collective-permute-start(bf16[4,4,4,16,1792]{4,3,2,1,0:T(8,128)(2,1)S(1)} %slice.92), channel_id=1, source_target_pairs={{0,7},{1,0},{2,1},{3,2},{4,3},{5,4},{6,5},{7,6},{8,15},{9,8},{10,9... | collective-permute-start | bytes 11010056 | tf_op jit(solution)/shard_map/ppermute | solution.py:15
  9.9 43.0 %collective-permute-start.1 = (bf16[4,2,4,16,1792]{4,3,2,1,0:T(8,128)(2,1)S(1)}, bf16[4,2,4,16,1792]{4,3,2,1,0:T(8,128)(2,1)S(1)}, u32[]{:S(2)}, u32[]{:S(2)}) collective-permute-start(bf16[4,2,4,16,1792]{4,3,2,1,0:T(8,128)(2,1)S(1)} %pad_maximum_fusion.10), channel_id=1, source_target_pairs={{0,24},{8,0},{16,8},{24,16},{1,25},{9,1},{17,9},{25,17},{2,26},{10... | collective-permute-start | bytes 5505032 | tf_op jit(solution)/shard_map/ppermute | solution.py:15
  50.4 41.1 %collective-permute-start.2 = (bf16[4,2,4,16,1792]{4,3,2,1,0:T(8,128)(2,1)S(1)}, bf16[4,2,4,16,1792]{4,3,2,1,0:T(8,128)(2,1)S(1)}, u32[]{:S(2)}, u32[]{:S(2)}) collective-permute-start(bf16[4,2,4,16,1792]{4,3,2,1,0:T(8,128)(2,1)S(1)} %get-tuple-element.11), channel_id=1, source_target_pairs={{0,24},{8,0},{16,8},{24,16},{1,25},{9,1},{17,9},{25,17},{2,26},{10... | collective-permute-start | bytes 5505032 | tf_op jit(solution)/shard_map/ppermute | solution.py:15
  122.2 4.1 %copy-start.5 = (bf16[1,2,14,4,8,8,128]{6,5,4,3,2,1,0:T(8,128)(2,1)S(1)}, bf16[1,2,14,4,8,8,128]{6,5,4,3,2,1,0:T(8,128)(2,1)}, u32[]{:S(2)}) copy-start(bf16[1,2,14,4,8,8,128]{6,5,4,3,2,1,0:T(8,128)(2,1)} %get-tuple-element.4) | copy-start | bytes 5505028
  126.3 1.5 copy-start.6
  126.3 3.5 %slice-start = ((s8[7340032]{0:T(1024)(128)(4,1)}), s8[4194304]{0:T(1024)(128)(4,1)S(1)}, s32[]{:S(2)}) async-start(s8[7340032]{0:T(1024)(128)(4,1)} %bitcast.68), calls=%async_computation | async-start | bytes 8388608
  127.8 2.4 %slice-start.1 = ((s8[7340032]{0:T(1024)(128)(4,1)}), s8[3145728]{0:T(1024)(128)(4,1)S(1)}, s32[]{:S(2)}) async-start(s8[7340032]{0:T(1024)(128)(4,1)} %bitcast.68), calls=%async_computation.1 | async-start | bytes 6291456
  130.2 1.5 copy-start.4
  140.1 34.3 %collective-permute-start.3 = (bf16[3,4,4,16,1792]{4,3,2,1,0:T(8,128)(2,1)S(1)}, bf16[3,4,4,16,1792]{4,3,2,1,0:T(8,128)(2,1)S(1)}, u32[]{:S(2)}, u32[]{:S(2)}) collective-permute-start(bf16[3,4,4,16,1792]{4,3,2,1,0:T(8,128)(2,1)S(1)} %fusion.13), channel_id=1, source_target_pairs={{0,1},{1,2},{2,3},{3,4},{4,5},{5,6},{6,7},{7,0},{8,9},{9,10},{10,1... | collective-permute-start | bytes 8257544 | tf_op jit(solution)/shard_map/ppermute | solution.py:15
  140.7 36.4 %collective-permute-start.5 = (bf16[3,2,4,16,1792]{4,3,2,1,0:T(8,128)(2,1)S(1)}, bf16[3,2,4,16,1792]{4,3,2,1,0:T(8,128)(2,1)S(1)}, u32[]{:S(2)}, u32[]{:S(2)}) collective-permute-start(bf16[3,2,4,16,1792]{4,3,2,1,0:T(8,128)(2,1)S(1)} %fusion.14), channel_id=1, source_target_pairs={{0,8},{8,16},{16,24},{24,0},{1,9},{9,17},{17,25},{25,1},{2,10},{10... | collective-permute-start | bytes 4128776 | tf_op jit(solution)/shard_map/ppermute | solution.py:15
  174.6 29.5 %collective-permute-start.4 = (bf16[3,2,4,16,1792]{4,3,2,1,0:T(8,128)(2,1)S(1)}, bf16[3,2,4,16,1792]{4,3,2,1,0:T(8,128)(2,1)S(1)}, u32[]{:S(2)}, u32[]{:S(2)}) collective-permute-start(bf16[3,2,4,16,1792]{4,3,2,1,0:T(8,128)(2,1)S(1)} %get-tuple-element.12), channel_id=1, source_target_pairs={{0,8},{8,16},{16,24},{24,0},{1,9},{9,17},{17,25},{25,1},{2,10},{10... | collective-permute-start | bytes 4128776 | tf_op jit(solution)/shard_map/ppermute | solution.py:15
where the time goes:
time: 208 us
  waiting for transfers between devices  135 us (65%)
  other arithmetic  26.3 us (13%)
  local copies, waits for them, and re-layouts  18.3 us (9%)
  starting transfers between devices  14.5 us (7%)
  matrix products  13.6 us (7%)
    ppermute x6, waiting for transfers between devices, passed_along(): lax.ppermute(value, axis, [(i, (i + by) % size) for i in range(size)])  135 us
    ppermute x6, starting transfers between devices, passed_along(): lax.ppermute(value, axis, [(i, (i + by) % size) for i in range(size)])  14.5 us
    slice x1, local copies, waits for them, and re-layouts, shards(): rolled = jnp.roll(shifted, -(WW // 2), axis=3)  9.81 us
    transpose x1, other arithmetic, shards(): windowed.transpose(0, 3, 5, 1, 2, 4, 6)  6.99 us
    sub x1, matrix products, window_grads(): weights = jax.nn.softmax(scores, axis=-1)  6.83 us
  transfers between devices with their start and end apart: 6, of which 4 were waited for; matrix products, arithmetic and copies ran while one was open for 1% of the time, Pallas kernels for 0%

commit v1 on v0

v1 whole, which is shorter than its diff:
```python
import math

import jax
import jax.numpy as jnp
from jax import lax
from jax.experimental import pallas as pl
from jax.experimental.pallas import tpu as pltpu
from jax.sharding import PartitionSpec as P

WW = 8
HEAD_DIM = 128
CHUNKS = 4
AXES = ("tm", "rows")
VMEM_BYTES = 40 * 1024 * 1024


def moved(value, by_time, by_rows):
    times, rows = lax.axis_size("tm"), lax.axis_size("rows")
    pairs = [
        (t * rows + r, ((t + by_time) % times) * rows + (r + by_rows) % rows)
        for t in range(times)
        for r in range(rows)
    ]
    return lax.ppermute(value, AXES, pairs)


def chunk_bounds(heads):
    count = min(CHUNKS, heads)
    sizes = [heads // count + (1 if i < heads % count else 0) for i in range(count)]
    bounds, start = [], 0
    for size in sizes:
        bounds.append((start, size))
        start += size
    return bounds


def late_half(shape):
    return lax.broadcasted_iota(jnp.int32, shape, 1) >= WW // 2


def split_windows(parts):
    tokens = jnp.concatenate(parts, axis=0).astype(jnp.float32)
    first, second = tokens[:, :WW], tokens[:, WW:]
    late = late_half(first.shape)
    flat = (first.shape[0] * WW, first.shape[2])
    inner = jnp.where(late, first, second).reshape(flat).astype(jnp.bfloat16)
    outer = jnp.where(late, second, first).reshape(flat).astype(jnp.bfloat16)
    return inner, outer


def join_windows(inner, outer):
    shape = (inner.shape[0] // WW, WW, inner.shape[1])
    inner, outer = inner.reshape(shape), outer.reshape(shape)
    late = late_half(shape)
    first = jnp.where(late, inner, outer)
    second = jnp.where(late, outer, inner)
    return jnp.concatenate((first, second), axis=1).astype(jnp.bfloat16)


def dot(a, b, dims):
    return lax.dot_general(a, b, (dims, ((), ())), preferred_element_type=jnp.float32)


def window_grads(query, key, value, grad):
    factor = 1.0 / math.sqrt(HEAD_DIM)
    scores = dot(key, query, ((1,), (1,))) * factor
    top = jnp.max(scores, axis=0, keepdims=True)
    weights = jnp.exp(scores - top)
    weights = weights * (1.0 / jnp.sum(weights, axis=0, keepdims=True))
    weights_b = weights.astype(jnp.bfloat16)
    weight_grad = dot(value, grad, ((1,), (1,)))
    row_dot = jnp.sum(weights_b.astype(jnp.float32) * weight_grad, axis=0, keepdims=True)
    score_grad = (weights * (weight_grad - row_dot) * factor).astype(jnp.bfloat16)
    value_out = dot(weights_b, grad, ((1,), (0,)))
    key_out = dot(score_grad, query, ((1,), (0,)))
    query_out = dot(score_grad, key, ((0,), (0,)))
    return query_out, key_out, value_out


def grads_kernel(*refs):
    q_ref, k_ref, v_ref, g_ref, row_ref, time_ref, corner_ref = refs[:7]
    frames, rows, columns, depth = q_ref.shape
    slots = frames * rows
    windows = []
    for index, ref in enumerate((q_ref, k_ref, v_ref, g_ref)):
        parts = [ref[...], row_ref[index], time_ref[index], corner_ref[index]]
        windows.append(split_windows([p.reshape(slots, columns, depth) for p in parts]))
    inner = window_grads(*[w[0] for w in windows])
    outer = window_grads(*[w[1] for w in windows])
    for index in range(3):
        tokens = join_windows(inner[index], outer[index])
        tokens = tokens.reshape(4, frames, rows, columns, depth)
        for place, ref in enumerate(refs[7:]):
            ref[index] = tokens[place]


def chunk_grads(inputs, received, start, size):
    frames, rows, columns, features = inputs[0].shape
    half = (frames // 2, rows // 2, columns)
    own = pl.BlockSpec(half + (HEAD_DIM,), lambda h: (1, 1, 0, start + h))
    sent = lambda n: pl.BlockSpec((n,) + half + (HEAD_DIM,), lambda h: (0, 0, 0, 0, h))
    piece = jax.ShapeDtypeStruct((3,) + half + (size * HEAD_DIM,), jnp.bfloat16)
    length = 4 * half[0] * half[1] * WW
    return pl.pallas_call(
        grads_kernel,
        grid=(size,),
        in_specs=[own] * 4 + [sent(4)] * 3,
        out_specs=[sent(3)] * 4,
        out_shape=[piece] * 4,
        compiler_params=pltpu.CompilerParams(vmem_limit_bytes=VMEM_BYTES),
        cost_estimate=pl.CostEstimate(
            flops=size * 2 * 5 * 2 * length * length * HEAD_DIM,
            bytes_accessed=7 * 2 * size * 2 * length * HEAD_DIM,
            transcendentals=size * 2 * length * length,
        ),
    )(*inputs, *received)


def place_kernel(*refs):
    own_ref, row_ref, time_ref, corner_ref = refs[:4]
    for index, out in enumerate(refs[-3:]):
        frames, rows, _, _ = out.shape
        f, r = frames // 2, rows // 2
        out[f:, r:] = own_ref[index]
        out[f:, :r] = row_ref[index]
        out[:f, r:] = time_ref[index]
        out[:f, :r] = corner_ref[index]


def placed(outs, pieces, whole, start, size):
    frames, rows, columns, features = whole.shape
    half = (frames // 2, rows // 2, columns)
    sent = pl.BlockSpec((3,) + half + (HEAD_DIM,), lambda h: (0, 0, 0, 0, h))
    full = pl.BlockSpec((frames, rows, columns, HEAD_DIM), lambda h: (0, 0, 0, start + h))
    outs = () if outs is None else outs
    return pl.pallas_call(
        place_kernel,
        grid=(size,),
        in_specs=[sent] * 4 + [pl.BlockSpec(memory_space=pl.ANY)] * len(outs),
        out_specs=[full] * 3,
        out_shape=[jax.ShapeDtypeStruct(whole.shape, whole.dtype)] * 3,
        input_output_aliases={4 + i: i for i in range(len(outs))},
        compiler_params=pltpu.CompilerParams(vmem_limit_bytes=VMEM_BYTES),
        cost_estimate=pl.CostEstimate(
            flops=0, bytes_accessed=sum(4 * p.size for p in pieces), transcendentals=0
        ),
    )(*pieces, *outs)


def shards(queries, keys, values, out_grad):
    inputs = (queries, keys, values, out_grad)
    frames, rows, columns, features = queries.shape
    early_f, late_f = slice(0, frames // 2), slice(frames // 2, frames)
    early_r, late_r = slice(0, rows // 2), slice(rows // 2, rows)
    bounds = chunk_bounds(features // HEAD_DIM)
    received = []
    for start, size in bounds:
        lanes = slice(start * HEAD_DIM, (start + size) * HEAD_DIM)
        cut = lambda f, r: jnp.stack([x[f, r, :, lanes] for x in inputs])
        time = moved(cut(early_f, late_r), -1, 0)
        corner = moved(cut(early_f, early_r), -1, -1)
        row = moved(cut(late_f, early_r), 0, -1)
        received.append((row, time, corner))
    returned = []
    for (start, size), got in zip(bounds, received):
        own, row, time, corner = chunk_grads(inputs, got, start, size)
        time = moved(time, 1, 0)
        corner = moved(corner, 1, 1)
        row = moved(row, 0, 1)
        returned.append((own, row, time, corner))
    outs = None
    for (start, size), pieces in zip(bounds, returned):
        outs = placed(outs, pieces, queries, start, size)
    return tuple(outs)


def solution(mesh):
    spec = P("tm", "rows", None, None)
    return jax.shard_map(
        shards,
        mesh=mesh,
        in_specs=(spec,) * 4,
        out_specs=(spec,) * 3,
        check_vma=False,
    )
```

time: 208 us -> 152 us (0.73)
  waiting for transfers between devices: 135 us -> 55.6 us
  starting transfers between devices: 14.5 us -> 66.8 us
  other arithmetic: 26.3 us -> 0.79 us
  Pallas kernels: 0 us -> 23.9 us
  local copies, waits for them, and re-layouts: 18.3 us -> 3.99 us
  matrix products: 13.6 us -> 0 us
    ppermute x6 -> x24, waiting for transfers between devices: 135 us -> 55.6 us  [moved(): return lax.ppermute(value, AXES, pairs)]
    ppermute x6 -> x24, starting transfers between devices: 14.5 us -> 66.8 us  [moved(): return lax.ppermute(value, AXES, pairs)]
    pallas_call x0 -> x8, Pallas kernels: none -> 23.9 us  [the longest x4 16.6 us: chunk_grads(): pl.pallas_call(grads_kernel, grid=(size,), in_specs=[own] * 4 + [sent(4)]...]
    slice x6 -> x0, local copies, waits for them, and re-layouts: 14.8 us -> none  [the longest x1 9.81 us: shards(): rolled = jnp.roll(shifted, -(WW // 2), axis=3)]
    transpose x1 -> x0, other arithmetic: 6.99 us -> none  [shards(): windowed.transpose(0, 3, 5, 1, 2, 4, 6)]
    sub x1 -> x0, matrix products: 6.83 us -> none  [window_grads(): weights = jax.nn.softmax(scores, axis=-1)]
    concatenate x4 -> x0, other arithmetic: 6.79 us -> none  [the longest x1 3.73 us: forward_route(): return jnp.concatenate((top_half, bottom_half), axis=1)]
    dot_general x5 -> x0, matrix products: 6.75 us -> none  [the longest x1 2.02 us: window_grads(): jnp.einsum('bhqk,bhkd->bhqd', weights_b, value_w, preferred_element_type=...]
  transfers between devices with their start and end apart: 6 -> 24, of which waited for: 4 -> 11; matrix products, arithmetic and copies ran while one was open for 1% -> 1% of each run, Pallas kernels for 0% -> 15%
where the time goes in v1:
time: 152 us
  starting transfers between devices  66.8 us (44%)
  waiting for transfers between devices  55.6 us (37%)
  Pallas kernels  23.9 us (16%)
  local copies, waits for them, and re-layouts  3.99 us (3%)
    ppermute x24, starting transfers between devices, moved(): return lax.ppermute(value, AXES, pairs)  66.8 us
    ppermute x24, waiting for transfers between devices, moved(): return lax.ppermute(value, AXES, pairs)  55.6 us
    pallas_call x4, Pallas kernels, chunk_grads(): pl.pallas_call(grads_kernel, grid=(size,), in_specs=[own] * 4 + [sent(4)]...  16.6 us
    pallas_call x4, Pallas kernels, placed(): pl.pallas_call(place_kernel, grid=(size,), in_specs=[sent] * 4 + [pl.Bloc...  7.32 us
    another operation x4, local copies, waits for them, and re-layouts, shards(): cut = lambda f, r: jnp.stack([x[f, r, :, lanes] for x in inputs])  3.69 us
  transfers between devices with their start and end apart: 24, of which 11 were waited for; matrix products, arithmetic and copies ran while one was open for 1% of the time, Pallas kernels for 15%

profile of v1, /device:TPU:0, one launch (start us, length us, event | category | flops | bytes accessed | tf_op | source)
XLA Modules:
  0.0 152.0 jit_solution(9186712658938721467)
XLA Ops:
  0.6 1.8 %slice_bitcast_fusion = (bf16[1,2,4,16,512]{4,3,2,1,0:T(8,128)(2,1)S(1)}, bf16[1,2,4,16,512]{4,3,2,1,0:T(8,128)(2,1)S(1)}, bf16[1,2,4,16,512]{4,3,2,1,0:T(8,128)...) fusion(bf16[4,8,16,1792]{3,2,1,0:T(8,128)(2,1)} %refs_3_.7, ...), kind=kLoop, calls=%fused_computation.12 | loop fusion | bytes 3145728 | tf_op jit(solution)/shard_map/stack | solution.py:159
  2.4 0.3 copy-done
  2.7 1.5 %slice_bitcast_fusion.2 = (bf16[1,2,4,16,512]{4,3,2,1,0:T(8,128)(2,1)S(1)}, bf16[1,2,4,16,512]{4,3,2,1,0:T(8,128)(2,1)S(1)}, bf16[1,2,4,16,512]{4,3,2,1,0:T(8,12...) fusion(bf16[4,8,16,1792]{3,2,1,0:T(8,128)(2,1)} %refs_1_.7, ...), kind=kLoop, calls=%fused_computation.14 | loop fusion | bytes 3145728 | tf_op jit(solution)/shard_map/stack | solution.py:159
  4.3 0.1 pad_maximum_fusion.3
  4.3 4.5 %collective-permute-start.18 = (bf16[4,2,4,16,512]{4,3,2,1,0:T(8,128)(2,1)S(1)}, bf16[4,2,4,16,512]{4,3,2,1,0:T(8,128)(2,1)S(1)}, u32[]{:S(2)}, u32[]{:S(2)}) collective-permute-start(bf16[4,2,4,16,512]{4,3,2,1,0:T(8,128)(2,1)S(1)} %pad_maximum_fusion.3), channel_id=1, source_target_pairs={{0,7},{1,0},{2,1},{3,2},{4,3},{5,4},{6,5},{7,6},{8,15},{9,8},{10,9... | collective-permute-start | bytes 1572872 | tf_op jit(solution)/shard_map/ppermute | solution.py:24
  8.9 0.2 slice_bitcast_fusion.24
  9.1 0.2 slice_bitcast_fusion.26
  9.4 1.4 collective-permute-start.6
  10.8 2.5 %collective-permute-start.7 = (bf16[4,2,4,16,384]{4,3,2,1,0:T(8,128)(2,1)S(1)}, bf16[4,2,4,16,384]{4,3,2,1,0:T(8,128)(2,1)S(1)}, u32[]{:S(2)}, u32[]{:S(2)}) collective-permute-start(bf16[4,2,4,16,384]{4,3,2,1,0:T(8,128)(2,1)S(1)} %pad_maximum_fusion.10), channel_id=1, source_target_pairs={{0,24},{1,25},{2,26},{3,27},{4,28},{5,29},{6,30},{7,31},{8,0},{9,1... | collective-permute-start | bytes 1179656 | tf_op jit(solution)/shard_map/ppermute | solution.py:24
  13.4 0.4 collective-permute-start.8
  13.8 0.1 pad_maximum_fusion.4
  13.9 1.5 collective-permute-start.19
  15.4 0.1 pad_maximum_fusion.5
  15.5 0.1 pad_maximum_fusion
  15.5 4.3 %collective-permute-done.6.refs_4_ = bf16[4,2,4,16,384]{4,3,2,1,0:T(8,128)(2,1)S(1)} collective-permute-done((bf16[4,2,4,16,384]{4,3,2,1,0:T(8,128)(2,1)S(1)}, bf16[4,2,4,16,384]{4,3,2,1,0:T(8,128)(2,1)S(1)}, u32[]{:S(2)}, u32[]{:S(2)}) %collective-permute-start.6) | collective-permute-done | bytes 393248 | tf_op jit(solution)/shard_map/ppermute | solution.py:24
  19.8 5.6 %collective-permute-start.20 = (bf16[4,2,4,16,512]{4,3,2,1,0:T(8,128)(2,1)S(1)}, bf16[4,2,4,16,512]{4,3,2,1,0:T(8,128)(2,1)S(1)}, u32[]{:S(2)}, u32[]{:S(2)}) collective-permute-start(bf16[4,2,4,16,512]{4,3,2,1,0:T(8,128)(2,1)S(1)} %pad_maximum_fusion.5), channel_id=1, source_target_pairs={{0,31},{1,24},{2,25},{3,26},{4,27},{5,28},{6,29},{7,30},{8,7},{9,0... | collective-permute-start | bytes 1572872 | tf_op jit(solution)/shard_map/ppermute | solution.py:24
  25.4 7.4 %collective-permute-done.7.refs_5_ = bf16[4,2,4,16,384]{4,3,2,1,0:T(8,128)(2,1)S(1)} collective-permute-done((bf16[4,2,4,16,384]{4,3,2,1,0:T(8,128)(2,1)S(1)}, bf16[4,2,4,16,384]{4,3,2,1,0:T(8,128)(2,1)S(1)}, u32[]{:S(2)}, u32[]{:S(2)}) %collective-permute-start.7) | collective-permute-done | bytes 393248 | tf_op jit(solution)/shard_map/ppermute | solution.py:24
  32.8 0.1 pad_maximum_fusion.1
  32.9 4.6 %collective-permute-done.8.refs_6_ = bf16[4,2,4,16,384]{4,3,2,1,0:T(8,128)(2,1)S(1)} collective-permute-done((bf16[4,2,4,16,384]{4,3,2,1,0:T(8,128)(2,1)S(1)}, bf16[4,2,4,16,384]{4,3,2,1,0:T(8,128)(2,1)S(1)}, u32[]{:S(2)}, u32[]{:S(2)}) %collective-permute-start.8) | collective-permute-done | bytes 393248 | tf_op jit(solution)/shard_map/ppermute | solution.py:24
  37.4 3.3 %collective-permute-start.13 = (bf16[4,2,4,16,512]{4,3,2,1,0:T(8,128)(2,1)S(1)}, bf16[4,2,4,16,512]{4,3,2,1,0:T(8,128)(2,1)S(1)}, u32[]{:S(2)}, u32[]{:S(2)}) collective-permute-start(bf16[4,2,4,16,512]{4,3,2,1,0:T(8,128)(2,1)S(1)} %pad_maximum_fusion.1), channel_id=1, source_target_pairs={{0,24},{1,25},{2,26},{3,27},{4,28},{5,29},{6,30},{7,31},{8,0},{9,1... | collective-permute-start | bytes 1572872 | tf_op jit(solution)/shard_map/ppermute | solution.py:24
  40.9 0.9 collective-permute-start.14
  42.0 7.6 %collective-permute-done.19.refs_5_ = bf16[4,2,4,16,512]{4,3,2,1,0:T(8,128)(2,1)S(1)} collective-permute-done((bf16[4,2,4,16,512]{4,3,2,1,0:T(8,128)(2,1)S(1)}, bf16[4,2,4,16,512]{4,3,2,1,0:T(8,128)(2,1)S(1)}, u32[]{:S(2)}, u32[]{:S(2)}) %collective-permute-start.19) | collective-permute-done | bytes 524320 | tf_op jit(solution)/shard_map/ppermute | solution.py:24
  49.6 9.6 %collective-permute-start.2 = (bf16[4,2,4,16,384]{4,3,2,1,0:T(8,128)(2,1)S(1)}, bf16[4,2,4,16,384]{4,3,2,1,0:T(8,128)(2,1)S(1)}, u32[]{:S(2)}, u32[]{:S(2)}) collective-permute-start(bf16[4,2,4,16,384]{4,3,2,1,0:T(8,128)(2,1)S(1)} %pad_maximum_fusion.8), channel_id=1, source_target_pairs={{0,31},{1,24},{2,25},{3,26},{4,27},{5,28},{6,29},{7,30},{8,7},{9,0... | collective-permute-start | bytes 1179656 | tf_op jit(solution)/shard_map/ppermute | solution.py:24
  59.3 8.1 %collective-permute-done.20.refs_6_ = bf16[4,2,4,16,512]{4,3,2,1,0:T(8,128)(2,1)S(1)} collective-permute-done((bf16[4,2,4,16,512]{4,3,2,1,0:T(8,128)(2,1)S(1)}, bf16[4,2,4,16,512]{4,3,2,1,0:T(8,128)(2,1)S(1)}, u32[]{:S(2)}, u32[]{:S(2)}) %collective-permute-start.20) | collective-permute-done | bytes 524320 | tf_op jit(solution)/shard_map/ppermute | solution.py:24
  67.4 3.3 %collective-permute-start.1 = (bf16[4,2,4,16,384]{4,3,2,1,0:T(8,128)(2,1)S(1)}, bf16[4,2,4,16,384]{4,3,2,1,0:T(8,128)(2,1)S(1)}, u32[]{:S(2)}, u32[]{:S(2)}) collective-permute-start(bf16[4,2,4,16,384]{4,3,2,1,0:T(8,128)(2,1)S(1)} %pad_maximum_fusion.7), channel_id=1, source_target_pairs={{0,24},{1,25},{2,26},{3,27},{4,28},{5,29},{6,30},{7,31},{8,0},{9,1... | collective-permute-start | bytes 1179656 | tf_op jit(solution)/shard_map/ppermute | solution.py:24
  70.8 4.7 %shard_map.70 = (bf16[3,2,4,16,512]{4,3,2,1,0:T(8,128)(2,1)S(1)}, bf16[3,2,4,16,512]{4,3,2,1,0:T(8,128)(2,1)S(1)}, bf16[3,2,4,16,512]{4,3,2,1,0:T(8,128)(2,1)S(1)}, bf16[3,2,4,16,512]{4,3,2,1,0:T(8,128)(2,1)S(1)}) custom-call(bf16[4,8,16,1792]{3,2,1,0:T(8,128)(2,1)S(1)} %copy-done, bf16[4,8,16,1792]{3,2,1,0:T(8,128)(2,1)S(1)} %copy-done.1, ...), custom_call_target="tpu_custom_call" | custom-call | flops 671088640 | bytes 3670016 | tf_op jit(solution)/shard_map/pallas_call | solution.py:104
  75.5 0.6 collective-permute-start.21
  76.1 3.6 %shard_map.68 = (bf16[3,2,4,16,384]{4,3,2,1,0:T(8,128)(2,1)S(1)}, bf16[3,2,4,16,384]{4,3,2,1,0:T(8,128)(2,1)S(1)}, bf16[3,2,4,16,384]{4,3,2,1,0:T(8,128)(2,1)S(1)}, bf16[3,2,4,16,384]{4,3,2,1,0:T(8,128)(2,1)S(1)}) custom-call(bf16[4,8,16,1792]{3,2,1,0:T(8,128)(2,1)S(1)} %copy-done, bf16[4,8,16,1792]{3,2,1,0:T(8,128)(2,1)S(1)} %copy-done.1, ...), custom_call_target="tpu_custom_call" | custom-call | flops 503316480 | bytes 2752512 | tf_op jit(solution)/shard_map/pallas_call | solution.py:104
  79.6 3.2 %collective-permute-done.14.refs_6_ = bf16[4,2,4,16,512]{4,3,2,1,0:T(8,128)(2,1)S(1)} collective-permute-done((bf16[4,2,4,16,512]{4,3,2,1,0:T(8,128)(2,1)S(1)}, bf16[4,2,4,16,512]{4,3,2,1,0:T(8,128)(2,1)S(1)}, u32[]{:S(2)}, u32[]{:S(2)}) %collective-permute-start.14) | collective-permute-done | bytes 524320 | tf_op jit(solution)/shard_map/ppermute | solution.py:24
  82.9 2.4 %collective-permute-start.10 = (bf16[3,2,4,16,384]{4,3,2,1,0:T(8,128)(2,1)S(1)}, bf16[3,2,4,16,384]{4,3,2,1,0:T(8,128)(2,1)S(1)}, u32[]{:S(2)}, u32[]{:S(2)}) collective-permute-start(bf16[3,2,4,16,384]{4,3,2,1,0:T(8,128)(2,1)S(1)} %get-tuple-element.34), channel_id=1, source_target_pairs={{0,8},{1,9},{2,10},{3,11},{4,12},{5,13},{6,14},{7,15},{8,16},{9,17... | collective-permute-start | bytes 884744 | tf_op jit(solution)/shard_map/ppermute | solution.py:24
  85.3 4.7 %shard_map.69 = (bf16[3,2,4,16,512]{4,3,2,1,0:T(8,128)(2,1)S(1)}, bf16[3,2,4,16,512]{4,3,2,1,0:T(8,128)(2,1)S(1)}, bf16[3,2,4,16,512]{4,3,2,1,0:T(8,128)(2,1)S(1)}, bf16[3,2,4,16,512]{4,3,2,1,0:T(8,128)(2,1)S(1)}) custom-call(bf16[4,8,16,1792]{3,2,1,0:T(8,128)(2,1)S(1)} %copy-done, bf16[4,8,16,1792]{3,2,1,0:T(8,128)(2,1)S(1)} %copy-done.1, ...), custom_call_target="tpu_custom_call" | custom-call | flops 671088640 | bytes 3670016 | tf_op jit(solution)/shard_map/pallas_call | solution.py:104
  90.0 0.6 collective-permute-start.22
  90.7 6.3 %collective-permute-start.23 = (bf16[3,2,4,16,512]{4,3,2,1,0:T(8,128)(2,1)S(1)}, bf16[3,2,4,16,512]{4,3,2,1,0:T(8,128)(2,1)S(1)}, u32[]{:S(2)}, u32[]{:S(2)}) collective-permute-start(bf16[3,2,4,16,512]{4,3,2,1,0:T(8,128)(2,1)S(1)} %get-tuple-element.43), channel_id=1, source_target_pairs={{0,9},{1,10},{2,11},{3,12},{4,13},{5,14},{6,15},{7,8},{8,17},{9,18... | collective-permute-start | bytes 1179656 | tf_op jit(solution)/shard_map/ppermute | solution.py:24
  97.0 1.1 collective-permute-start.16
  98.0 10.6 %collective-permute-start.17 = (bf16[3,2,4,16,512]{4,3,2,1,0:T(8,128)(2,1)S(1)}, bf16[3,2,4,16,512]{4,3,2,1,0:T(8,128)(2,1)S(1)}, u32[]{:S(2)}, u32[]{:S(2)}) collective-permute-start(bf16[3,2,4,16,512]{4,3,2,1,0:T(8,128)(2,1)S(1)} %get-tuple-element.39), channel_id=1, source_target_pairs={{0,9},{1,10},{2,11},{3,12},{4,13},{5,14},{6,15},{7,8},{8,17},{9,18... | collective-permute-start | bytes 1179656 | tf_op jit(solution)/shard_map/ppermute | solution.py:24
  108.6 3.6 %shard_map.67 = (bf16[3,2,4,16,384]{4,3,2,1,0:T(8,128)(2,1)S(1)}, bf16[3,2,4,16,384]{4,3,2,1,0:T(8,128)(2,1)S(1)}, bf16[3,2,4,16,384]{4,3,2,1,0:T(8,128)(2,1)S(1)}, bf16[3,2,4,16,384]{4,3,2,1,0:T(8,128)(2,1)S(1)}) custom-call(bf16[4,8,16,1792]{3,2,1,0:T(8,128)(2,1)S(1)} %copy-done, bf16[4,8,16,1792]{3,2,1,0:T(8,128)(2,1)S(1)} %copy-done.1, ...), custom_call_target="tpu_custom_call" | custom-call | flops 503316480 | bytes 2752512 | tf_op jit(solution)/shard_map/pallas_call | solution.py:104
  112.2 9.3 %collective-permute-start.11 = (bf16[3,2,4,16,384]{4,3,2,1,0:T(8,128)(2,1)S(1)}, bf16[3,2,4,16,384]{4,3,2,1,0:T(8,128)(2,1)S(1)}, u32[]{:S(2)}, u32[]{:S(2)}) collective-permute-start(bf16[3,2,4,16,384]{4,3,2,1,0:T(8,128)(2,1)S(1)} %get-tuple-element.35), channel_id=1, source_target_pairs={{0,9},{1,10},{2,11},{3,12},{4,13},{5,14},{6,15},{7,8},{8,17},{9,18... | collective-permute-start | bytes 884744 | tf_op jit(solution)/shard_map/ppermute | solution.py:24
  121.6 9.7 %collective-permute-done.16.refs_2_ = bf16[3,2,4,16,512]{4,3,2,1,0:T(8,128)(2,1)S(1)} collective-permute-done((bf16[3,2,4,16,512]{4,3,2,1,0:T(8,128)(2,1)S(1)}, bf16[3,2,4,16,512]{4,3,2,1,0:T(8,128)(2,1)S(1)}, u32[]{:S(2)}, u32[]{:S(2)}) %collective-permute-start.16) | collective-permute-done | bytes 393248 | tf_op jit(solution)/shard_map/ppermute | solution.py:24
  131.2 0.8 collective-permute-start.4
  132.1 3.2 %collective-permute-done.17.refs_3_ = bf16[3,2,4,16,512]{4,3,2,1,0:T(8,128)(2,1)S(1)} collective-permute-done((bf16[3,2,4,16,512]{4,3,2,1,0:T(8,128)(2,1)S(1)}, bf16[3,2,4,16,512]{4,3,2,1,0:T(8,128)(2,1)S(1)}, u32[]{:S(2)}, u32[]{:S(2)}) %collective-permute-start.17) | collective-permute-done | bytes 393248 | tf_op jit(solution)/shard_map/ppermute | solution.py:24
  135.2 1.9 %collective-permute-start.5 = (bf16[3,2,4,16,384]{4,3,2,1,0:T(8,128)(2,1)S(1)}, bf16[3,2,4,16,384]{4,3,2,1,0:T(8,128)(2,1)S(1)}, u32[]{:S(2)}, u32[]{:S(2)}) collective-permute-start(bf16[3,2,4,16,384]{4,3,2,1,0:T(8,128)(2,1)S(1)} %get-tuple-element.31), channel_id=1, source_target_pairs={{0,9},{1,10},{2,11},{3,12},{4,13},{5,14},{6,15},{7,8},{8,17},{9,18... | collective-permute-start | bytes 884744 | tf_op jit(solution)/shard_map/ppermute | solution.py:24
  137.2 1.9 %shard_map.71 = (bf16[4,8,16,1792]{3,2,1,0:T(8,128)(2,1)}, bf16[4,8,16,1792]{3,2,1,0:T(8,128)(2,1)}, bf16[4,8,16,1792]{3,2,1,0:T(8,128)(2,1)}) custom-call(bf16[3,2,4,16,512]{4,3,2,1,0:T(8,128)(2,1)S(1)} %get-tuple-element.40.refs_0_, bf16[3,2,4,16,512]{4,3,2,1,0:T(8,128)(2,1)S(1)} %collective-permute-done.21.refs_1_, ...), custom_call_target="tpu_custom_call" | custom-call | bytes 3145728 | tf_op jit(solution)/shard_map/pallas_call | solution.py:136
  139.1 1.9 %shard_map.72 = (bf16[4,8,16,1792]{3,2,1,0:T(8,128)(2,1)}, bf16[4,8,16,1792]{3,2,1,0:T(8,128)(2,1)}, bf16[4,8,16,1792]{3,2,1,0:T(8,128)(2,1)}) custom-call(bf16[3,2,4,16,512]{4,3,2,1,0:T(8,128)(2,1)S(1)} %get-tuple-element.36.refs_0_, ...), custom_call_target="tpu_custom_call", output_to_operand_aliasing={{0}: (4, {}), {1}: (5, {}), {2}: (6, {})} | custom-call | bytes 3145728 | tf_op jit(solution)/shard_map/pallas_call | solution.py:136
  141.0 2.9 %collective-permute-done.11.refs_3_ = bf16[3,2,4,16,384]{4,3,2,1,0:T(8,128)(2,1)S(1)} collective-permute-done((bf16[3,2,4,16,384]{4,3,2,1,0:T(8,128)(2,1)S(1)}, bf16[3,2,4,16,384]{4,3,2,1,0:T(8,128)(2,1)S(1)}, u32[]{:S(2)}, u32[]{:S(2)}) %collective-permute-start.11) | collective-permute-done | bytes 294944 | tf_op jit(solution)/shard_map/ppermute | solution.py:24
  143.9 1.7 %shard_map.73 = (bf16[4,8,16,1792]{3,2,1,0:T(8,128)(2,1)}, bf16[4,8,16,1792]{3,2,1,0:T(8,128)(2,1)}, bf16[4,8,16,1792]{3,2,1,0:T(8,128)(2,1)}) custom-call(bf16[3,2,4,16,384]{4,3,2,1,0:T(8,128)(2,1)S(1)} %get-tuple-element.32.refs_0_, ...), custom_call_target="tpu_custom_call", output_to_operand_aliasing={{0}: (4, {}), {1}: (5, {}), {2}: (6, {})} | custom-call | bytes 2359296 | tf_op jit(solution)/shard_map/pallas_call | solution.py:136
  145.7 2.4 %collective-permute-done.4.refs_2_ = bf16[3,2,4,16,384]{4,3,2,1,0:T(8,128)(2,1)S(1)} collective-permute-done((bf16[3,2,4,16,384]{4,3,2,1,0:T(8,128)(2,1)S(1)}, bf16[3,2,4,16,384]{4,3,2,1,0:T(8,128)(2,1)S(1)}, u32[]{:S(2)}, u32[]{:S(2)}) %collective-permute-start.4) | collective-permute-done | bytes 294944 | tf_op jit(solution)/shard_map/ppermute | solution.py:24
  148.1 2.2 %collective-permute-done.5.refs_3_ = bf16[3,2,4,16,384]{4,3,2,1,0:T(8,128)(2,1)S(1)} collective-permute-done((bf16[3,2,4,16,384]{4,3,2,1,0:T(8,128)(2,1)S(1)}, bf16[3,2,4,16,384]{4,3,2,1,0:T(8,128)(2,1)S(1)}, u32[]{:S(2)}, u32[]{:S(2)}) %collective-permute-start.5) | collective-permute-done | bytes 294944 | tf_op jit(solution)/shard_map/ppermute | solution.py:24
  150.2 1.7 %shard_map.74 = (bf16[4,8,16,1792]{3,2,1,0:T(8,128)(2,1)}, bf16[4,8,16,1792]{3,2,1,0:T(8,128)(2,1)}, bf16[4,8,16,1792]{3,2,1,0:T(8,128)(2,1)}) custom-call(bf16[3,2,4,16,384]{4,3,2,1,0:T(8,128)(2,1)S(1)} %get-tuple-element.28.refs_0_, ...), custom_call_target="tpu_custom_call", output_to_operand_aliasing={{0}: (4, {}), {1}: (5, {}), {2}: (6, {})} | custom-call | bytes 2359296 | tf_op jit(solution)/shard_map/pallas_call | solution.py:136
  (32 shorter events, 0.6 us)
Async XLA Ops:
  0.6 2.1 %copy-start = (bf16[4,8,16,1792]{3,2,1,0:T(8,128)(2,1)S(1)}, bf16[4,8,16,1792]{3,2,1,0:T(8,128)(2,1)}, u32[]{:S(2)}) copy-start(bf16[4,8,16,1792]{3,2,1,0:T(8,128)(2,1)} %refs_0_.7) | copy-start | bytes 5505028
  2.7 6.2 %copy-start.2 = (bf16[4,8,16,1792]{3,2,1,0:T(8,128)(2,1)S(1)}, bf16[4,8,16,1792]{3,2,1,0:T(8,128)(2,1)}, u32[]{:S(2)}) copy-start(bf16[4,8,16,1792]{3,2,1,0:T(8,128)(2,1)} %refs_2_.7) | copy-start | bytes 5505028
  2.7 6.2 %copy-start.3 = (bf16[4,8,16,1792]{3,2,1,0:T(8,128)(2,1)S(1)}, bf16[4,8,16,1792]{3,2,1,0:T(8,128)(2,1)}, u32[]{:S(2)}) copy-start(bf16[4,8,16,1792]{3,2,1,0:T(8,128)(2,1)} %refs_3_.7) | copy-start | bytes 5505028
  4.2 4.8 %copy-start.1 = (bf16[4,8,16,1792]{3,2,1,0:T(8,128)(2,1)S(1)}, bf16[4,8,16,1792]{3,2,1,0:T(8,128)(2,1)}, u32[]{:S(2)}) copy-start(bf16[4,8,16,1792]{3,2,1,0:T(8,128)(2,1)} %refs_1_.7) | copy-start | bytes 5505028
  4.3 36.5 %collective-permute-start.18 = (bf16[4,2,4,16,512]{4,3,2,1,0:T(8,128)(2,1)S(1)}, bf16[4,2,4,16,512]{4,3,2,1,0:T(8,128)(2,1)S(1)}, u32[]{:S(2)}, u32[]{:S(2)}) collective-permute-start(bf16[4,2,4,16,512]{4,3,2,1,0:T(8,128)(2,1)S(1)} %pad_maximum_fusion.3), channel_id=1, source_target_pairs={{0,7},{1,0},{2,1},{3,2},{4,3},{5,4},{6,5},{7,6},{8,15},{9,8},{10,9... | collective-permute-start | bytes 1572872 | tf_op jit(solution)/shard_map/ppermute | solution.py:24
  9.4 10.4 %collective-permute-start.6 = (bf16[4,2,4,16,384]{4,3,2,1,0:T(8,128)(2,1)S(1)}, bf16[4,2,4,16,384]{4,3,2,1,0:T(8,128)(2,1)S(1)}, u32[]{:S(2)}, u32[]{:S(2)}) collective-permute-start(bf16[4,2,4,16,384]{4,3,2,1,0:T(8,128)(2,1)S(1)} %pad_maximum_fusion.9), channel_id=1, source_target_pairs={{0,7},{1,0},{2,1},{3,2},{4,3},{5,4},{6,5},{7,6},{8,15},{9,8},{10,9... | collective-permute-start | bytes 1179656 | tf_op jit(solution)/shard_map/ppermute | solution.py:24
  10.8 21.9 %collective-permute-start.7 = (bf16[4,2,4,16,384]{4,3,2,1,0:T(8,128)(2,1)S(1)}, bf16[4,2,4,16,384]{4,3,2,1,0:T(8,128)(2,1)S(1)}, u32[]{:S(2)}, u32[]{:S(2)}) collective-permute-start(bf16[4,2,4,16,384]{4,3,2,1,0:T(8,128)(2,1)S(1)} %pad_maximum_fusion.10), channel_id=1, source_target_pairs={{0,24},{1,25},{2,26},{3,27},{4,28},{5,29},{6,30},{7,31},{8,0},{9,1... | collective-permute-start | bytes 1179656 | tf_op jit(solution)/shard_map/ppermute | solution.py:24
  13.4 24.0 %collective-permute-start.8 = (bf16[4,2,4,16,384]{4,3,2,1,0:T(8,128)(2,1)S(1)}, bf16[4,2,4,16,384]{4,3,2,1,0:T(8,128)(2,1)S(1)}, u32[]{:S(2)}, u32[]{:S(2)}) collective-permute-start(bf16[4,2,4,16,384]{4,3,2,1,0:T(8,128)(2,1)S(1)} %pad_maximum_fusion.11), channel_id=1, source_target_pairs={{0,31},{1,24},{2,25},{3,26},{4,27},{5,28},{6,29},{7,30},{8,7},{9,0... | collective-permute-start | bytes 1179656 | tf_op jit(solution)/shard_map/ppermute | solution.py:24
  13.9 35.7 %collective-permute-start.19 = (bf16[4,2,4,16,512]{4,3,2,1,0:T(8,128)(2,1)S(1)}, bf16[4,2,4,16,512]{4,3,2,1,0:T(8,128)(2,1)S(1)}, u32[]{:S(2)}, u32[]{:S(2)}) collective-permute-start(bf16[4,2,4,16,512]{4,3,2,1,0:T(8,128)(2,1)S(1)} %pad_maximum_fusion.4), channel_id=1, source_target_pairs={{0,24},{1,25},{2,26},{3,27},{4,28},{5,29},{6,30},{7,31},{8,0},{9,1... | collective-permute-start | bytes 1572872 | tf_op jit(solution)/shard_map/ppermute | solution.py:24
  19.8 47.6 %collective-permute-start.20 = (bf16[4,2,4,16,512]{4,3,2,1,0:T(8,128)(2,1)S(1)}, bf16[4,2,4,16,512]{4,3,2,1,0:T(8,128)(2,1)S(1)}, u32[]{:S(2)}, u32[]{:S(2)}) collective-permute-start(bf16[4,2,4,16,512]{4,3,2,1,0:T(8,128)(2,1)S(1)} %pad_maximum_fusion.5), channel_id=1, source_target_pairs={{0,31},{1,24},{2,25},{3,26},{4,27},{5,28},{6,29},{7,30},{8,7},{9,0... | collective-permute-start | bytes 1572872 | tf_op jit(solution)/shard_map/ppermute | solution.py:24
  32.8 38.0 %collective-permute-start.12 = (bf16[4,2,4,16,512]{4,3,2,1,0:T(8,128)(2,1)S(1)}, bf16[4,2,4,16,512]{4,3,2,1,0:T(8,128)(2,1)S(1)}, u32[]{:S(2)}, u32[]{:S(2)}) collective-permute-start(bf16[4,2,4,16,512]{4,3,2,1,0:T(8,128)(2,1)S(1)} %pad_maximum_fusion), channel_id=1, source_target_pairs={{0,7},{1,0},{2,1},{3,2},{4,3},{5,4},{6,5},{7,6},{8,15},{9,8},{10,9... | collective-permute-start | bytes 1572872 | tf_op jit(solution)/shard_map/ppermute | solution.py:24
  37.4 38.1 %collective-permute-start.13 = (bf16[4,2,4,16,512]{4,3,2,1,0:T(8,128)(2,1)S(1)}, bf16[4,2,4,16,512]{4,3,2,1,0:T(8,128)(2,1)S(1)}, u32[]{:S(2)}, u32[]{:S(2)}) collective-permute-start(bf16[4,2,4,16,512]{4,3,2,1,0:T(8,128)(2,1)S(1)} %pad_maximum_fusion.1), channel_id=1, source_target_pairs={{0,24},{1,25},{2,26},{3,27},{4,28},{5,29},{6,30},{7,31},{8,0},{9,1... | collective-permute-start | bytes 1572872 | tf_op jit(solution)/shard_map/ppermute | solution.py:24
  40.9 42.0 %collective-permute-start.14 = (bf16[4,2,4,16,512]{4,3,2,1,0:T(8,128)(2,1)S(1)}, bf16[4,2,4,16,512]{4,3,2,1,0:T(8,128)(2,1)S(1)}, u32[]{:S(2)}, u32[]{:S(2)}) collective-permute-start(bf16[4,2,4,16,512]{4,3,2,1,0:T(8,128)(2,1)S(1)} %pad_maximum_fusion.2), channel_id=1, source_target_pairs={{0,31},{1,24},{2,25},{3,26},{4,27},{5,28},{6,29},{7,30},{8,7},{9,0... | collective-permute-start | bytes 1572872 | tf_op jit(solution)/shard_map/ppermute | solution.py:24
  49.6 40.4 %collective-permute-start.2 = (bf16[4,2,4,16,384]{4,3,2,1,0:T(8,128)(2,1)S(1)}, bf16[4,2,4,16,384]{4,3,2,1,0:T(8,128)(2,1)S(1)}, u32[]{:S(2)}, u32[]{:S(2)}) collective-permute-start(bf16[4,2,4,16,384]{4,3,2,1,0:T(8,128)(2,1)S(1)} %pad_maximum_fusion.8), channel_id=1, source_target_pairs={{0,31},{1,24},{2,25},{3,26},{4,27},{5,28},{6,29},{7,30},{8,7},{9,0... | collective-permute-start | bytes 1179656 | tf_op jit(solution)/shard_map/ppermute | solution.py:24
  67.4 23.2 %collective-permute-start.1 = (bf16[4,2,4,16,384]{4,3,2,1,0:T(8,128)(2,1)S(1)}, bf16[4,2,4,16,384]{4,3,2,1,0:T(8,128)(2,1)S(1)}, u32[]{:S(2)}, u32[]{:S(2)}) collective-permute-start(bf16[4,2,4,16,384]{4,3,2,1,0:T(8,128)(2,1)S(1)} %pad_maximum_fusion.7), channel_id=1, source_target_pairs={{0,24},{1,25},{2,26},{3,27},{4,28},{5,29},{6,30},{7,31},{8,0},{9,1... | collective-permute-start | bytes 1179656 | tf_op jit(solution)/shard_map/ppermute | solution.py:24
  70.8 26.2 %collective-permute-start = (bf16[4,2,4,16,384]{4,3,2,1,0:T(8,128)(2,1)S(1)}, bf16[4,2,4,16,384]{4,3,2,1,0:T(8,128)(2,1)S(1)}, u32[]{:S(2)}, u32[]{:S(2)}) collective-permute-start(bf16[4,2,4,16,384]{4,3,2,1,0:T(8,128)(2,1)S(1)} %pad_maximum_fusion.6), channel_id=1, source_target_pairs={{0,7},{1,0},{2,1},{3,2},{4,3},{5,4},{6,5},{7,6},{8,15},{9,8},{10,9... | collective-permute-start | bytes 1179656 | tf_op jit(solution)/shard_map/ppermute | solution.py:24
  75.5 22.5 %collective-permute-start.21 = (bf16[3,2,4,16,512]{4,3,2,1,0:T(8,128)(2,1)S(1)}, bf16[3,2,4,16,512]{4,3,2,1,0:T(8,128)(2,1)S(1)}, u32[]{:S(2)}, u32[]{:S(2)}) collective-permute-start(bf16[3,2,4,16,512]{4,3,2,1,0:T(8,128)(2,1)S(1)} %get-tuple-element.41), channel_id=1, source_target_pairs={{0,1},{1,2},{2,3},{3,4},{4,5},{5,6},{6,7},{7,0},{8,9},{9,10},{10,1... | collective-permute-start | bytes 1179656 | tf_op jit(solution)/shard_map/ppermute | solution.py:24
  82.9 14.1 %collective-permute-start.10 = (bf16[3,2,4,16,384]{4,3,2,1,0:T(8,128)(2,1)S(1)}, bf16[3,2,4,16,384]{4,3,2,1,0:T(8,128)(2,1)S(1)}, u32[]{:S(2)}, u32[]{:S(2)}) collective-permute-start(bf16[3,2,4,16,384]{4,3,2,1,0:T(8,128)(2,1)S(1)} %get-tuple-element.34), channel_id=1, source_target_pairs={{0,8},{1,9},{2,10},{3,11},{4,12},{5,13},{6,14},{7,15},{8,16},{9,17... | collective-permute-start | bytes 884744 | tf_op jit(solution)/shard_map/ppermute | solution.py:24
  90.0 22.1 %collective-permute-start.22 = (bf16[3,2,4,16,512]{4,3,2,1,0:T(8,128)(2,1)S(1)}, bf16[3,2,4,16,512]{4,3,2,1,0:T(8,128)(2,1)S(1)}, u32[]{:S(2)}, u32[]{:S(2)}) collective-permute-start(bf16[3,2,4,16,512]{4,3,2,1,0:T(8,128)(2,1)S(1)} %get-tuple-element.42), channel_id=1, source_target_pairs={{0,8},{1,9},{2,10},{3,11},{4,12},{5,13},{6,14},{7,15},{8,16},{9,17... | collective-permute-start | bytes 1179656 | tf_op jit(solution)/shard_map/ppermute | solution.py:24
  90.7 30.8 %collective-permute-start.23 = (bf16[3,2,4,16,512]{4,3,2,1,0:T(8,128)(2,1)S(1)}, bf16[3,2,4,16,512]{4,3,2,1,0:T(8,128)(2,1)S(1)}, u32[]{:S(2)}, u32[]{:S(2)}) collective-permute-start(bf16[3,2,4,16,512]{4,3,2,1,0:T(8,128)(2,1)S(1)} %get-tuple-element.43), channel_id=1, source_target_pairs={{0,9},{1,10},{2,11},{3,12},{4,13},{5,14},{6,15},{7,8},{8,17},{9,18... | collective-permute-start | bytes 1179656 | tf_op jit(solution)/shard_map/ppermute | solution.py:24
  97.0 24.5 %collective-permute-start.15 = (bf16[3,2,4,16,512]{4,3,2,1,0:T(8,128)(2,1)S(1)}, bf16[3,2,4,16,512]{4,3,2,1,0:T(8,128)(2,1)S(1)}, u32[]{:S(2)}, u32[]{:S(2)}) collective-permute-start(bf16[3,2,4,16,512]{4,3,2,1,0:T(8,128)(2,1)S(1)} %get-tuple-element.37), channel_id=1, source_target_pairs={{0,1},{1,2},{2,3},{3,4},{4,5},{5,6},{6,7},{7,0},{8,9},{9,10},{10,1... | collective-permute-start | bytes 1179656 | tf_op jit(solution)/shard_map/ppermute | solution.py:24
  97.0 34.3 %collective-permute-start.16 = (bf16[3,2,4,16,512]{4,3,2,1,0:T(8,128)(2,1)S(1)}, bf16[3,2,4,16,512]{4,3,2,1,0:T(8,128)(2,1)S(1)}, u32[]{:S(2)}, u32[]{:S(2)}) collective-permute-start(bf16[3,2,4,16,512]{4,3,2,1,0:T(8,128)(2,1)S(1)} %get-tuple-element.38), channel_id=1, source_target_pairs={{0,8},{1,9},{2,10},{3,11},{4,12},{5,13},{6,14},{7,15},{8,16},{9,17... | collective-permute-start | bytes 1179656 | tf_op jit(solution)/shard_map/ppermute | solution.py:24
  98.0 37.2 %collective-permute-start.17 = (bf16[3,2,4,16,512]{4,3,2,1,0:T(8,128)(2,1)S(1)}, bf16[3,2,4,16,512]{4,3,2,1,0:T(8,128)(2,1)S(1)}, u32[]{:S(2)}, u32[]{:S(2)}) collective-permute-start(bf16[3,2,4,16,512]{4,3,2,1,0:T(8,128)(2,1)S(1)} %get-tuple-element.39), channel_id=1, source_target_pairs={{0,9},{1,10},{2,11},{3,12},{4,13},{5,14},{6,15},{7,8},{8,17},{9,18... | collective-permute-start | bytes 1179656 | tf_op jit(solution)/shard_map/ppermute | solution.py:24
  112.2 31.8 %collective-permute-start.11 = (bf16[3,2,4,16,384]{4,3,2,1,0:T(8,128)(2,1)S(1)}, bf16[3,2,4,16,384]{4,3,2,1,0:T(8,128)(2,1)S(1)}, u32[]{:S(2)}, u32[]{:S(2)}) collective-permute-start(bf16[3,2,4,16,384]{4,3,2,1,0:T(8,128)(2,1)S(1)} %get-tuple-element.35), channel_id=1, source_target_pairs={{0,9},{1,10},{2,11},{3,12},{4,13},{5,14},{6,15},{7,8},{8,17},{9,18... | collective-permute-start | bytes 884744 | tf_op jit(solution)/shard_map/ppermute | solution.py:24
  121.5 22.4 %collective-permute-start.9 = (bf16[3,2,4,16,384]{4,3,2,1,0:T(8,128)(2,1)S(1)}, bf16[3,2,4,16,384]{4,3,2,1,0:T(8,128)(2,1)S(1)}, u32[]{:S(2)}, u32[]{:S(2)}) collective-permute-start(bf16[3,2,4,16,384]{4,3,2,1,0:T(8,128)(2,1)S(1)} %get-tuple-element.33), channel_id=1, source_target_pairs={{0,1},{1,2},{2,3},{3,4},{4,5},{5,6},{6,7},{7,0},{8,9},{9,10},{10,1... | collective-permute-start | bytes 884744 | tf_op jit(solution)/shard_map/ppermute | solution.py:24
  121.5 24.2 %collective-permute-start.3 = (bf16[3,2,4,16,384]{4,3,2,1,0:T(8,128)(2,1)S(1)}, bf16[3,2,4,16,384]{4,3,2,1,0:T(8,128)(2,1)S(1)}, u32[]{:S(2)}, u32[]{:S(2)}) collective-permute-start(bf16[3,2,4,16,384]{4,3,2,1,0:T(8,128)(2,1)S(1)} %get-tuple-element.29), channel_id=1, source_target_pairs={{0,1},{1,2},{2,3},{3,4},{4,5},{5,6},{6,7},{7,0},{8,9},{9,10},{10,1... | collective-permute-start | bytes 884744 | tf_op jit(solution)/shard_map/ppermute | solution.py:24
  131.2 16.9 %collective-permute-start.4 = (bf16[3,2,4,16,384]{4,3,2,1,0:T(8,128)(2,1)S(1)}, bf16[3,2,4,16,384]{4,3,2,1,0:T(8,128)(2,1)S(1)}, u32[]{:S(2)}, u32[]{:S(2)}) collective-permute-start(bf16[3,2,4,16,384]{4,3,2,1,0:T(8,128)(2,1)S(1)} %get-tuple-element.30), channel_id=1, source_target_pairs={{0,8},{1,9},{2,10},{3,11},{4,12},{5,13},{6,14},{7,15},{8,16},{9,17... | collective-permute-start | bytes 884744 | tf_op jit(solution)/shard_map/ppermute | solution.py:24
  135.2 15.0 %collective-permute-start.5 = (bf16[3,2,4,16,384]{4,3,2,1,0:T(8,128)(2,1)S(1)}, bf16[3,2,4,16,384]{4,3,2,1,0:T(8,128)(2,1)S(1)}, u32[]{:S(2)}, u32[]{:S(2)}) collective-permute-start(bf16[3,2,4,16,384]{4,3,2,1,0:T(8,128)(2,1)S(1)} %get-tuple-element.31), channel_id=1, source_target_pairs={{0,9},{1,10},{2,11},{3,12},{4,13},{5,14},{6,15},{7,8},{8,17},{9,18... | collective-permute-start | bytes 884744 | tf_op jit(solution)/shard_map/ppermute | solution.py:24

commit v2 on v1

v2 whole, which is shorter than its diff:
```python
import math

import jax
import jax.numpy as jnp
from jax import lax
from jax.experimental import pallas as pl
from jax.experimental.pallas import tpu as pltpu
from jax.sharding import PartitionSpec as P

WW = 8
HEAD_DIM = 128
AXES = ("tm", "rows")
VMEM_BYTES = 40 * 1024 * 1024


def moved(value, parity, by_rows):
    times, rows = lax.axis_size("tm"), lax.axis_size("rows")
    pairs = []
    for t in range(times):
        step = 0 if parity is None else (1 if t % 2 == parity else -1)
        for r in range(rows):
            pairs.append((t * rows + r, ((t + step) % times) * rows + (r + by_rows) % rows))
    return lax.ppermute(value, AXES, pairs)


def late_half(shape):
    return lax.broadcasted_iota(jnp.int32, shape, 1) >= WW // 2


def split_windows(parts):
    tokens = jnp.concatenate(parts, axis=0).astype(jnp.float32)
    first, second = tokens[:, :WW], tokens[:, WW:]
    late = late_half(first.shape)
    flat = (first.shape[0] * WW, first.shape[2])
    inner = jnp.where(late, first, second).reshape(flat).astype(jnp.bfloat16)
    outer = jnp.where(late, second, first).reshape(flat).astype(jnp.bfloat16)
    return inner, outer


def join_windows(inner, outer):
    shape = (inner.shape[0] // WW, WW, inner.shape[1])
    inner, outer = inner.reshape(shape), outer.reshape(shape)
    late = late_half(shape)
    first = jnp.where(late, inner, outer)
    second = jnp.where(late, outer, inner)
    return jnp.concatenate((first, second), axis=1).astype(jnp.bfloat16)


def dot(a, b, dims):
    return lax.dot_general(a, b, (dims, ((), ())), preferred_element_type=jnp.float32)


def key_sum(value):
    return jnp.sum(value, axis=0, keepdims=True)


def products(query, key, value, grad):
    factor = 1.0 / math.sqrt(HEAD_DIM)
    scores = dot(key, query, ((1,), (1,))) * factor
    weight_grad = dot(value, grad, ((1,), (1,)))
    return scores, weight_grad


def partial_stats(query, key, value, grad):
    scores, weight_grad = products(query, key, value, grad)
    top = jnp.max(scores, axis=0, keepdims=True)
    powers = jnp.exp(scores - top)
    return top, key_sum(powers), key_sum(powers * weight_grad)


def partial_grads(query, key, value, grad, mine, other):
    factor = 1.0 / math.sqrt(HEAD_DIM)
    top = jnp.maximum(mine[0], other[0])
    scale_mine, scale_other = jnp.exp(mine[0] - top), jnp.exp(other[0] - top)
    inverse = 1.0 / (mine[1] * scale_mine + other[1] * scale_other)
    row_dot = (mine[2] * scale_mine + other[2] * scale_other) * inverse
    scores, weight_grad = products(query, key, value, grad)
    weights = jnp.exp(scores - top) * inverse
    score_grad = (weights * (weight_grad - row_dot) * factor).astype(jnp.bfloat16)
    value_out = dot(weights.astype(jnp.bfloat16), grad, ((1,), (0,)))
    key_out = dot(score_grad, query, ((1,), (0,)))
    query_out = dot(score_grad, key, ((0,), (0,)))
    return query_out, key_out, value_out


def window_tokens(refs, head):
    q_ref, k_ref, v_ref, g_ref, qg_ref, key_row_ref, value_row_ref, near_ref, corner_ref = refs
    frames, rows, columns, _ = q_ref.shape
    lanes = pl.ds(head * HEAD_DIM, HEAD_DIM)
    flat = lambda p: p.reshape(frames * rows, columns, HEAD_DIM)
    at = lambda ref, *index: flat(ref[(*index, slice(None), slice(None), slice(None), lanes)])
    query = split_windows([at(q_ref), at(qg_ref, 0)])
    grad = split_windows([at(g_ref), at(qg_ref, 1)])
    key = split_windows([at(k_ref), at(key_row_ref, 0)])
    value = split_windows([at(v_ref), at(value_row_ref, 0)])
    far_query = split_windows([at(near_ref, 0), at(corner_ref, 0)])
    far_grad = split_windows([at(near_ref, 1), at(corner_ref, 1)])
    both = lambda own, far: jnp.concatenate((own, far), axis=0)
    return [
        (both(query[w], far_query[w]), key[w], value[w], both(grad[w], far_grad[w])) for w in (0, 1)
    ]


def stats_kernel(late_ref, *refs):
    out = refs[9]
    for head in range(out.shape[0]):
        found = []
        for window in window_tokens(refs[:9], head):
            found.extend(partial_stats(*window))
        blank = jnp.zeros_like(found[0])
        out[head] = jnp.concatenate(found + [blank] * (out.shape[1] - len(found)), axis=0)


def grads_kernel(late_ref, *refs):
    mine_ref, other_ref, kept_out = refs[9:12]
    if len(refs) == 14:
        row_outs = [refs[12].at[index] for index in range(3)]
        near_out, corner_out = refs[13].at[0], refs[13].at[1]
    else:
        row_outs = [refs[12], refs[13].at[0], refs[13].at[1]]
        near_out, corner_out = refs[14:]
    _, frames, rows, columns, width = kept_out.shape
    shape = (2, frames, rows, columns, HEAD_DIM)
    for head in range(width // HEAD_DIM):
        lanes = pl.ds(head * HEAD_DIM, HEAD_DIM)
        grads = []
        for w, window in enumerate(window_tokens(refs[:9], head)):
            mine = [mine_ref[head, pl.ds(3 * w + i, 1)] for i in range(3)]
            other = [other_ref[head, pl.ds(3 * w + i, 1)] for i in range(3)]
            half = window[1].shape[0]
            other = [jnp.concatenate((o[:, half:], o[:, :half]), axis=1) for o in other]
            grads.append(partial_grads(*window, mine, other))
        kept = [[g[0][:half] for g in grads], [g[1] for g in grads], [g[2] for g in grads]]
        for index, windows in enumerate(kept):
            tokens = join_windows(*windows).reshape(shape)
            kept_out[index, :, :, :, lanes] = tokens[0]
            row_outs[index][:, :, :, lanes] = tokens[1]
        tokens = join_windows(*[g[0][half:] for g in grads]).reshape(shape)
        near_out[:, :, :, lanes] = tokens[0]
        corner_out[:, :, :, lanes] = tokens[1]


def lane_block(shape, lanes, place=None):
    index = lambda h, late: ((0,) * (len(shape) - 1) if place is None else place(late)) + (h,)
    return pl.BlockSpec(tuple(shape[:-1]) + (lanes,), index)


def heads_per_step(heads):
    return 2 if heads % 2 == 0 else 1


def small():
    return pl.CostEstimate(flops=1, bytes_accessed=1, transcendentals=0)


def called(kernel, late, operands, in_specs, out_specs, out_shape, steps, aliases=None):
    return pl.pallas_call(
        kernel,
        grid_spec=pltpu.PrefetchScalarGridSpec(
            num_scalar_prefetch=1, grid=(steps,), in_specs=in_specs, out_specs=out_specs
        ),
        out_shape=out_shape,
        input_output_aliases=aliases or {},
        compiler_params=pltpu.CompilerParams(vmem_limit_bytes=VMEM_BYTES),
        cost_estimate=small(),
    )(late, *operands)


def window_specs(inputs, received, lanes):
    frames, rows, columns, _ = inputs[0].shape
    own = lane_block((frames // 2, rows // 2, columns, 0), lanes, lambda late: (late[0], 1, 0))
    return [own] * 4 + [lane_block(r.shape, lanes) for r in received]


def stats_block(heads, length):
    return pl.BlockSpec((heads, 8, length), lambda h, late: (h, 0, 0))


def family_stats(late, inputs, received):
    frames, rows, _, features = inputs[0].shape
    heads, length = features // HEAD_DIM, frames * rows * WW
    step = heads_per_step(heads)
    return called(
        stats_kernel,
        late,
        (*inputs, *received),
        window_specs(inputs, received, step * HEAD_DIM),
        stats_block(step, length),
        jax.ShapeDtypeStruct((heads, 8, length), jnp.float32),
        heads // step,
    )


def family_grads(late, inputs, received, mine, other, joined):
    frames, rows, columns, features = inputs[0].shape
    heads, length = features // HEAD_DIM, frames * rows * WW
    step = heads_per_step(heads)
    sent = jax.ShapeDtypeStruct((frames // 2, rows // 2, columns, features), jnp.bfloat16)
    kept = jax.ShapeDtypeStruct((3,) + sent.shape, jnp.bfloat16)
    two = jax.ShapeDtypeStruct((2,) + sent.shape, jnp.bfloat16)
    shapes = [kept, kept, two] if joined else [kept, sent, two, sent, sent]
    return called(
        grads_kernel,
        late,
        (*inputs, *received, mine, other),
        window_specs(inputs, received, step * HEAD_DIM) + [stats_block(step, length)] * 2,
        [lane_block(s.shape, step * HEAD_DIM) for s in shapes],
        shapes,
        heads // step,
    )


def place_pair_kernel(late_ref, *refs):
    own_ref, outs = refs[0], refs[-2:]
    row_ref = refs[1]
    first = row_ref.shape[0] - len(outs)
    for index, out in enumerate(outs):
        half = out.shape[1] // 2
        out[:, half:] = own_ref[1 + index]
        out[:, :half] = row_ref[first + index]


def place_sum_kernel(late_ref, *refs):
    own_ref, row_ref, near_ref, corner_ref = refs[:4]
    out = refs[-1]
    half = out.shape[1] // 2
    row_ref, near_ref = [r if r.ndim == 4 else r.at[0] for r in (row_ref, near_ref)]
    total = lambda a, b: (a.astype(jnp.float32) + b.astype(jnp.float32)).astype(jnp.bfloat16)
    out[:, half:] = total(own_ref[0], near_ref[...])
    out[:, :half] = total(row_ref[...], corner_ref[...])


def placed(kernel, number, late, outs, pieces, counts, whole):
    frames, rows, columns, features = whole.shape
    lanes = features // heads_per_step(features // HEAD_DIM)
    outs = () if outs is None else outs
    shape = lambda p, n: ((n,) + p.shape[1:]) if p.ndim == 5 else p.shape
    full = lane_block((frames // 2, rows, columns, 0), lanes, lambda late: (late[0], 0, 0))
    return called(
        kernel,
        late,
        (*pieces, *outs),
        [lane_block(shape(p, n), lanes) for p, n in zip(pieces, counts)]
        + [pl.BlockSpec(memory_space=pl.ANY)] * len(outs),
        [full] * number,
        [jax.ShapeDtypeStruct(whole.shape, whole.dtype)] * number,
        features // lanes,
        {1 + len(pieces) + i: i for i in range(len(outs))},
    )


def after(value, *earlier):
    return lax.optimization_barrier((value,) + earlier)[0]


def shards(queries, keys, values, out_grad):
    inputs = (queries, keys, values, out_grad)
    frames, rows, columns, features = queries.shape
    time = lax.axis_index("tm")
    late = [jnp.where(time % 2 == parity, 1, 0).astype(jnp.int32) for parity in (0, 1)]

    def cut(xs, parity, row_start):
        sizes = (frames // 2, rows // 2, columns, features)
        start = (late[parity] * (frames // 2), row_start, 0, 0)
        return jnp.stack([lax.dynamic_slice(x, start, sizes) for x in xs])

    def near_of(parity, *wait):
        return moved(after(cut((queries, out_grad), parity, rows // 2), *wait), parity, 0)

    def row_of(xs, parity, *wait):
        return moved(after(cut(xs, parity, 0), *wait), None, -1)

    def rows_of_both(parity, *wait):
        return [row_of((x,), parity, *wait) for x in (keys, values)]

    qg = (queries, out_grad)
    spot = [flag.reshape(1) for flag in late]
    near0 = near_of(0)
    row_qg0 = row_of(qg, 0)
    corner0 = moved(row_qg0, 0, 0)
    row_kv0 = rows_of_both(0, row_qg0)
    near1 = near_of(1, near0)
    got0 = (row_qg0, *row_kv0, near0, corner0)
    stats0 = family_stats(spot[0], inputs, got0)
    other0 = moved(stats0, 0, 0)
    row_qg1 = jnp.concatenate([row_of((x,), 1, *row_kv0) for x in qg])
    row_kv1 = rows_of_both(1, other0)
    corner1 = moved(after(row_qg1, other0, near1), 1, 0)
    kept0, row0, far0 = family_grads(spot[0], inputs, got0, stats0, other0, True)
    got1 = (row_qg1, *row_kv1, near1, after(corner1, far0))
    stats1 = family_stats(spot[1], inputs, got1)
    other1 = moved(stats1, 1, 0)
    row0 = moved(after(row0, *row_kv1), None, 1)
    far0 = moved(after(far0, other1), 0, 0)
    kept1, row1, pair1, near_b1, corner_b1 = family_grads(
        spot[1], inputs, got1, stats1, after(other1, row0), False
    )
    near_b1 = moved(after(near_b1, far0), 1, 0)
    corner_b1 = moved(corner_b1, 1, 1)
    row1, pair1 = moved(row1, None, 1), moved(pair1, None, 1)
    corner_b0 = moved(after(far0[1], row1), None, 1)
    pair = placed(place_pair_kernel, 2, spot[0], None, (kept0, row0), (3, 3), queries)
    total = placed(
        place_sum_kernel, 1, spot[0], None, (kept0, row0, far0, corner_b0), (1, 1, 1, 1), queries
    )
    pair = placed(place_pair_kernel, 2, spot[1], pair, (kept1, pair1), (3, 2), queries)
    total = placed(
        place_sum_kernel, 1, spot[1], total, (kept1, row1, near_b1, corner_b1), (1, 1, 1, 1), queries
    )
    return (total[0], pair[0], pair[1])


def solution(mesh):
    spec = P("tm", "rows", None, None)
    return jax.shard_map(
        shards,
        mesh=mesh,
        in_specs=(spec,) * 4,
        out_specs=(spec,) * 3,
        check_vma=False,
    )
```

time: 152 us -> 147 us (0.967)
  starting transfers between devices: 66.8 us -> 31.7 us
  waiting for transfers between devices: 55.6 us -> 78.6 us
  Pallas kernels: 23.9 us -> 32.5 us
    ppermute x24 -> x20, starting transfers between devices: 66.8 us -> 31.7 us  [moved(): return lax.ppermute(value, AXES, pairs)]
    ppermute x24 -> x20, waiting for transfers between devices: 55.6 us -> 78.6 us  [moved(): return lax.ppermute(value, AXES, pairs)]
    pallas_call x8, Pallas kernels: 23.9 us -> 32.5 us  [called(): pl.pallas_call(kernel, grid_spec=pltpu.PrefetchScalarGridSpec(num_scalar_...]
    another operation x4 -> x3, local copies, waits for them, and re-layouts: 3.69 us -> 2.38 us  [cut(): return jnp.stack([lax.dynamic_slice(x, start, sizes) for x in xs])]
  transfers between devices with their start and end apart: 24 -> 20, of which waited for: 11 -> 13; matrix products, arithmetic and copies ran while one was open for 1% -> 0% of each run, Pallas kernels for 15% -> 21%
where the time goes in v2:
time: 147 us; the launch traced here: 146 us
  waiting for transfers between devices  78.6 us (53%)
  Pallas kernels  32.5 us (22%)
  starting transfers between devices  31.7 us (22%)
  local copies, waits for them, and re-layouts  2.5 us (2%)
    ppermute x20, waiting for transfers between devices, moved(): return lax.ppermute(value, AXES, pairs)  78.6 us
    pallas_call x8, Pallas kernels, called(): pl.pallas_call(kernel, grid_spec=pltpu.PrefetchScalarGridSpec(num_scalar_...  32.5 us
    ppermute x20, starting transfers between devices, moved(): return lax.ppermute(value, AXES, pairs)  31.7 us
  transfers between devices with their start and end apart: 20, of which 13 were waited for; matrix products, arithmetic and copies ran while one was open for 0% of the time, Pallas kernels for 21%

profile of v2, /device:TPU:0, one launch (start us, length us, event | category | flops | bytes accessed | tf_op | source)
XLA Modules:
  0.0 146.3 jit_solution(7956561215645482564)
XLA Ops:
  0.7 2.2 %dynamic-slice_bitcast_fusion = (bf16[1,2,4,16,1792]{4,3,2,1,0:T(8,128)(2,1)S(1)}, bf16[1,2,4,16,1792]{4,3,2,1,0:T(8,128)(2,1)S(1)}, bf16[1,2,4,16,1792]{4,3,2,1...) fusion(bf16[4,8,16,1792]{3,2,1,0:T(8,128)(2,1)} %refs_3_.7, ...), kind=kLoop, calls=%fused_computation.4 | loop fusion | bytes 7340040 | tf_op jit(solution)/shard_map/stack | solution.py:265
  2.9 0.0 copy-start.3
  2.9 0.1 pad_maximum_fusion
  3.0 4.5 %collective-permute-start = (bf16[2,2,4,16,1792]{4,3,2,1,0:T(8,128)(2,1)S(1)}, bf16[2,2,4,16,1792]{4,3,2,1,0:T(8,128)(2,1)S(1)}, u32[]{:S(2)}, u32[]{:S(2)}) collective-permute-start(bf16[2,2,4,16,1792]{4,3,2,1,0:T(8,128)(2,1)S(1)} %pad_maximum_fusion), channel_id=1, source_target_pairs={{0,7},{1,0},{2,1},{3,2},{4,3},{5,4},{6,5},{7,6},{8,15},{9,8},{10,9... | collective-permute-start | bytes 2752520 | tf_op jit(solution)/shard_map/ppermute | solution.py:23
  7.6 0.1 pad_maximum_fusion.1
  7.6 1.6 %collective-permute-start.5 = (bf16[2,2,4,16,1792]{4,3,2,1,0:T(8,128)(2,1)S(1)}, bf16[2,2,4,16,1792]{4,3,2,1,0:T(8,128)(2,1)S(1)}, u32[]{:S(2)}, u32[]{:S(2)}) collective-permute-start(bf16[2,2,4,16,1792]{4,3,2,1,0:T(8,128)(2,1)S(1)} %pad_maximum_fusion.1), channel_id=1, source_target_pairs={{0,8},{1,9},{2,10},{3,11},{4,12},{5,13},{6,14},{7,15},{8,0},{9,1},... | collective-permute-start | bytes 2752520 | tf_op jit(solution)/shard_map/ppermute | solution.py:23
  9.2 0.1 dynamic-slice_bitcast_fusion.5
  9.3 0.0 copy-start
  9.3 0.0 copy-start.1
  9.3 0.1 dynamic-slice_bitcast_fusion.2
  9.4 9.1 %collective-permute-done.refs_4_ = bf16[2,2,4,16,1792]{4,3,2,1,0:T(8,128)(2,1)S(1)} collective-permute-done((bf16[2,2,4,16,1792]{4,3,2,1,0:T(8,128)(2,1)S(1)}, bf16[2,2,4,16,1792]{4,3,2,1,0:T(8,128)(2,1)S(1)}, u32[]{:S(2)}, u32[]{:S(2)}) %collective-permute-start) | collective-permute-done | bytes 917536 | tf_op jit(solution)/shard_map/ppermute | solution.py:23
  18.5 3.7 %collective-permute-start.1 = (bf16[1,2,4,16,1792]{4,3,2,1,0:T(8,128)(2,1)S(1)}, bf16[1,2,4,16,1792]{4,3,2,1,0:T(8,128)(2,1)S(1)}, u32[]{:S(2)}, u32[]{:S(2)}) collective-permute-start(bf16[1,2,4,16,1792]{4,3,2,1,0:T(8,128)(2,1)S(1)} %get-tuple-element.29), channel_id=1, source_target_pairs={{0,7},{1,0},{2,1},{3,2},{4,3},{5,4},{6,5},{7,6},{8,15},{9,8},{10,9... | collective-permute-start | bytes 1376264 | tf_op jit(solution)/shard_map/ppermute | solution.py:23
  22.2 0.0 collective-permute-start.2
  22.2 1.5 %collective-permute-start.6 = (bf16[2,2,4,16,1792]{4,3,2,1,0:T(8,128)(2,1)S(1)}, bf16[2,2,4,16,1792]{4,3,2,1,0:T(8,128)(2,1)S(1)}, u32[]{:S(2)}, u32[]{:S(2)}) collective-permute-start(bf16[2,2,4,16,1792]{4,3,2,1,0:T(8,128)(2,1)S(1)} %collective-permute-done.refs_4_), channel_id=1, source_target_pairs={{0,8},{1,9},{2,10},{3,11},{4,12},{5,13},{6,14},{7,15},{8,0},{9,1},... | collective-permute-start | bytes 2752520 | tf_op jit(solution)/shard_map/ppermute | solution.py:23
  23.7 4.5 %collective-permute-done.1.refs_5_ = bf16[1,2,4,16,1792]{4,3,2,1,0:T(8,128)(2,1)S(1)} collective-permute-done((bf16[1,2,4,16,1792]{4,3,2,1,0:T(8,128)(2,1)S(1)}, bf16[1,2,4,16,1792]{4,3,2,1,0:T(8,128)(2,1)S(1)}, u32[]{:S(2)}, u32[]{:S(2)}) %collective-permute-start.1) | collective-permute-done | bytes 458784 | tf_op jit(solution)/shard_map/ppermute | solution.py:23
  28.2 4.9 %collective-permute-done.2.refs_6_ = bf16[1,2,4,16,1792]{4,3,2,1,0:T(8,128)(2,1)S(1)} collective-permute-done((bf16[1,2,4,16,1792]{4,3,2,1,0:T(8,128)(2,1)S(1)}, bf16[1,2,4,16,1792]{4,3,2,1,0:T(8,128)(2,1)S(1)}, u32[]{:S(2)}, u32[]{:S(2)}) %collective-permute-start.2) | collective-permute-done | bytes 458784 | tf_op jit(solution)/shard_map/ppermute | solution.py:23
  33.1 3.7 %collective-permute-start.3 = (bf16[1,2,4,16,1792]{4,3,2,1,0:T(8,128)(2,1)S(1)}, bf16[1,2,4,16,1792]{4,3,2,1,0:T(8,128)(2,1)S(1)}, u32[]{:S(2)}, u32[]{:S(2)}) collective-permute-start(bf16[1,2,4,16,1792]{4,3,2,1,0:T(8,128)(2,1)S(1)} %get-tuple-element.31), channel_id=1, source_target_pairs={{0,7},{1,0},{2,1},{3,2},{4,3},{5,4},{6,5},{7,6},{8,15},{9,8},{10,9... | collective-permute-start | bytes 1376264 | tf_op jit(solution)/shard_map/ppermute | solution.py:23
  36.8 0.1 pad_maximum_fusion.2
  36.9 2.5 %collective-permute-start.10 = (bf16[2,2,4,16,1792]{4,3,2,1,0:T(8,128)(2,1)S(1)}, bf16[2,2,4,16,1792]{4,3,2,1,0:T(8,128)(2,1)S(1)}, u32[]{:S(2)}, u32[]{:S(2)}) collective-permute-start(bf16[2,2,4,16,1792]{4,3,2,1,0:T(8,128)(2,1)S(1)} %pad_maximum_fusion.2), channel_id=1, source_target_pairs={{0,24},{1,25},{2,26},{3,27},{4,28},{5,29},{6,30},{7,31},{8,16},{9,... | collective-permute-start | bytes 2752520 | tf_op jit(solution)/shard_map/ppermute | solution.py:23
  39.4 9.3 %collective-permute-done.6.refs_8_ = bf16[2,2,4,16,1792]{4,3,2,1,0:T(8,128)(2,1)S(1)} collective-permute-done((bf16[2,2,4,16,1792]{4,3,2,1,0:T(8,128)(2,1)S(1)}, bf16[2,2,4,16,1792]{4,3,2,1,0:T(8,128)(2,1)S(1)}, u32[]{:S(2)}, u32[]{:S(2)}) %collective-permute-start.6) | collective-permute-done | bytes 917536 | tf_op jit(solution)/shard_map/ppermute | solution.py:23
  48.7 4.0 %shard_map.67.refs_9_ = f32[14,8,256]{2,1,0:T(8,128)S(1)} custom-call(s32[1]{0:T(128)} %bitcast.8.late_ref, bf16[4,8,16,1792]{3,2,1,0:T(8,128)(2,1)S(1)} %copy-done, bf16[4,8,16,1792]{3,2,1,0:T(8,128)(2,1)S(1)} %copy-done.3, bf16[4,8,16,1792]{3,2,1,0:T(8,128)(2,1)S(1)} %copy-done.4, bf16[4,8,16,1792]{3,2,1,0:T(8,128)(2,1)S(1)} %copy-done.1, ...), custom_call_target="tpu_custom_call" | custom-call | flops 1 | bytes 1 | tf_op jit(solution)/shard_map/pallas_call | solution.py:157
  52.7 2.1 %collective-permute-start.7 = (f32[14,8,256]{2,1,0:T(8,128)S(1)}, f32[14,8,256]{2,1,0:T(8,128)S(1)}, u32[]{:S(2)}, u32[]{:S(2)}) collective-permute-start(f32[14,8,256]{2,1,0:T(8,128)S(1)} %shard_map.67.refs_9_), channel_id=1, source_target_pairs={{0,8},{1,9},{2,10},{3,11},{4,12},{5,13},{6,14},{7,15},{8,0},{9,1},... | collective-permute-start | bytes 344072 | tf_op jit(solution)/shard_map/ppermute | solution.py:23
  54.8 14.1 %collective-permute-done.10.refs_7_ = bf16[2,2,4,16,1792]{4,3,2,1,0:T(8,128)(2,1)S(1)} collective-permute-done((bf16[2,2,4,16,1792]{4,3,2,1,0:T(8,128)(2,1)S(1)}, bf16[2,2,4,16,1792]{4,3,2,1,0:T(8,128)(2,1)S(1)}, u32[]{:S(2)}, u32[]{:S(2)}) %collective-permute-start.10) | collective-permute-done | bytes 917536 | tf_op jit(solution)/shard_map/ppermute | solution.py:23
  68.9 0.0 collective-permute-done.7.refs_10_
  69.0 2.7 %collective-permute-start.11 = (bf16[2,2,4,16,1792]{4,3,2,1,0:T(8,128)(2,1)S(1)}, bf16[2,2,4,16,1792]{4,3,2,1,0:T(8,128)(2,1)S(1)}, u32[]{:S(2)}, u32[]{:S(2)}) collective-permute-start(bf16[2,2,4,16,1792]{4,3,2,1,0:T(8,128)(2,1)S(1)} %constant_dynamic-update-slice_fusion.refs_4_), channel_id=1, source_target_pairs={{0,24},{1,25},{2,26},{3,27},{4,28},{5,29},{6,30},{7,31},{8,16},{9,... | collective-permute-start | bytes 2752520 | tf_op jit(solution)/shard_map/ppermute | solution.py:23
  71.7 2.6 %collective-permute-start.8 = (bf16[1,2,4,16,1792]{4,3,2,1,0:T(8,128)(2,1)S(1)}, bf16[1,2,4,16,1792]{4,3,2,1,0:T(8,128)(2,1)S(1)}, u32[]{:S(2)}, u32[]{:S(2)}) collective-permute-start(bf16[1,2,4,16,1792]{4,3,2,1,0:T(8,128)(2,1)S(1)} %get-tuple-element.33), channel_id=1, source_target_pairs={{0,7},{1,0},{2,1},{3,2},{4,3},{5,4},{6,5},{7,6},{8,15},{9,8},{10,9... | collective-permute-start | bytes 1376264 | tf_op jit(solution)/shard_map/ppermute | solution.py:23
  74.3 1.1 collective-permute-start.9
  75.4 9.5 %shard_map.68 = (bf16[3,2,4,16,1792]{4,3,2,1,0:T(8,128)(2,1)S(1)}, bf16[3,2,4,16,1792]{4,3,2,1,0:T(8,128)(2,1)S(1)}, bf16[2,2,4,16,1792]{4,3,2,1,0:T(8,128)(2,1)S(1)}) custom-call(s32[1]{0:T(128)} %bitcast.8.late_ref, bf16[4,8,16,1792]{3,2,1,0:T(8,128)(2,1)S(1)} %copy-done, bf16[4,8,16,1792]{3,2,1,0:T(8,128)(2,1)S(1)} %copy-done.3, ...), custom_call_target="tpu_custom_call" | custom-call | flops 1 | bytes 1 | tf_op jit(solution)/shard_map/pallas_call | solution.py:157
  84.9 0.0 collective-permute-done.8.refs_5_
  84.9 0.3 collective-permute-done.9.refs_6_
  85.2 5.2 %collective-permute-done.11.refs_8_ = bf16[2,2,4,16,1792]{4,3,2,1,0:T(8,128)(2,1)S(1)} collective-permute-done((bf16[2,2,4,16,1792]{4,3,2,1,0:T(8,128)(2,1)S(1)}, bf16[2,2,4,16,1792]{4,3,2,1,0:T(8,128)(2,1)S(1)}, u32[]{:S(2)}, u32[]{:S(2)}) %collective-permute-start.11) | collective-permute-done | bytes 917536 | tf_op jit(solution)/shard_map/ppermute | solution.py:23
  90.4 4.0 %shard_map.69.refs_9_ = f32[14,8,256]{2,1,0:T(8,128)S(1)} custom-call(s32[1]{0:T(128)} %bitcast.late_ref, bf16[4,8,16,1792]{3,2,1,0:T(8,128)(2,1)S(1)} %copy-done, bf16[4,8,16,1792]{3,2,1,0:T(8,128)(2,1)S(1)} %copy-done.3, bf16[4,8,16,1792]{3,2,1,0:T(8,128)(2,1)S(1)} %copy-done.4, bf16[4,8,16,1792]{3,2,1,0:T(8,128)(2,1)S(1)} %copy-done.2, ...), custom_call_target="tpu_custom_call" | custom-call | flops 1 | bytes 1 | tf_op jit(solution)/shard_map/pallas_call | solution.py:157
  94.4 2.5 %collective-permute-start.12 = (f32[14,8,256]{2,1,0:T(8,128)S(1)}, f32[14,8,256]{2,1,0:T(8,128)S(1)}, u32[]{:S(2)}, u32[]{:S(2)}) collective-permute-start(f32[14,8,256]{2,1,0:T(8,128)S(1)} %shard_map.69.refs_9_), channel_id=1, source_target_pairs={{0,24},{1,25},{2,26},{3,27},{4,28},{5,29},{6,30},{7,31},{8,16},{9,... | collective-permute-start | bytes 344072 | tf_op jit(solution)/shard_map/ppermute | solution.py:23
  96.9 3.5 %collective-permute-done.12.refs_10_ = f32[14,8,256]{2,1,0:T(8,128)S(1)} collective-permute-done((f32[14,8,256]{2,1,0:T(8,128)S(1)}, f32[14,8,256]{2,1,0:T(8,128)S(1)}, u32[]{:S(2)}, u32[]{:S(2)}) %collective-permute-start.12) | collective-permute-done | bytes 114720 | tf_op jit(solution)/shard_map/ppermute | solution.py:23
  100.4 1.4 collective-permute-start.15
  101.8 3.1 %collective-permute-done.13.refs_1_ = bf16[3,2,4,16,1792]{4,3,2,1,0:T(8,128)(2,1)S(1)} collective-permute-done((bf16[3,2,4,16,1792]{4,3,2,1,0:T(8,128)(2,1)S(1)}, bf16[3,2,4,16,1792]{4,3,2,1,0:T(8,128)(2,1)S(1)}, u32[]{:S(2)}, u32[]{:S(2)}) %collective-permute-start.13) | collective-permute-done | bytes 1376288 | tf_op jit(solution)/shard_map/ppermute | solution.py:23
  104.9 9.5 %shard_map.70 = (bf16[3,2,4,16,1792]{4,3,2,1,0:T(8,128)(2,1)S(1)}, bf16[2,4,16,1792]{3,2,1,0:T(8,128)(2,1)S(1)}, bf16[2,2,4,16,1792]{4,3,2,1,0:T(8,128)(2,1)S(1)...) custom-call(s32[1]{0:T(128)} %bitcast.late_ref, bf16[4,8,16,1792]{3,2,1,0:T(8,128)(2,1)S(1)} %copy-done, ...), custom_call_target="tpu_custom_call" | custom-call | flops 1 | bytes 1 | tf_op jit(solution)/shard_map/pallas_call | solution.py:157
  114.4 0.1 collective-permute-start.14
  114.5 1.2 collective-permute-start.17
  115.7 4.1 %collective-permute-done.15.refs_2_ = bf16[2,2,4,16,1792]{4,3,2,1,0:T(8,128)(2,1)S(1)} collective-permute-done((bf16[2,2,4,16,1792]{4,3,2,1,0:T(8,128)(2,1)S(1)}, bf16[2,2,4,16,1792]{4,3,2,1,0:T(8,128)(2,1)S(1)}, u32[]{:S(2)}, u32[]{:S(2)}) %collective-permute-start.15) | collective-permute-done | bytes 917536 | tf_op jit(solution)/shard_map/ppermute | solution.py:23
  119.9 4.3 %collective-permute-done.14.refs_1_ = bf16[2,4,16,1792]{3,2,1,0:T(8,128)(2,1)S(1)} collective-permute-done((bf16[2,4,16,1792]{3,2,1,0:T(8,128)(2,1)S(1)}, bf16[2,4,16,1792]{3,2,1,0:T(8,128)(2,1)S(1)}, u32[]{:S(2)}, u32[]{:S(2)}) %collective-permute-start.14) | collective-permute-done | bytes 458784 | tf_op jit(solution)/shard_map/ppermute | solution.py:23
  124.2 0.5 collective-permute-start.16
  124.7 1.5 %shard_map.73 = (bf16[4,8,16,1792]{3,2,1,0:T(8,128)(2,1)}, bf16[4,8,16,1792]{3,2,1,0:T(8,128)(2,1)}) custom-call(s32[1]{0:T(128)} %bitcast.8.late_ref, bf16[3,2,4,16,1792]{4,3,2,1,0:T(8,128)(2,1)S(1)} %get-tuple-element.48.refs_0_, bf16[3,2,4,16,1792]{4,3,2,1,0:T(8,128)(2,1)S(1)} %collective-permute-done.13.refs_1_), custom_call_target="tpu_custom_call" | custom-call | flops 1 | bytes 1 | tf_op jit(solution)/shard_map/pallas_call | solution.py:157
  126.2 12.8 %collective-permute-done.19.refs_1_ = bf16[2,2,4,16,1792]{4,3,2,1,0:T(8,128)(2,1)S(1)} collective-permute-done((bf16[2,2,4,16,1792]{4,3,2,1,0:T(8,128)(2,1)S(1)}, bf16[2,2,4,16,1792]{4,3,2,1,0:T(8,128)(2,1)S(1)}, u32[]{:S(2)}, u32[]{:S(2)}) %collective-permute-start.19) | collective-permute-done | bytes 917536 | tf_op jit(solution)/shard_map/ppermute | solution.py:23
  139.0 1.5 %shard_map.74 = (bf16[4,8,16,1792]{3,2,1,0:T(8,128)(2,1)}, bf16[4,8,16,1792]{3,2,1,0:T(8,128)(2,1)}) custom-call(s32[1]{0:T(128)} %bitcast.late_ref, bf16[3,2,4,16,1792]{4,3,2,1,0:T(8,128)(2,1)S(1)} %get-tuple-element.42.refs_0_, bf16[2,2,4,16,1792]{4,3,2,1,0:T(8,128)(2,1)S(1)} %collective-permute-done.19.refs_1_, ...), custom_call_target="tpu_custom_call", output_to_operand_aliasing={{0}: (3, {}), {1}: (4, {})} | custom-call | flops 1 | bytes 1 | tf_op jit(solution)/shard_map/pallas_call | solution.py:157
  140.5 3.4 %collective-permute-done.18.refs_3_ = bf16[2,4,16,1792]{3,2,1,0:T(8,128)(2,1)S(1)} collective-permute-done((bf16[2,4,16,1792]{3,2,1,0:T(8,128)(2,1)S(1)}, bf16[2,4,16,1792]{3,2,1,0:T(8,128)(2,1)S(1)}, u32[]{:S(2)}, u32[]{:S(2)}) %collective-permute-start.18) | collective-permute-done | bytes 458784 | tf_op jit(solution)/shard_map/ppermute | solution.py:23
  143.9 1.2 shard_map.71.refs_4_
  145.1 1.2 shard_map.72
  (19 shorter events, 0.1 us)
Async XLA Ops:
  2.9 6.3 %copy-start.3 = (bf16[4,8,16,1792]{3,2,1,0:T(8,128)(2,1)S(1)}, bf16[4,8,16,1792]{3,2,1,0:T(8,128)(2,1)}, u32[]{:S(2)}) copy-start(bf16[4,8,16,1792]{3,2,1,0:T(8,128)(2,1)} %refs_1_.7) | copy-start | bytes 5505028
  3.0 15.5 %collective-permute-start = (bf16[2,2,4,16,1792]{4,3,2,1,0:T(8,128)(2,1)S(1)}, bf16[2,2,4,16,1792]{4,3,2,1,0:T(8,128)(2,1)S(1)}, u32[]{:S(2)}, u32[]{:S(2)}) collective-permute-start(bf16[2,2,4,16,1792]{4,3,2,1,0:T(8,128)(2,1)S(1)} %pad_maximum_fusion), channel_id=1, source_target_pairs={{0,7},{1,0},{2,1},{3,2},{4,3},{5,4},{6,5},{7,6},{8,15},{9,8},{10,9... | collective-permute-start | bytes 2752520 | tf_op jit(solution)/shard_map/ppermute | solution.py:23
  7.6 1.7 %copy-start.4 = (bf16[4,8,16,1792]{3,2,1,0:T(8,128)(2,1)S(1)}, bf16[4,8,16,1792]{3,2,1,0:T(8,128)(2,1)}, u32[]{:S(2)}) copy-start(bf16[4,8,16,1792]{3,2,1,0:T(8,128)(2,1)} %refs_2_.7) | copy-start | bytes 5505028
  7.6 29.2 %collective-permute-start.5 = (bf16[2,2,4,16,1792]{4,3,2,1,0:T(8,128)(2,1)S(1)}, bf16[2,2,4,16,1792]{4,3,2,1,0:T(8,128)(2,1)S(1)}, u32[]{:S(2)}, u32[]{:S(2)}) collective-permute-start(bf16[2,2,4,16,1792]{4,3,2,1,0:T(8,128)(2,1)S(1)} %pad_maximum_fusion.1), channel_id=1, source_target_pairs={{0,8},{1,9},{2,10},{3,11},{4,12},{5,13},{6,14},{7,15},{8,0},{9,1},... | collective-permute-start | bytes 2752520 | tf_op jit(solution)/shard_map/ppermute | solution.py:23
  9.3 39.4 %copy-start = (bf16[4,8,16,1792]{3,2,1,0:T(8,128)(2,1)S(1)}, bf16[4,8,16,1792]{3,2,1,0:T(8,128)(2,1)}, u32[]{:S(2)}) copy-start(bf16[4,8,16,1792]{3,2,1,0:T(8,128)(2,1)} %refs_0_.7) | copy-start | bytes 5505028
  9.3 39.4 %copy-start.1 = (bf16[4,8,16,1792]{3,2,1,0:T(8,128)(2,1)S(1)}, bf16[4,8,16,1792]{3,2,1,0:T(8,128)(2,1)}, u32[]{:S(2)}) copy-start(bf16[4,8,16,1792]{3,2,1,0:T(8,128)(2,1)} %refs_3_.7) | copy-start | bytes 5505028
  18.5 9.7 %collective-permute-start.1 = (bf16[1,2,4,16,1792]{4,3,2,1,0:T(8,128)(2,1)S(1)}, bf16[1,2,4,16,1792]{4,3,2,1,0:T(8,128)(2,1)S(1)}, u32[]{:S(2)}, u32[]{:S(2)}) collective-permute-start(bf16[1,2,4,16,1792]{4,3,2,1,0:T(8,128)(2,1)S(1)} %get-tuple-element.29), channel_id=1, source_target_pairs={{0,7},{1,0},{2,1},{3,2},{4,3},{5,4},{6,5},{7,6},{8,15},{9,8},{10,9... | collective-permute-start | bytes 1376264 | tf_op jit(solution)/shard_map/ppermute | solution.py:23
  22.2 10.9 %collective-permute-start.2 = (bf16[1,2,4,16,1792]{4,3,2,1,0:T(8,128)(2,1)S(1)}, bf16[1,2,4,16,1792]{4,3,2,1,0:T(8,128)(2,1)S(1)}, u32[]{:S(2)}, u32[]{:S(2)}) collective-permute-start(bf16[1,2,4,16,1792]{4,3,2,1,0:T(8,128)(2,1)S(1)} %get-tuple-element.30), channel_id=1, source_target_pairs={{0,7},{1,0},{2,1},{3,2},{4,3},{5,4},{6,5},{7,6},{8,15},{9,8},{10,9... | collective-permute-start | bytes 1376264 | tf_op jit(solution)/shard_map/ppermute | solution.py:23
  22.2 26.5 %collective-permute-start.6 = (bf16[2,2,4,16,1792]{4,3,2,1,0:T(8,128)(2,1)S(1)}, bf16[2,2,4,16,1792]{4,3,2,1,0:T(8,128)(2,1)S(1)}, u32[]{:S(2)}, u32[]{:S(2)}) collective-permute-start(bf16[2,2,4,16,1792]{4,3,2,1,0:T(8,128)(2,1)S(1)} %collective-permute-done.refs_4_), channel_id=1, source_target_pairs={{0,8},{1,9},{2,10},{3,11},{4,12},{5,13},{6,14},{7,15},{8,0},{9,1},... | collective-permute-start | bytes 2752520 | tf_op jit(solution)/shard_map/ppermute | solution.py:23
  33.1 21.7 %collective-permute-start.3 = (bf16[1,2,4,16,1792]{4,3,2,1,0:T(8,128)(2,1)S(1)}, bf16[1,2,4,16,1792]{4,3,2,1,0:T(8,128)(2,1)S(1)}, u32[]{:S(2)}, u32[]{:S(2)}) collective-permute-start(bf16[1,2,4,16,1792]{4,3,2,1,0:T(8,128)(2,1)S(1)} %get-tuple-element.31), channel_id=1, source_target_pairs={{0,7},{1,0},{2,1},{3,2},{4,3},{5,4},{6,5},{7,6},{8,15},{9,8},{10,9... | collective-permute-start | bytes 1376264 | tf_op jit(solution)/shard_map/ppermute | solution.py:23
  36.9 32.1 %collective-permute-start.10 = (bf16[2,2,4,16,1792]{4,3,2,1,0:T(8,128)(2,1)S(1)}, bf16[2,2,4,16,1792]{4,3,2,1,0:T(8,128)(2,1)S(1)}, u32[]{:S(2)}, u32[]{:S(2)}) collective-permute-start(bf16[2,2,4,16,1792]{4,3,2,1,0:T(8,128)(2,1)S(1)} %pad_maximum_fusion.2), channel_id=1, source_target_pairs={{0,24},{1,25},{2,26},{3,27},{4,28},{5,29},{6,30},{7,31},{8,16},{9,... | collective-permute-start | bytes 2752520 | tf_op jit(solution)/shard_map/ppermute | solution.py:23
  39.4 15.4 %collective-permute-start.4 = (bf16[1,2,4,16,1792]{4,3,2,1,0:T(8,128)(2,1)S(1)}, bf16[1,2,4,16,1792]{4,3,2,1,0:T(8,128)(2,1)S(1)}, u32[]{:S(2)}, u32[]{:S(2)}) collective-permute-start(bf16[1,2,4,16,1792]{4,3,2,1,0:T(8,128)(2,1)S(1)} %get-tuple-element.32), channel_id=1, source_target_pairs={{0,7},{1,0},{2,1},{3,2},{4,3},{5,4},{6,5},{7,6},{8,15},{9,8},{10,9... | collective-permute-start | bytes 1376264 | tf_op jit(solution)/shard_map/ppermute | solution.py:23
  52.7 16.3 %collective-permute-start.7 = (f32[14,8,256]{2,1,0:T(8,128)S(1)}, f32[14,8,256]{2,1,0:T(8,128)S(1)}, u32[]{:S(2)}, u32[]{:S(2)}) collective-permute-start(f32[14,8,256]{2,1,0:T(8,128)S(1)} %shard_map.67.refs_9_), channel_id=1, source_target_pairs={{0,8},{1,9},{2,10},{3,11},{4,12},{5,13},{6,14},{7,15},{8,0},{9,1},... | collective-permute-start | bytes 344072 | tf_op jit(solution)/shard_map/ppermute | solution.py:23
  69.0 21.4 %collective-permute-start.11 = (bf16[2,2,4,16,1792]{4,3,2,1,0:T(8,128)(2,1)S(1)}, bf16[2,2,4,16,1792]{4,3,2,1,0:T(8,128)(2,1)S(1)}, u32[]{:S(2)}, u32[]{:S(2)}) collective-permute-start(bf16[2,2,4,16,1792]{4,3,2,1,0:T(8,128)(2,1)S(1)} %constant_dynamic-update-slice_fusion.refs_4_), channel_id=1, source_target_pairs={{0,24},{1,25},{2,26},{3,27},{4,28},{5,29},{6,30},{7,31},{8,16},{9,... | collective-permute-start | bytes 2752520 | tf_op jit(solution)/shard_map/ppermute | solution.py:23
  71.7 13.2 %collective-permute-start.8 = (bf16[1,2,4,16,1792]{4,3,2,1,0:T(8,128)(2,1)S(1)}, bf16[1,2,4,16,1792]{4,3,2,1,0:T(8,128)(2,1)S(1)}, u32[]{:S(2)}, u32[]{:S(2)}) collective-permute-start(bf16[1,2,4,16,1792]{4,3,2,1,0:T(8,128)(2,1)S(1)} %get-tuple-element.33), channel_id=1, source_target_pairs={{0,7},{1,0},{2,1},{3,2},{4,3},{5,4},{6,5},{7,6},{8,15},{9,8},{10,9... | collective-permute-start | bytes 1376264 | tf_op jit(solution)/shard_map/ppermute | solution.py:23
  74.3 16.1 %copy-start.2 = (bf16[4,8,16,1792]{3,2,1,0:T(8,128)(2,1)S(1)}, bf16[4,8,16,1792]{3,2,1,0:T(8,128)(2,1)}, u32[]{:S(2)}) copy-start(bf16[4,8,16,1792]{3,2,1,0:T(8,128)(2,1)} %refs_3_.7) | copy-start | bytes 5505028
  74.3 10.9 %collective-permute-start.9 = (bf16[1,2,4,16,1792]{4,3,2,1,0:T(8,128)(2,1)S(1)}, bf16[1,2,4,16,1792]{4,3,2,1,0:T(8,128)(2,1)S(1)}, u32[]{:S(2)}, u32[]{:S(2)}) collective-permute-start(bf16[1,2,4,16,1792]{4,3,2,1,0:T(8,128)(2,1)S(1)} %get-tuple-element.34), channel_id=1, source_target_pairs={{0,7},{1,0},{2,1},{3,2},{4,3},{5,4},{6,5},{7,6},{8,15},{9,8},{10,9... | collective-permute-start | bytes 1376264 | tf_op jit(solution)/shard_map/ppermute | solution.py:23
  85.2 19.7 %collective-permute-start.13 = (bf16[3,2,4,16,1792]{4,3,2,1,0:T(8,128)(2,1)S(1)}, bf16[3,2,4,16,1792]{4,3,2,1,0:T(8,128)(2,1)S(1)}, u32[]{:S(2)}, u32[]{:S(2)}) collective-permute-start(bf16[3,2,4,16,1792]{4,3,2,1,0:T(8,128)(2,1)S(1)} %get-tuple-element.40), channel_id=1, source_target_pairs={{0,1},{1,2},{2,3},{3,4},{4,5},{5,6},{6,7},{7,0},{8,9},{9,10},{10,1... | collective-permute-start | bytes 4128776 | tf_op jit(solution)/shard_map/ppermute | solution.py:23
  94.4 6.0 %collective-permute-start.12 = (f32[14,8,256]{2,1,0:T(8,128)S(1)}, f32[14,8,256]{2,1,0:T(8,128)S(1)}, u32[]{:S(2)}, u32[]{:S(2)}) collective-permute-start(f32[14,8,256]{2,1,0:T(8,128)S(1)} %shard_map.69.refs_9_), channel_id=1, source_target_pairs={{0,24},{1,25},{2,26},{3,27},{4,28},{5,29},{6,30},{7,31},{8,16},{9,... | collective-permute-start | bytes 344072 | tf_op jit(solution)/shard_map/ppermute | solution.py:23
  100.4 19.4 %collective-permute-start.15 = (bf16[2,2,4,16,1792]{4,3,2,1,0:T(8,128)(2,1)S(1)}, bf16[2,2,4,16,1792]{4,3,2,1,0:T(8,128)(2,1)S(1)}, u32[]{:S(2)}, u32[]{:S(2)}) collective-permute-start(bf16[2,2,4,16,1792]{4,3,2,1,0:T(8,128)(2,1)S(1)} %get-tuple-element.45), channel_id=1, source_target_pairs={{0,8},{1,9},{2,10},{3,11},{4,12},{5,13},{6,14},{7,15},{8,0},{9,1},... | collective-permute-start | bytes 2752520 | tf_op jit(solution)/shard_map/ppermute | solution.py:23
  114.4 9.8 %collective-permute-start.14 = (bf16[2,4,16,1792]{3,2,1,0:T(8,128)(2,1)S(1)}, bf16[2,4,16,1792]{3,2,1,0:T(8,128)(2,1)S(1)}, u32[]{:S(2)}, u32[]{:S(2)}) collective-permute-start(bf16[2,4,16,1792]{3,2,1,0:T(8,128)(2,1)S(1)} %get-tuple-element.43), channel_id=1, source_target_pairs={{0,1},{1,2},{2,3},{3,4},{4,5},{5,6},{6,7},{7,0},{8,9},{9,10},{10,1... | collective-permute-start | bytes 1376264 | tf_op jit(solution)/shard_map/ppermute | solution.py:23
  114.5 30.6 %collective-permute-start.17 = (bf16[2,4,16,1792]{3,2,1,0:T(8,128)(2,1)S(1)}, bf16[2,4,16,1792]{3,2,1,0:T(8,128)(2,1)S(1)}, u32[]{:S(2)}, u32[]{:S(2)}) collective-permute-start(bf16[2,4,16,1792]{3,2,1,0:T(8,128)(2,1)S(1)} %get-tuple-element.47), channel_id=1, source_target_pairs={{0,25},{1,26},{2,27},{3,28},{4,29},{5,30},{6,31},{7,24},{8,17},{9,... | collective-permute-start | bytes 1376264 | tf_op jit(solution)/shard_map/ppermute | solution.py:23
  115.7 23.3 %collective-permute-start.19 = (bf16[2,2,4,16,1792]{4,3,2,1,0:T(8,128)(2,1)S(1)}, bf16[2,2,4,16,1792]{4,3,2,1,0:T(8,128)(2,1)S(1)}, u32[]{:S(2)}, u32[]{:S(2)}) collective-permute-start(bf16[2,2,4,16,1792]{4,3,2,1,0:T(8,128)(2,1)S(1)} %get-tuple-element.50), channel_id=1, source_target_pairs={{0,1},{1,2},{2,3},{3,4},{4,5},{5,6},{6,7},{7,0},{8,9},{9,10},{10,1... | collective-permute-start | bytes 2752520 | tf_op jit(solution)/shard_map/ppermute | solution.py:23
  124.2 19.7 %collective-permute-start.18 = (bf16[2,4,16,1792]{3,2,1,0:T(8,128)(2,1)S(1)}, bf16[2,4,16,1792]{3,2,1,0:T(8,128)(2,1)S(1)}, u32[]{:S(2)}, u32[]{:S(2)}) collective-permute-start(bf16[2,4,16,1792]{3,2,1,0:T(8,128)(2,1)S(1)} %slice_bitcast_fusion), channel_id=1, source_target_pairs={{0,1},{1,2},{2,3},{3,4},{4,5},{5,6},{6,7},{7,0},{8,9},{9,10},{10,1... | collective-permute-start | bytes 1376264 | tf_op jit(solution)/shard_map/ppermute | solution.py:23
  124.2 20.9 %collective-permute-start.16 = (bf16[2,4,16,1792]{3,2,1,0:T(8,128)(2,1)S(1)}, bf16[2,4,16,1792]{3,2,1,0:T(8,128)(2,1)S(1)}, u32[]{:S(2)}, u32[]{:S(2)}) collective-permute-start(bf16[2,4,16,1792]{3,2,1,0:T(8,128)(2,1)S(1)} %get-tuple-element.46), channel_id=1, source_target_pairs={{0,24},{1,25},{2,26},{3,27},{4,28},{5,29},{6,30},{7,31},{8,16},{9,... | collective-permute-start | bytes 1376264 | tf_op jit(solution)/shard_map/ppermute | solution.py:23

commit v3 on v2

--- a/solution.py
+++ b/solution.py
@@ -23,27 +23,30 @@
     return lax.ppermute(value, AXES, pairs)
 
 
-def late_half(shape):
-    return lax.broadcasted_iota(jnp.int32, shape, 1) >= WW // 2
+def middle(shape):
+    column = lax.broadcasted_iota(jnp.int32, shape, 1)
+    return (column >= WW // 2) & (column < WW + WW // 2)
+
+
+def turned(tokens):
+    return jnp.concatenate((tokens[:, WW:], tokens[:, :WW]), axis=1)
 
 
 def split_windows(parts):
-    tokens = jnp.concatenate(parts, axis=0).astype(jnp.float32)
-    first, second = tokens[:, :WW], tokens[:, WW:]
-    late = late_half(first.shape)
-    flat = (first.shape[0] * WW, first.shape[2])
-    inner = jnp.where(late, first, second).reshape(flat).astype(jnp.bfloat16)
-    outer = jnp.where(late, second, first).reshape(flat).astype(jnp.bfloat16)
+    first, second = parts[0], turned(parts[1])
+    inside = middle(first.shape)
+    flat = (first.shape[0] * first.shape[1], first.shape[2])
+    inner = jnp.where(inside, first, second).reshape(flat)
+    outer = jnp.where(inside, second, first).reshape(flat)
     return inner, outer
 
 
-def join_windows(inner, outer):
-    shape = (inner.shape[0] // WW, WW, inner.shape[1])
-    inner, outer = inner.reshape(shape), outer.reshape(shape)
-    late = late_half(shape)
-    first = jnp.where(late, inner, outer)
-    second = jnp.where(late, outer, inner)
-    return jnp.concatenate((first, second), axis=1).astype(jnp.bfloat16)
+def join_windows(inner, outer, slots):
+    shape = (slots, 2 * WW, inner.shape[1])
+    inner = inner.astype(jnp.bfloat16).reshape(shape)
+    outer = outer.astype(jnp.bfloat16).reshape(shape)
+    inside = middle(shape)
+    return jnp.where(inside, inner, outer), turned(jnp.where(inside, outer, inner))
 
 
 def dot(a, b, dims):
@@ -68,19 +71,27 @@
     return top, key_sum(powers), key_sum(powers * weight_grad)
 
 
-def partial_grads(query, key, value, grad, mine, other):
+def partial_grads(windows, mine, other):
     factor = 1.0 / math.sqrt(HEAD_DIM)
-    top = jnp.maximum(mine[0], other[0])
-    scale_mine, scale_other = jnp.exp(mine[0] - top), jnp.exp(other[0] - top)
-    inverse = 1.0 / (mine[1] * scale_mine + other[1] * scale_other)
-    row_dot = (mine[2] * scale_mine + other[2] * scale_other) * inverse
-    scores, weight_grad = products(query, key, value, grad)
-    weights = jnp.exp(scores - top) * inverse
-    score_grad = (weights * (weight_grad - row_dot) * factor).astype(jnp.bfloat16)
-    value_out = dot(weights.astype(jnp.bfloat16), grad, ((1,), (0,)))
-    key_out = dot(score_grad, query, ((1,), (0,)))
-    query_out = dot(score_grad, key, ((0,), (0,)))
-    return query_out, key_out, value_out
+    each = range(len(windows))
+    made = [products(*w) for w in windows]
+    tops, inverses, row_dots = [], [], []
+    for a, b in zip(mine, other):
+        top = jnp.maximum(a[0], b[0])
+        scale_a, scale_b = jnp.exp(a[0] - top), jnp.exp(b[0] - top)
+        inverse = 1.0 / (a[1] * scale_a + b[1] * scale_b)
+        tops.append(top)
+        inverses.append(inverse)
+        row_dots.append((a[2] * scale_a + b[2] * scale_b) * inverse)
+    weights = [jnp.exp(made[i][0] - tops[i]) * inverses[i] for i in each]
+    weights_b = [w.astype(jnp.bfloat16) for w in weights]
+    score_grads = [
+        (weights[i] * ((made[i][1] - row_dots[i]) * factor)).astype(jnp.bfloat16) for i in each
+    ]
+    value_out = [dot(weights_b[i], windows[i][3], ((1,), (0,))) for i in each]
+    key_out = [dot(score_grads[i], windows[i][0], ((1,), (0,))) for i in each]
+    query_out = [dot(score_grads[i], windows[i][1], ((0,), (0,))) for i in each]
+    return list(zip(query_out, key_out, value_out))
 
 
 def window_tokens(refs, head):
@@ -113,29 +124,25 @@
 
 def grads_kernel(late_ref, *refs):
     mine_ref, other_ref, kept_out = refs[9:12]
-    if len(refs) == 14:
-        row_outs = [refs[12].at[index] for index in range(3)]
-        near_out, corner_out = refs[13].at[0], refs[13].at[1]
-    else:
-        row_outs = [refs[12], refs[13].at[0], refs[13].at[1]]
-        near_out, corner_out = refs[14:]
+    near_out, corner_out = refs[-2:]
+    row_outs = [refs[12], refs[13].at[0], refs[13].at[1]]
     _, frames, rows, columns, width = kept_out.shape
-    shape = (2, frames, rows, columns, HEAD_DIM)
+    shape = (frames, rows, columns, HEAD_DIM)
     for head in range(width // HEAD_DIM):
         lanes = pl.ds(head * HEAD_DIM, HEAD_DIM)
-        grads = []
-        for w, window in enumerate(window_tokens(refs[:9], head)):
-            mine = [mine_ref[head, pl.ds(3 * w + i, 1)] for i in range(3)]
-            other = [other_ref[head, pl.ds(3 * w + i, 1)] for i in range(3)]
-            half = window[1].shape[0]
-            other = [jnp.concatenate((o[:, half:], o[:, :half]), axis=1) for o in other]
-            grads.append(partial_grads(*window, mine, other))
+        windows = window_tokens(refs[:9], head)
+        half = windows[0][1].shape[0]
+        stat = lambda ref, w: [ref[head, pl.ds(3 * w + i, 1)] for i in range(3)]
+        swapped = lambda o: jnp.concatenate((o[:, half:], o[:, :half]), axis=1)
+        mine = [stat(mine_ref, w) for w in (0, 1)]
+        other = [[swapped(o) for o in stat(other_ref, w)] for w in (0, 1)]
+        grads = partial_grads(windows, mine, other)
         kept = [[g[0][:half] for g in grads], [g[1] for g in grads], [g[2] for g in grads]]
         for index, windows in enumerate(kept):
-            tokens = join_windows(*windows).reshape(shape)
+            tokens = [p.reshape(shape) for p in join_windows(*windows, frames * rows)]
             kept_out[index, :, :, :, lanes] = tokens[0]
             row_outs[index][:, :, :, lanes] = tokens[1]
-        tokens = join_windows(*[g[0][half:] for g in grads]).reshape(shape)
+        tokens = [p.reshape(shape) for p in join_windows(*[g[0][half:] for g in grads], frames * rows)]
         near_out[:, :, :, lanes] = tokens[0]
         corner_out[:, :, :, lanes] = tokens[1]
 
@@ -146,7 +153,7 @@
 
 
 def heads_per_step(heads):
-    return 2 if heads % 2 == 0 else 1
+    return next(n for n in range(14, 0, -1) if heads % n == 0)
 
 
 def small():
@@ -191,14 +198,14 @@
     )
 
 
-def family_grads(late, inputs, received, mine, other, joined):
+def family_grads(late, inputs, received, mine, other):
     frames, rows, columns, features = inputs[0].shape
     heads, length = features // HEAD_DIM, frames * rows * WW
     step = heads_per_step(heads)
     sent = jax.ShapeDtypeStruct((frames // 2, rows // 2, columns, features), jnp.bfloat16)
     kept = jax.ShapeDtypeStruct((3,) + sent.shape, jnp.bfloat16)
     two = jax.ShapeDtypeStruct((2,) + sent.shape, jnp.bfloat16)
-    shapes = [kept, kept, two] if joined else [kept, sent, two, sent, sent]
+    shapes = [kept, sent, two, sent, sent]
     return called(
         grads_kernel,
         late,
@@ -232,7 +239,7 @@
 
 def placed(kernel, number, late, outs, pieces, counts, whole):
     frames, rows, columns, features = whole.shape
-    lanes = features // heads_per_step(features // HEAD_DIM)
+    lanes = features // 2
     outs = () if outs is None else outs
     shape = lambda p, n: ((n,) + p.shape[1:]) if p.ndim == 5 else p.shape
     full = lane_block((frames // 2, rows, columns, 0), lanes, lambda late: (late[0], 0, 0))
@@ -286,22 +293,22 @@
     row_qg1 = jnp.concatenate([row_of((x,), 1, *row_kv0) for x in qg])
     row_kv1 = rows_of_both(1, other0)
     corner1 = moved(after(row_qg1, other0, near1), 1, 0)
-    kept0, row0, far0 = family_grads(spot[0], inputs, got0, stats0, other0, True)
-    got1 = (row_qg1, *row_kv1, near1, after(corner1, far0))
+    kept0, row0, pair0, near_b0, corner_b0 = family_grads(spot[0], inputs, got0, stats0, other0)
+    got1 = (row_qg1, *row_kv1, near1, after(corner1, corner_b0))
     stats1 = family_stats(spot[1], inputs, got1)
     other1 = moved(stats1, 1, 0)
-    row0 = moved(after(row0, *row_kv1), None, 1)
-    far0 = moved(after(far0, other1), 0, 0)
+    row0, pair0 = [moved(after(r, *row_kv1), None, 1) for r in (row0, pair0)]
+    near_b0 = moved(near_b0, 0, 0)
+    corner_b0 = moved(after(corner_b0, other1), 0, 1)
     kept1, row1, pair1, near_b1, corner_b1 = family_grads(
-        spot[1], inputs, got1, stats1, after(other1, row0), False
-    )
-    near_b1 = moved(after(near_b1, far0), 1, 0)
-    corner_b1 = moved(corner_b1, 1, 1)
+        spot[1], inputs, got1, stats1, after(other1, row0, pair0, near_b0)
+    )
+    near_b1 = moved(near_b1, 1, 0)
+    corner_b1 = moved(after(corner_b1, near_b0, corner_b0), 1, 1)
     row1, pair1 = moved(row1, None, 1), moved(pair1, None, 1)
-    corner_b0 = moved(after(far0[1], row1), None, 1)
-    pair = placed(place_pair_kernel, 2, spot[0], None, (kept0, row0), (3, 3), queries)
+    pair = placed(place_pair_kernel, 2, spot[0], None, (kept0, pair0), (3, 2), queries)
     total = placed(
-        place_sum_kernel, 1, spot[0], None, (kept0, row0, far0, corner_b0), (1, 1, 1, 1), queries
+        place_sum_kernel, 1, spot[0], None, (kept0, row0, near_b0, corner_b0), (1, 1, 1, 1), queries
     )
     pair = placed(place_pair_kernel, 2, spot[1], pair, (kept1, pair1), (3, 2), queries)
     total = placed(

time: 147 us -> 144 us (0.980)
  Pallas kernels: 32.5 us -> 20.8 us
  starting transfers between devices: 31.7 us -> 35.9 us
  waiting for transfers between devices: 78.6 us -> 82.5 us
    pallas_call x8, Pallas kernels: 32.5 us -> 20.8 us  [called(): pl.pallas_call(kernel, grid_spec=pltpu.PrefetchScalarGridSpec(num_scalar_...]
    ppermute x20 -> x21, starting transfers between devices: 31.7 us -> 35.9 us  [moved(): return lax.ppermute(value, AXES, pairs)]
    ppermute x20 -> x21, waiting for transfers between devices: 78.6 us -> 82.5 us  [moved(): return lax.ppermute(value, AXES, pairs)]
  transfers between devices with their start and end apart: 20 -> 21, of which waited for: 13 -> 11; matrix products, arithmetic and copies ran while one was open for 0% -> 0% of each run, Pallas kernels for 21% -> 13%
where the time goes in v3:
time: 144 us; the launch traced here: 143 us
  waiting for transfers between devices  82.5 us (57%)
  starting transfers between devices  35.9 us (25%)
  Pallas kernels  20.8 us (14%)
  local copies, waits for them, and re-layouts  2.47 us (2%)
    ppermute x21, waiting for transfers between devices, moved(): return lax.ppermute(value, AXES, pairs)  82.5 us
    ppermute x21, starting transfers between devices, moved(): return lax.ppermute(value, AXES, pairs)  35.9 us
    pallas_call x8, Pallas kernels, called(): pl.pallas_call(kernel, grid_spec=pltpu.PrefetchScalarGridSpec(num_scalar_...  20.8 us
  transfers between devices with their start and end apart: 21, of which 11 were waited for; matrix products, arithmetic and copies ran while one was open for 0% of the time, Pallas kernels for 13%

profile of v3, /device:TPU:0, one launch (start us, length us, event | category | flops | bytes accessed | tf_op | source)
XLA Modules:
  0.0 142.7 jit_solution(12051022780067803338)
XLA Ops:
  0.7 2.2 %dynamic-slice_bitcast_fusion = (bf16[1,2,4,16,1792]{4,3,2,1,0:T(8,128)(2,1)S(1)}, bf16[1,2,4,16,1792]{4,3,2,1,0:T(8,128)(2,1)S(1)}, bf16[1,2,4,16,1792]{4,3,2,1...) fusion(bf16[4,8,16,1792]{3,2,1,0:T(8,128)(2,1)} %refs_3_.7, ...), kind=kLoop, calls=%fused_computation.3 | loop fusion | bytes 7340040 | tf_op jit(solution)/shard_map/stack | solution.py:272
  2.9 0.0 copy-start.3
  2.9 0.1 pad_maximum_fusion
  3.0 4.5 %collective-permute-start = (bf16[2,2,4,16,1792]{4,3,2,1,0:T(8,128)(2,1)S(1)}, bf16[2,2,4,16,1792]{4,3,2,1,0:T(8,128)(2,1)S(1)}, u32[]{:S(2)}, u32[]{:S(2)}) collective-permute-start(bf16[2,2,4,16,1792]{4,3,2,1,0:T(8,128)(2,1)S(1)} %pad_maximum_fusion), channel_id=1, source_target_pairs={{0,7},{1,0},{2,1},{3,2},{4,3},{5,4},{6,5},{7,6},{8,15},{9,8},{10,9... | collective-permute-start | bytes 2752520 | tf_op jit(solution)/shard_map/ppermute | solution.py:23
  7.6 0.1 pad_maximum_fusion.1
  7.6 1.6 %collective-permute-start.5 = (bf16[2,2,4,16,1792]{4,3,2,1,0:T(8,128)(2,1)S(1)}, bf16[2,2,4,16,1792]{4,3,2,1,0:T(8,128)(2,1)S(1)}, u32[]{:S(2)}, u32[]{:S(2)}) collective-permute-start(bf16[2,2,4,16,1792]{4,3,2,1,0:T(8,128)(2,1)S(1)} %pad_maximum_fusion.1), channel_id=1, source_target_pairs={{0,8},{1,9},{2,10},{3,11},{4,12},{5,13},{6,14},{7,15},{8,0},{9,1},... | collective-permute-start | bytes 2752520 | tf_op jit(solution)/shard_map/ppermute | solution.py:23
  9.2 0.1 dynamic-slice_bitcast_fusion.5
  9.3 0.0 copy-start
  9.3 0.0 copy-start.1
  9.3 0.1 dynamic-slice_bitcast_fusion.2
  9.4 9.1 %collective-permute-done.refs_4_ = bf16[2,2,4,16,1792]{4,3,2,1,0:T(8,128)(2,1)S(1)} collective-permute-done((bf16[2,2,4,16,1792]{4,3,2,1,0:T(8,128)(2,1)S(1)}, bf16[2,2,4,16,1792]{4,3,2,1,0:T(8,128)(2,1)S(1)}, u32[]{:S(2)}, u32[]{:S(2)}) %collective-permute-start) | collective-permute-done | bytes 917536 | tf_op jit(solution)/shard_map/ppermute | solution.py:23
  18.5 3.7 %collective-permute-start.1 = (bf16[1,2,4,16,1792]{4,3,2,1,0:T(8,128)(2,1)S(1)}, bf16[1,2,4,16,1792]{4,3,2,1,0:T(8,128)(2,1)S(1)}, u32[]{:S(2)}, u32[]{:S(2)}) collective-permute-start(bf16[1,2,4,16,1792]{4,3,2,1,0:T(8,128)(2,1)S(1)} %get-tuple-element.31), channel_id=1, source_target_pairs={{0,7},{1,0},{2,1},{3,2},{4,3},{5,4},{6,5},{7,6},{8,15},{9,8},{10,9... | collective-permute-start | bytes 1376264 | tf_op jit(solution)/shard_map/ppermute | solution.py:23
  22.2 0.0 collective-permute-start.2
  22.2 1.5 %collective-permute-start.6 = (bf16[2,2,4,16,1792]{4,3,2,1,0:T(8,128)(2,1)S(1)}, bf16[2,2,4,16,1792]{4,3,2,1,0:T(8,128)(2,1)S(1)}, u32[]{:S(2)}, u32[]{:S(2)}) collective-permute-start(bf16[2,2,4,16,1792]{4,3,2,1,0:T(8,128)(2,1)S(1)} %collective-permute-done.refs_4_), channel_id=1, source_target_pairs={{0,8},{1,9},{2,10},{3,11},{4,12},{5,13},{6,14},{7,15},{8,0},{9,1},... | collective-permute-start | bytes 2752520 | tf_op jit(solution)/shard_map/ppermute | solution.py:23
  23.7 4.5 %collective-permute-done.1.refs_5_ = bf16[1,2,4,16,1792]{4,3,2,1,0:T(8,128)(2,1)S(1)} collective-permute-done((bf16[1,2,4,16,1792]{4,3,2,1,0:T(8,128)(2,1)S(1)}, bf16[1,2,4,16,1792]{4,3,2,1,0:T(8,128)(2,1)S(1)}, u32[]{:S(2)}, u32[]{:S(2)}) %collective-permute-start.1) | collective-permute-done | bytes 458784 | tf_op jit(solution)/shard_map/ppermute | solution.py:23
  28.2 4.9 %collective-permute-done.2.refs_6_ = bf16[1,2,4,16,1792]{4,3,2,1,0:T(8,128)(2,1)S(1)} collective-permute-done((bf16[1,2,4,16,1792]{4,3,2,1,0:T(8,128)(2,1)S(1)}, bf16[1,2,4,16,1792]{4,3,2,1,0:T(8,128)(2,1)S(1)}, u32[]{:S(2)}, u32[]{:S(2)}) %collective-permute-start.2) | collective-permute-done | bytes 458784 | tf_op jit(solution)/shard_map/ppermute | solution.py:23
  33.1 3.7 %collective-permute-start.3 = (bf16[1,2,4,16,1792]{4,3,2,1,0:T(8,128)(2,1)S(1)}, bf16[1,2,4,16,1792]{4,3,2,1,0:T(8,128)(2,1)S(1)}, u32[]{:S(2)}, u32[]{:S(2)}) collective-permute-start(bf16[1,2,4,16,1792]{4,3,2,1,0:T(8,128)(2,1)S(1)} %get-tuple-element.33), channel_id=1, source_target_pairs={{0,7},{1,0},{2,1},{3,2},{4,3},{5,4},{6,5},{7,6},{8,15},{9,8},{10,9... | collective-permute-start | bytes 1376264 | tf_op jit(solution)/shard_map/ppermute | solution.py:23
  36.8 0.1 pad_maximum_fusion.2
  36.9 2.5 %collective-permute-start.10 = (bf16[2,2,4,16,1792]{4,3,2,1,0:T(8,128)(2,1)S(1)}, bf16[2,2,4,16,1792]{4,3,2,1,0:T(8,128)(2,1)S(1)}, u32[]{:S(2)}, u32[]{:S(2)}) collective-permute-start(bf16[2,2,4,16,1792]{4,3,2,1,0:T(8,128)(2,1)S(1)} %pad_maximum_fusion.2), channel_id=1, source_target_pairs={{0,24},{1,25},{2,26},{3,27},{4,28},{5,29},{6,30},{7,31},{8,16},{9,... | collective-permute-start | bytes 2752520 | tf_op jit(solution)/shard_map/ppermute | solution.py:23
  39.4 9.3 %collective-permute-done.6.refs_8_ = bf16[2,2,4,16,1792]{4,3,2,1,0:T(8,128)(2,1)S(1)} collective-permute-done((bf16[2,2,4,16,1792]{4,3,2,1,0:T(8,128)(2,1)S(1)}, bf16[2,2,4,16,1792]{4,3,2,1,0:T(8,128)(2,1)S(1)}, u32[]{:S(2)}, u32[]{:S(2)}) %collective-permute-start.6) | collective-permute-done | bytes 917536 | tf_op jit(solution)/shard_map/ppermute | solution.py:23
  48.7 2.4 %shard_map.67.refs_9_ = f32[14,8,256]{2,1,0:T(8,128)S(1)} custom-call(s32[1]{0:T(128)} %bitcast.8.late_ref, bf16[4,8,16,1792]{3,2,1,0:T(8,128)(2,1)S(1)} %copy-done, bf16[4,8,16,1792]{3,2,1,0:T(8,128)(2,1)S(1)} %copy-done.3, bf16[4,8,16,1792]{3,2,1,0:T(8,128)(2,1)S(1)} %copy-done.4, bf16[4,8,16,1792]{3,2,1,0:T(8,128)(2,1)S(1)} %copy-done.1, ...), custom_call_target="tpu_custom_call" | custom-call | flops 1 | bytes 1 | tf_op jit(solution)/shard_map/pallas_call | solution.py:164
  51.1 2.1 %collective-permute-start.7 = (f32[14,8,256]{2,1,0:T(8,128)S(1)}, f32[14,8,256]{2,1,0:T(8,128)S(1)}, u32[]{:S(2)}, u32[]{:S(2)}) collective-permute-start(f32[14,8,256]{2,1,0:T(8,128)S(1)} %shard_map.67.refs_9_), channel_id=1, source_target_pairs={{0,8},{1,9},{2,10},{3,11},{4,12},{5,13},{6,14},{7,15},{8,0},{9,1},... | collective-permute-start | bytes 344072 | tf_op jit(solution)/shard_map/ppermute | solution.py:23
  53.2 15.8 %collective-permute-done.7.refs_10_ = f32[14,8,256]{2,1,0:T(8,128)S(1)} collective-permute-done((f32[14,8,256]{2,1,0:T(8,128)S(1)}, f32[14,8,256]{2,1,0:T(8,128)S(1)}, u32[]{:S(2)}, u32[]{:S(2)}) %collective-permute-start.7) | collective-permute-done | bytes 114720 | tf_op jit(solution)/shard_map/ppermute | solution.py:23
  69.0 3.1 %collective-permute-start.8 = (bf16[1,2,4,16,1792]{4,3,2,1,0:T(8,128)(2,1)S(1)}, bf16[1,2,4,16,1792]{4,3,2,1,0:T(8,128)(2,1)S(1)}, u32[]{:S(2)}, u32[]{:S(2)}) collective-permute-start(bf16[1,2,4,16,1792]{4,3,2,1,0:T(8,128)(2,1)S(1)} %get-tuple-element.35), channel_id=1, source_target_pairs={{0,7},{1,0},{2,1},{3,2},{4,3},{5,4},{6,5},{7,6},{8,15},{9,8},{10,9... | collective-permute-start | bytes 1376264 | tf_op jit(solution)/shard_map/ppermute | solution.py:23
  72.1 0.8 collective-permute-start.9
  72.9 0.0 collective-permute-done.3
  73.0 0.0 copy-start.2
  73.0 2.5 %collective-permute-start.11 = (bf16[2,2,4,16,1792]{4,3,2,1,0:T(8,128)(2,1)S(1)}, bf16[2,2,4,16,1792]{4,3,2,1,0:T(8,128)(2,1)S(1)}, u32[]{:S(2)}, u32[]{:S(2)}) collective-permute-start(bf16[2,2,4,16,1792]{4,3,2,1,0:T(8,128)(2,1)S(1)} %constant_dynamic-update-slice_fusion.refs_4_), channel_id=1, source_target_pairs={{0,24},{1,25},{2,26},{3,27},{4,28},{5,29},{6,30},{7,31},{8,16},{9,... | collective-permute-start | bytes 2752520 | tf_op jit(solution)/shard_map/ppermute | solution.py:23
  75.6 5.2 %shard_map.68 = (bf16[3,2,4,16,1792]{4,3,2,1,0:T(8,128)(2,1)S(1)}, bf16[2,4,16,1792]{3,2,1,0:T(8,128)(2,1)S(1)}, bf16[2,2,4,16,1792]{4,3,2,1,0:T(8,128)(2,1)S(1)...) custom-call(s32[1]{0:T(128)} %bitcast.8.late_ref, bf16[4,8,16,1792]{3,2,1,0:T(8,128)(2,1)S(1)} %copy-done, ...), custom_call_target="tpu_custom_call" | custom-call | flops 1 | bytes 1 | tf_op jit(solution)/shard_map/pallas_call | solution.py:164
  80.8 2.5 %collective-permute-done.9.refs_6_ = bf16[1,2,4,16,1792]{4,3,2,1,0:T(8,128)(2,1)S(1)} collective-permute-done((bf16[1,2,4,16,1792]{4,3,2,1,0:T(8,128)(2,1)S(1)}, bf16[1,2,4,16,1792]{4,3,2,1,0:T(8,128)(2,1)S(1)}, u32[]{:S(2)}, u32[]{:S(2)}) %collective-permute-start.9) | collective-permute-done | bytes 458784 | tf_op jit(solution)/shard_map/ppermute | solution.py:23
  83.3 1.5 %collective-permute-start.15 = (bf16[2,4,16,1792]{3,2,1,0:T(8,128)(2,1)S(1)}, bf16[2,4,16,1792]{3,2,1,0:T(8,128)(2,1)S(1)}, u32[]{:S(2)}, u32[]{:S(2)}) collective-permute-start(bf16[2,4,16,1792]{3,2,1,0:T(8,128)(2,1)S(1)} %get-tuple-element.45), channel_id=1, source_target_pairs={{0,8},{1,9},{2,10},{3,11},{4,12},{5,13},{6,14},{7,15},{8,0},{9,1},... | collective-permute-start | bytes 1376264 | tf_op jit(solution)/shard_map/ppermute | solution.py:23
  84.8 12.5 %collective-permute-done.11.refs_8_ = bf16[2,2,4,16,1792]{4,3,2,1,0:T(8,128)(2,1)S(1)} collective-permute-done((bf16[2,2,4,16,1792]{4,3,2,1,0:T(8,128)(2,1)S(1)}, bf16[2,2,4,16,1792]{4,3,2,1,0:T(8,128)(2,1)S(1)}, u32[]{:S(2)}, u32[]{:S(2)}) %collective-permute-start.11) | collective-permute-done | bytes 917536 | tf_op jit(solution)/shard_map/ppermute | solution.py:23
  97.3 2.4 %shard_map.69.refs_9_ = f32[14,8,256]{2,1,0:T(8,128)S(1)} custom-call(s32[1]{0:T(128)} %bitcast.late_ref, bf16[4,8,16,1792]{3,2,1,0:T(8,128)(2,1)S(1)} %copy-done, bf16[4,8,16,1792]{3,2,1,0:T(8,128)(2,1)S(1)} %copy-done.3, bf16[4,8,16,1792]{3,2,1,0:T(8,128)(2,1)S(1)} %copy-done.4, bf16[4,8,16,1792]{3,2,1,0:T(8,128)(2,1)S(1)} %copy-done.2, ...), custom_call_target="tpu_custom_call" | custom-call | flops 1 | bytes 1 | tf_op jit(solution)/shard_map/pallas_call | solution.py:164
  99.7 2.5 %collective-permute-start.12 = (f32[14,8,256]{2,1,0:T(8,128)S(1)}, f32[14,8,256]{2,1,0:T(8,128)S(1)}, u32[]{:S(2)}, u32[]{:S(2)}) collective-permute-start(f32[14,8,256]{2,1,0:T(8,128)S(1)} %shard_map.69.refs_9_), channel_id=1, source_target_pairs={{0,24},{1,25},{2,26},{3,27},{4,28},{5,29},{6,30},{7,31},{8,16},{9,... | collective-permute-start | bytes 344072 | tf_op jit(solution)/shard_map/ppermute | solution.py:23
  102.2 6.0 %collective-permute-done.12.refs_10_ = f32[14,8,256]{2,1,0:T(8,128)S(1)} collective-permute-done((f32[14,8,256]{2,1,0:T(8,128)S(1)}, f32[14,8,256]{2,1,0:T(8,128)S(1)}, u32[]{:S(2)}, u32[]{:S(2)}) %collective-permute-start.12) | collective-permute-done | bytes 114720 | tf_op jit(solution)/shard_map/ppermute | solution.py:23
  108.2 0.0 collective-permute-start.18
  108.3 5.2 %shard_map.70 = (bf16[3,2,4,16,1792]{4,3,2,1,0:T(8,128)(2,1)S(1)}, bf16[2,4,16,1792]{3,2,1,0:T(8,128)(2,1)S(1)}, bf16[2,2,4,16,1792]{4,3,2,1,0:T(8,128)(2,1)S(1)...) custom-call(s32[1]{0:T(128)} %bitcast.late_ref, bf16[4,8,16,1792]{3,2,1,0:T(8,128)(2,1)S(1)} %copy-done, ...), custom_call_target="tpu_custom_call" | custom-call | flops 1 | bytes 1 | tf_op jit(solution)/shard_map/pallas_call | solution.py:164
  113.5 0.1 collective-permute-start.20
  113.6 0.1 collective-permute-start.16
  113.6 2.5 %collective-permute-start.17 = (bf16[2,4,16,1792]{3,2,1,0:T(8,128)(2,1)S(1)}, bf16[2,4,16,1792]{3,2,1,0:T(8,128)(2,1)S(1)}, u32[]{:S(2)}, u32[]{:S(2)}) collective-permute-start(bf16[2,4,16,1792]{3,2,1,0:T(8,128)(2,1)S(1)} %get-tuple-element.49), channel_id=1, source_target_pairs={{0,24},{1,25},{2,26},{3,27},{4,28},{5,29},{6,30},{7,31},{8,16},{9,... | collective-permute-start | bytes 1376264 | tf_op jit(solution)/shard_map/ppermute | solution.py:23
  116.2 4.2 %collective-permute-done.18.refs_3_ = bf16[2,4,16,1792]{3,2,1,0:T(8,128)(2,1)S(1)} collective-permute-done((bf16[2,4,16,1792]{3,2,1,0:T(8,128)(2,1)S(1)}, bf16[2,4,16,1792]{3,2,1,0:T(8,128)(2,1)S(1)}, u32[]{:S(2)}, u32[]{:S(2)}) %collective-permute-start.18) | collective-permute-done | bytes 458784 | tf_op jit(solution)/shard_map/ppermute | solution.py:23
  120.3 3.2 %collective-permute-start.19 = (bf16[2,4,16,1792]{3,2,1,0:T(8,128)(2,1)S(1)}, bf16[2,4,16,1792]{3,2,1,0:T(8,128)(2,1)S(1)}, u32[]{:S(2)}, u32[]{:S(2)}) collective-permute-start(bf16[2,4,16,1792]{3,2,1,0:T(8,128)(2,1)S(1)} %get-tuple-element.52), channel_id=1, source_target_pairs={{0,25},{1,26},{2,27},{3,28},{4,29},{5,30},{6,31},{7,24},{8,17},{9,... | collective-permute-start | bytes 1376264 | tf_op jit(solution)/shard_map/ppermute | solution.py:23
  123.5 1.5 %shard_map.73 = (bf16[4,8,16,1792]{3,2,1,0:T(8,128)(2,1)}, bf16[4,8,16,1792]{3,2,1,0:T(8,128)(2,1)}) custom-call(s32[1]{0:T(128)} %bitcast.8.late_ref, bf16[3,2,4,16,1792]{4,3,2,1,0:T(8,128)(2,1)S(1)} %get-tuple-element.53.refs_0_, bf16[2,2,4,16,1792]{4,3,2,1,0:T(8,128)(2,1)S(1)} %collective-permute-done.14.refs_1_), custom_call_target="tpu_custom_call" | custom-call | flops 1 | bytes 1 | tf_op jit(solution)/shard_map/pallas_call | solution.py:164
  125.0 1.2 shard_map.71.refs_4_
  126.2 7.8 %collective-permute-done.16.refs_1_ = bf16[2,4,16,1792]{3,2,1,0:T(8,128)(2,1)S(1)} collective-permute-done((bf16[2,4,16,1792]{3,2,1,0:T(8,128)(2,1)S(1)}, bf16[2,4,16,1792]{3,2,1,0:T(8,128)(2,1)S(1)}, u32[]{:S(2)}, u32[]{:S(2)}) %collective-permute-start.16) | collective-permute-done | bytes 458784 | tf_op jit(solution)/shard_map/ppermute | solution.py:23
  134.0 6.0 %collective-permute-done.19.refs_3_ = bf16[2,4,16,1792]{3,2,1,0:T(8,128)(2,1)S(1)} collective-permute-done((bf16[2,4,16,1792]{3,2,1,0:T(8,128)(2,1)S(1)}, bf16[2,4,16,1792]{3,2,1,0:T(8,128)(2,1)S(1)}, u32[]{:S(2)}, u32[]{:S(2)}) %collective-permute-start.19) | collective-permute-done | bytes 458784 | tf_op jit(solution)/shard_map/ppermute | solution.py:23
  140.0 1.2 shard_map.72
  141.2 1.5 %shard_map.74 = (bf16[4,8,16,1792]{3,2,1,0:T(8,128)(2,1)}, bf16[4,8,16,1792]{3,2,1,0:T(8,128)(2,1)}) custom-call(s32[1]{0:T(128)} %bitcast.late_ref, bf16[3,2,4,16,1792]{4,3,2,1,0:T(8,128)(2,1)S(1)} %get-tuple-element.47.refs_0_, bf16[2,2,4,16,1792]{4,3,2,1,0:T(8,128)(2,1)S(1)} %collective-permute-done.20.refs_1_, ...), custom_call_target="tpu_custom_call", output_to_operand_aliasing={{0}: (3, {}), {1}: (4, {})} | custom-call | flops 1 | bytes 1 | tf_op jit(solution)/shard_map/pallas_call | solution.py:164
  (20 shorter events, 0.1 us)
Async XLA Ops:
  2.9 6.3 %copy-start.3 = (bf16[4,8,16,1792]{3,2,1,0:T(8,128)(2,1)S(1)}, bf16[4,8,16,1792]{3,2,1,0:T(8,128)(2,1)}, u32[]{:S(2)}) copy-start(bf16[4,8,16,1792]{3,2,1,0:T(8,128)(2,1)} %refs_1_.7) | copy-start | bytes 5505028
  3.0 15.5 %collective-permute-start = (bf16[2,2,4,16,1792]{4,3,2,1,0:T(8,128)(2,1)S(1)}, bf16[2,2,4,16,1792]{4,3,2,1,0:T(8,128)(2,1)S(1)}, u32[]{:S(2)}, u32[]{:S(2)}) collective-permute-start(bf16[2,2,4,16,1792]{4,3,2,1,0:T(8,128)(2,1)S(1)} %pad_maximum_fusion), channel_id=1, source_target_pairs={{0,7},{1,0},{2,1},{3,2},{4,3},{5,4},{6,5},{7,6},{8,15},{9,8},{10,9... | collective-permute-start | bytes 2752520 | tf_op jit(solution)/shard_map/ppermute | solution.py:23
  7.6 1.7 %copy-start.4 = (bf16[4,8,16,1792]{3,2,1,0:T(8,128)(2,1)S(1)}, bf16[4,8,16,1792]{3,2,1,0:T(8,128)(2,1)}, u32[]{:S(2)}) copy-start(bf16[4,8,16,1792]{3,2,1,0:T(8,128)(2,1)} %refs_2_.7) | copy-start | bytes 5505028
  7.6 29.2 %collective-permute-start.5 = (bf16[2,2,4,16,1792]{4,3,2,1,0:T(8,128)(2,1)S(1)}, bf16[2,2,4,16,1792]{4,3,2,1,0:T(8,128)(2,1)S(1)}, u32[]{:S(2)}, u32[]{:S(2)}) collective-permute-start(bf16[2,2,4,16,1792]{4,3,2,1,0:T(8,128)(2,1)S(1)} %pad_maximum_fusion.1), channel_id=1, source_target_pairs={{0,8},{1,9},{2,10},{3,11},{4,12},{5,13},{6,14},{7,15},{8,0},{9,1},... | collective-permute-start | bytes 2752520 | tf_op jit(solution)/shard_map/ppermute | solution.py:23
  9.3 39.4 %copy-start = (bf16[4,8,16,1792]{3,2,1,0:T(8,128)(2,1)S(1)}, bf16[4,8,16,1792]{3,2,1,0:T(8,128)(2,1)}, u32[]{:S(2)}) copy-start(bf16[4,8,16,1792]{3,2,1,0:T(8,128)(2,1)} %refs_0_.7) | copy-start | bytes 5505028
  9.3 39.4 %copy-start.1 = (bf16[4,8,16,1792]{3,2,1,0:T(8,128)(2,1)S(1)}, bf16[4,8,16,1792]{3,2,1,0:T(8,128)(2,1)}, u32[]{:S(2)}) copy-start(bf16[4,8,16,1792]{3,2,1,0:T(8,128)(2,1)} %refs_3_.7) | copy-start | bytes 5505028
  18.5 9.7 %collective-permute-start.1 = (bf16[1,2,4,16,1792]{4,3,2,1,0:T(8,128)(2,1)S(1)}, bf16[1,2,4,16,1792]{4,3,2,1,0:T(8,128)(2,1)S(1)}, u32[]{:S(2)}, u32[]{:S(2)}) collective-permute-start(bf16[1,2,4,16,1792]{4,3,2,1,0:T(8,128)(2,1)S(1)} %get-tuple-element.31), channel_id=1, source_target_pairs={{0,7},{1,0},{2,1},{3,2},{4,3},{5,4},{6,5},{7,6},{8,15},{9,8},{10,9... | collective-permute-start | bytes 1376264 | tf_op jit(solution)/shard_map/ppermute | solution.py:23
  22.2 10.9 %collective-permute-start.2 = (bf16[1,2,4,16,1792]{4,3,2,1,0:T(8,128)(2,1)S(1)}, bf16[1,2,4,16,1792]{4,3,2,1,0:T(8,128)(2,1)S(1)}, u32[]{:S(2)}, u32[]{:S(2)}) collective-permute-start(bf16[1,2,4,16,1792]{4,3,2,1,0:T(8,128)(2,1)S(1)} %get-tuple-element.32), channel_id=1, source_target_pairs={{0,7},{1,0},{2,1},{3,2},{4,3},{5,4},{6,5},{7,6},{8,15},{9,8},{10,9... | collective-permute-start | bytes 1376264 | tf_op jit(solution)/shard_map/ppermute | solution.py:23
  22.2 26.5 %collective-permute-start.6 = (bf16[2,2,4,16,1792]{4,3,2,1,0:T(8,128)(2,1)S(1)}, bf16[2,2,4,16,1792]{4,3,2,1,0:T(8,128)(2,1)S(1)}, u32[]{:S(2)}, u32[]{:S(2)}) collective-permute-start(bf16[2,2,4,16,1792]{4,3,2,1,0:T(8,128)(2,1)S(1)} %collective-permute-done.refs_4_), channel_id=1, source_target_pairs={{0,8},{1,9},{2,10},{3,11},{4,12},{5,13},{6,14},{7,15},{8,0},{9,1},... | collective-permute-start | bytes 2752520 | tf_op jit(solution)/shard_map/ppermute | solution.py:23
  33.1 39.9 %collective-permute-start.3 = (bf16[1,2,4,16,1792]{4,3,2,1,0:T(8,128)(2,1)S(1)}, bf16[1,2,4,16,1792]{4,3,2,1,0:T(8,128)(2,1)S(1)}, u32[]{:S(2)}, u32[]{:S(2)}) collective-permute-start(bf16[1,2,4,16,1792]{4,3,2,1,0:T(8,128)(2,1)S(1)} %get-tuple-element.33), channel_id=1, source_target_pairs={{0,7},{1,0},{2,1},{3,2},{4,3},{5,4},{6,5},{7,6},{8,15},{9,8},{10,9... | collective-permute-start | bytes 1376264 | tf_op jit(solution)/shard_map/ppermute | solution.py:23
  36.9 36.1 %collective-permute-start.10 = (bf16[2,2,4,16,1792]{4,3,2,1,0:T(8,128)(2,1)S(1)}, bf16[2,2,4,16,1792]{4,3,2,1,0:T(8,128)(2,1)S(1)}, u32[]{:S(2)}, u32[]{:S(2)}) collective-permute-start(bf16[2,2,4,16,1792]{4,3,2,1,0:T(8,128)(2,1)S(1)} %pad_maximum_fusion.2), channel_id=1, source_target_pairs={{0,24},{1,25},{2,26},{3,27},{4,28},{5,29},{6,30},{7,31},{8,16},{9,... | collective-permute-start | bytes 2752520 | tf_op jit(solution)/shard_map/ppermute | solution.py:23
  39.4 33.6 %collective-permute-start.4 = (bf16[1,2,4,16,1792]{4,3,2,1,0:T(8,128)(2,1)S(1)}, bf16[1,2,4,16,1792]{4,3,2,1,0:T(8,128)(2,1)S(1)}, u32[]{:S(2)}, u32[]{:S(2)}) collective-permute-start(bf16[1,2,4,16,1792]{4,3,2,1,0:T(8,128)(2,1)S(1)} %get-tuple-element.34), channel_id=1, source_target_pairs={{0,7},{1,0},{2,1},{3,2},{4,3},{5,4},{6,5},{7,6},{8,15},{9,8},{10,9... | collective-permute-start | bytes 1376264 | tf_op jit(solution)/shard_map/ppermute | solution.py:23
  51.1 17.8 %collective-permute-start.7 = (f32[14,8,256]{2,1,0:T(8,128)S(1)}, f32[14,8,256]{2,1,0:T(8,128)S(1)}, u32[]{:S(2)}, u32[]{:S(2)}) collective-permute-start(f32[14,8,256]{2,1,0:T(8,128)S(1)} %shard_map.67.refs_9_), channel_id=1, source_target_pairs={{0,8},{1,9},{2,10},{3,11},{4,12},{5,13},{6,14},{7,15},{8,0},{9,1},... | collective-permute-start | bytes 344072 | tf_op jit(solution)/shard_map/ppermute | solution.py:23
  69.0 11.8 %collective-permute-start.8 = (bf16[1,2,4,16,1792]{4,3,2,1,0:T(8,128)(2,1)S(1)}, bf16[1,2,4,16,1792]{4,3,2,1,0:T(8,128)(2,1)S(1)}, u32[]{:S(2)}, u32[]{:S(2)}) collective-permute-start(bf16[1,2,4,16,1792]{4,3,2,1,0:T(8,128)(2,1)S(1)} %get-tuple-element.35), channel_id=1, source_target_pairs={{0,7},{1,0},{2,1},{3,2},{4,3},{5,4},{6,5},{7,6},{8,15},{9,8},{10,9... | collective-permute-start | bytes 1376264 | tf_op jit(solution)/shard_map/ppermute | solution.py:23
  72.1 11.2 %collective-permute-start.9 = (bf16[1,2,4,16,1792]{4,3,2,1,0:T(8,128)(2,1)S(1)}, bf16[1,2,4,16,1792]{4,3,2,1,0:T(8,128)(2,1)S(1)}, u32[]{:S(2)}, u32[]{:S(2)}) collective-permute-start(bf16[1,2,4,16,1792]{4,3,2,1,0:T(8,128)(2,1)S(1)} %get-tuple-element.36), channel_id=1, source_target_pairs={{0,7},{1,0},{2,1},{3,2},{4,3},{5,4},{6,5},{7,6},{8,15},{9,8},{10,9... | collective-permute-start | bytes 1376264 | tf_op jit(solution)/shard_map/ppermute | solution.py:23
  73.0 24.2 %copy-start.2 = (bf16[4,8,16,1792]{3,2,1,0:T(8,128)(2,1)S(1)}, bf16[4,8,16,1792]{3,2,1,0:T(8,128)(2,1)}, u32[]{:S(2)}) copy-start(bf16[4,8,16,1792]{3,2,1,0:T(8,128)(2,1)} %refs_3_.7) | copy-start | bytes 5505028
  73.0 24.2 %collective-permute-start.11 = (bf16[2,2,4,16,1792]{4,3,2,1,0:T(8,128)(2,1)S(1)}, bf16[2,2,4,16,1792]{4,3,2,1,0:T(8,128)(2,1)S(1)}, u32[]{:S(2)}, u32[]{:S(2)}) collective-permute-start(bf16[2,2,4,16,1792]{4,3,2,1,0:T(8,128)(2,1)S(1)} %constant_dynamic-update-slice_fusion.refs_4_), channel_id=1, source_target_pairs={{0,24},{1,25},{2,26},{3,27},{4,28},{5,29},{6,30},{7,31},{8,16},{9,... | collective-permute-start | bytes 2752520 | tf_op jit(solution)/shard_map/ppermute | solution.py:23
  83.3 24.9 %collective-permute-start.14 = (bf16[2,2,4,16,1792]{4,3,2,1,0:T(8,128)(2,1)S(1)}, bf16[2,2,4,16,1792]{4,3,2,1,0:T(8,128)(2,1)S(1)}, u32[]{:S(2)}, u32[]{:S(2)}) collective-permute-start(bf16[2,2,4,16,1792]{4,3,2,1,0:T(8,128)(2,1)S(1)} %get-tuple-element.44), channel_id=1, source_target_pairs={{0,1},{1,2},{2,3},{3,4},{4,5},{5,6},{6,7},{7,0},{8,9},{9,10},{10,1... | collective-permute-start | bytes 2752520 | tf_op jit(solution)/shard_map/ppermute | solution.py:23
  83.3 24.9 %collective-permute-start.15 = (bf16[2,4,16,1792]{3,2,1,0:T(8,128)(2,1)S(1)}, bf16[2,4,16,1792]{3,2,1,0:T(8,128)(2,1)S(1)}, u32[]{:S(2)}, u32[]{:S(2)}) collective-permute-start(bf16[2,4,16,1792]{3,2,1,0:T(8,128)(2,1)S(1)} %get-tuple-element.45), channel_id=1, source_target_pairs={{0,8},{1,9},{2,10},{3,11},{4,12},{5,13},{6,14},{7,15},{8,0},{9,1},... | collective-permute-start | bytes 1376264 | tf_op jit(solution)/shard_map/ppermute | solution.py:23
  84.8 23.4 %collective-permute-start.13 = (bf16[2,4,16,1792]{3,2,1,0:T(8,128)(2,1)S(1)}, bf16[2,4,16,1792]{3,2,1,0:T(8,128)(2,1)S(1)}, u32[]{:S(2)}, u32[]{:S(2)}) collective-permute-start(bf16[2,4,16,1792]{3,2,1,0:T(8,128)(2,1)S(1)} %get-tuple-element.42), channel_id=1, source_target_pairs={{0,1},{1,2},{2,3},{3,4},{4,5},{5,6},{6,7},{7,0},{8,9},{9,10},{10,1... | collective-permute-start | bytes 1376264 | tf_op jit(solution)/shard_map/ppermute | solution.py:23
  99.7 8.5 %collective-permute-start.12 = (f32[14,8,256]{2,1,0:T(8,128)S(1)}, f32[14,8,256]{2,1,0:T(8,128)S(1)}, u32[]{:S(2)}, u32[]{:S(2)}) collective-permute-start(f32[14,8,256]{2,1,0:T(8,128)S(1)} %shard_map.69.refs_9_), channel_id=1, source_target_pairs={{0,24},{1,25},{2,26},{3,27},{4,28},{5,29},{6,30},{7,31},{8,16},{9,... | collective-permute-start | bytes 344072 | tf_op jit(solution)/shard_map/ppermute | solution.py:23
  108.2 12.1 %collective-permute-start.18 = (bf16[2,4,16,1792]{3,2,1,0:T(8,128)(2,1)S(1)}, bf16[2,4,16,1792]{3,2,1,0:T(8,128)(2,1)S(1)}, u32[]{:S(2)}, u32[]{:S(2)}) collective-permute-start(bf16[2,4,16,1792]{3,2,1,0:T(8,128)(2,1)S(1)} %get-tuple-element.51), channel_id=1, source_target_pairs={{0,9},{1,10},{2,11},{3,12},{4,13},{5,14},{6,15},{7,8},{8,1},{9,2},... | collective-permute-start | bytes 1376264 | tf_op jit(solution)/shard_map/ppermute | solution.py:23
  113.5 27.7 %collective-permute-start.20 = (bf16[2,2,4,16,1792]{4,3,2,1,0:T(8,128)(2,1)S(1)}, bf16[2,2,4,16,1792]{4,3,2,1,0:T(8,128)(2,1)S(1)}, u32[]{:S(2)}, u32[]{:S(2)}) collective-permute-start(bf16[2,2,4,16,1792]{4,3,2,1,0:T(8,128)(2,1)S(1)} %get-tuple-element.54), channel_id=1, source_target_pairs={{0,1},{1,2},{2,3},{3,4},{4,5},{5,6},{6,7},{7,0},{8,9},{9,10},{10,1... | collective-permute-start | bytes 2752520 | tf_op jit(solution)/shard_map/ppermute | solution.py:23
  113.6 20.4 %collective-permute-start.16 = (bf16[2,4,16,1792]{3,2,1,0:T(8,128)(2,1)S(1)}, bf16[2,4,16,1792]{3,2,1,0:T(8,128)(2,1)S(1)}, u32[]{:S(2)}, u32[]{:S(2)}) collective-permute-start(bf16[2,4,16,1792]{3,2,1,0:T(8,128)(2,1)S(1)} %get-tuple-element.48), channel_id=1, source_target_pairs={{0,1},{1,2},{2,3},{3,4},{4,5},{5,6},{6,7},{7,0},{8,9},{9,10},{10,1... | collective-permute-start | bytes 1376264 | tf_op jit(solution)/shard_map/ppermute | solution.py:23
  113.6 20.4 %collective-permute-start.17 = (bf16[2,4,16,1792]{3,2,1,0:T(8,128)(2,1)S(1)}, bf16[2,4,16,1792]{3,2,1,0:T(8,128)(2,1)S(1)}, u32[]{:S(2)}, u32[]{:S(2)}) collective-permute-start(bf16[2,4,16,1792]{3,2,1,0:T(8,128)(2,1)S(1)} %get-tuple-element.49), channel_id=1, source_target_pairs={{0,24},{1,25},{2,26},{3,27},{4,28},{5,29},{6,30},{7,31},{8,16},{9,... | collective-permute-start | bytes 1376264 | tf_op jit(solution)/shard_map/ppermute | solution.py:23
  120.3 19.7 %collective-permute-start.19 = (bf16[2,4,16,1792]{3,2,1,0:T(8,128)(2,1)S(1)}, bf16[2,4,16,1792]{3,2,1,0:T(8,128)(2,1)S(1)}, u32[]{:S(2)}, u32[]{:S(2)}) collective-permute-start(bf16[2,4,16,1792]{3,2,1,0:T(8,128)(2,1)S(1)} %get-tuple-element.52), channel_id=1, source_target_pairs={{0,25},{1,26},{2,27},{3,28},{4,29},{5,30},{6,31},{7,24},{8,17},{9,... | collective-permute-start | bytes 1376264 | tf_op jit(solution)/shard_map/ppermute | solution.py:23

commit v4 on v3

--- a/solution.py
+++ b/solution.py
@@ -125,7 +125,7 @@
 def grads_kernel(late_ref, *refs):
     mine_ref, other_ref, kept_out = refs[9:12]
     near_out, corner_out = refs[-2:]
-    row_outs = [refs[12], refs[13].at[0], refs[13].at[1]]
+    row_outs = refs[12:15] if len(refs) == 17 else [refs[12], refs[13].at[0], refs[13].at[1]]
     _, frames, rows, columns, width = kept_out.shape
     shape = (frames, rows, columns, HEAD_DIM)
     for head in range(width // HEAD_DIM):
@@ -198,14 +198,14 @@
     )
 
 
-def family_grads(late, inputs, received, mine, other):
+def family_grads(late, inputs, received, mine, other, joined):
     frames, rows, columns, features = inputs[0].shape
     heads, length = features // HEAD_DIM, frames * rows * WW
     step = heads_per_step(heads)
     sent = jax.ShapeDtypeStruct((frames // 2, rows // 2, columns, features), jnp.bfloat16)
     kept = jax.ShapeDtypeStruct((3,) + sent.shape, jnp.bfloat16)
     two = jax.ShapeDtypeStruct((2,) + sent.shape, jnp.bfloat16)
-    shapes = [kept, sent, two, sent, sent]
+    shapes = [kept, sent] + ([two] if joined else [sent, sent]) + [sent, sent]
     return called(
         grads_kernel,
         late,
@@ -219,12 +219,11 @@
 
 def place_pair_kernel(late_ref, *refs):
     own_ref, outs = refs[0], refs[-2:]
-    row_ref = refs[1]
-    first = row_ref.shape[0] - len(outs)
+    row_refs = refs[1:3] if refs[1].ndim == 4 else [refs[1].at[0], refs[1].at[1]]
     for index, out in enumerate(outs):
         half = out.shape[1] // 2
         out[:, half:] = own_ref[1 + index]
-        out[:, :half] = row_ref[first + index]
+        out[:, :half] = row_refs[index][...]
 
 
 def place_sum_kernel(late_ref, *refs):
@@ -293,24 +292,26 @@
     row_qg1 = jnp.concatenate([row_of((x,), 1, *row_kv0) for x in qg])
     row_kv1 = rows_of_both(1, other0)
     corner1 = moved(after(row_qg1, other0, near1), 1, 0)
-    kept0, row0, pair0, near_b0, corner_b0 = family_grads(spot[0], inputs, got0, stats0, other0)
+    kept0, row0, pair0, near_b0, corner_b0 = family_grads(
+        spot[0], inputs, got0, stats0, other0, True
+    )
     got1 = (row_qg1, *row_kv1, near1, after(corner1, corner_b0))
     stats1 = family_stats(spot[1], inputs, got1)
     other1 = moved(stats1, 1, 0)
-    row0, pair0 = [moved(after(r, *row_kv1), None, 1) for r in (row0, pair0)]
+    row0, pair0 = moved(after(row0, *row_kv1), None, 1), moved(pair0, None, 1)
     near_b0 = moved(near_b0, 0, 0)
-    corner_b0 = moved(after(corner_b0, other1), 0, 1)
-    kept1, row1, pair1, near_b1, corner_b1 = family_grads(
-        spot[1], inputs, got1, stats1, after(other1, row0, pair0, near_b0)
+    corner_b0 = moved(after(corner_b0, other1, near_b0, row0, pair0), 0, 1)
+    kept1, *rows1, near_b1, corner_b1 = family_grads(
+        spot[1], inputs, got1, stats1, other1, False
     )
     near_b1 = moved(near_b1, 1, 0)
     corner_b1 = moved(after(corner_b1, near_b0, corner_b0), 1, 1)
-    row1, pair1 = moved(row1, None, 1), moved(pair1, None, 1)
+    row1, *pair1 = [moved(r, None, 1) for r in rows1]
     pair = placed(place_pair_kernel, 2, spot[0], None, (kept0, pair0), (3, 2), queries)
     total = placed(
         place_sum_kernel, 1, spot[0], None, (kept0, row0, near_b0, corner_b0), (1, 1, 1, 1), queries
     )
-    pair = placed(place_pair_kernel, 2, spot[1], pair, (kept1, pair1), (3, 2), queries)
+    pair = placed(place_pair_kernel, 2, spot[1], pair, (kept1, *pair1), (3, 1, 1), queries)
     total = placed(
         place_sum_kernel, 1, spot[1], total, (kept1, row1, near_b1, corner_b1), (1, 1, 1, 1), queries
     )

time: 144 us -> 138 us (0.958)
  waiting for transfers between devices: 82.5 us -> 73.9 us
  starting transfers between devices: 35.9 us -> 38.3 us
    ppermute x21 -> x22, waiting for transfers between devices: 82.5 us -> 73.9 us  [moved(): return lax.ppermute(value, AXES, pairs)]
    ppermute x21 -> x22, starting transfers between devices: 35.9 us -> 38.3 us  [moved(): return lax.ppermute(value, AXES, pairs)]
  transfers between devices with their start and end apart: 21 -> 22, of which waited for: 11 -> 12; matrix products, arithmetic and copies ran while one was open for 0% -> 0% of each run, Pallas kernels for 13% -> 14%
where the time goes in v4:
time: 138 us; the launch traced here: 136 us
  waiting for transfers between devices  73.9 us (54%)
  starting transfers between devices  38.3 us (28%)
  Pallas kernels  20.8 us (15%)
  local copies, waits for them, and re-layouts  2.47 us (2%)
    ppermute x22, waiting for transfers between devices, moved(): return lax.ppermute(value, AXES, pairs)  73.9 us
    ppermute x22, starting transfers between devices, moved(): return lax.ppermute(value, AXES, pairs)  38.3 us
    pallas_call x8, Pallas kernels, called(): pl.pallas_call(kernel, grid_spec=pltpu.PrefetchScalarGridSpec(num_scalar_...  20.8 us
  transfers between devices with their start and end apart: 22, of which 12 were waited for; matrix products, arithmetic and copies ran while one was open for 0% of the time, Pallas kernels for 14%

profile of v4, /device:TPU:0, one launch (start us, length us, event | category | flops | bytes accessed | tf_op | source)
XLA Modules:
  0.0 136.5 jit_solution(16899245665256896603)
XLA Ops:
  0.7 2.2 %dynamic-slice_bitcast_fusion = (bf16[1,2,4,16,1792]{4,3,2,1,0:T(8,128)(2,1)S(1)}, bf16[1,2,4,16,1792]{4,3,2,1,0:T(8,128)(2,1)S(1)}, bf16[1,2,4,16,1792]{4,3,2,1...) fusion(bf16[4,8,16,1792]{3,2,1,0:T(8,128)(2,1)} %refs_3_.7, ...), kind=kLoop, calls=%fused_computation.3 | loop fusion | bytes 7340040 | tf_op jit(solution)/shard_map/stack | solution.py:271
  2.9 0.0 copy-start.3
  2.9 0.1 pad_maximum_fusion
  3.0 4.5 %collective-permute-start = (bf16[2,2,4,16,1792]{4,3,2,1,0:T(8,128)(2,1)S(1)}, bf16[2,2,4,16,1792]{4,3,2,1,0:T(8,128)(2,1)S(1)}, u32[]{:S(2)}, u32[]{:S(2)}) collective-permute-start(bf16[2,2,4,16,1792]{4,3,2,1,0:T(8,128)(2,1)S(1)} %pad_maximum_fusion), channel_id=1, source_target_pairs={{0,7},{1,0},{2,1},{3,2},{4,3},{5,4},{6,5},{7,6},{8,15},{9,8},{10,9... | collective-permute-start | bytes 2752520 | tf_op jit(solution)/shard_map/ppermute | solution.py:23
  7.6 0.1 pad_maximum_fusion.1
  7.6 1.6 %collective-permute-start.5 = (bf16[2,2,4,16,1792]{4,3,2,1,0:T(8,128)(2,1)S(1)}, bf16[2,2,4,16,1792]{4,3,2,1,0:T(8,128)(2,1)S(1)}, u32[]{:S(2)}, u32[]{:S(2)}) collective-permute-start(bf16[2,2,4,16,1792]{4,3,2,1,0:T(8,128)(2,1)S(1)} %pad_maximum_fusion.1), channel_id=1, source_target_pairs={{0,8},{1,9},{2,10},{3,11},{4,12},{5,13},{6,14},{7,15},{8,0},{9,1},... | collective-permute-start | bytes 2752520 | tf_op jit(solution)/shard_map/ppermute | solution.py:23
  9.2 0.1 dynamic-slice_bitcast_fusion.5
  9.3 0.0 copy-start.1
  9.3 0.1 dynamic-slice_bitcast_fusion.2
  9.4 9.1 %collective-permute-done.refs_4_ = bf16[2,2,4,16,1792]{4,3,2,1,0:T(8,128)(2,1)S(1)} collective-permute-done((bf16[2,2,4,16,1792]{4,3,2,1,0:T(8,128)(2,1)S(1)}, bf16[2,2,4,16,1792]{4,3,2,1,0:T(8,128)(2,1)S(1)}, u32[]{:S(2)}, u32[]{:S(2)}) %collective-permute-start) | collective-permute-done | bytes 917536 | tf_op jit(solution)/shard_map/ppermute | solution.py:23
  18.5 3.7 %collective-permute-start.1 = (bf16[1,2,4,16,1792]{4,3,2,1,0:T(8,128)(2,1)S(1)}, bf16[1,2,4,16,1792]{4,3,2,1,0:T(8,128)(2,1)S(1)}, u32[]{:S(2)}, u32[]{:S(2)}) collective-permute-start(bf16[1,2,4,16,1792]{4,3,2,1,0:T(8,128)(2,1)S(1)} %get-tuple-element.30), channel_id=1, source_target_pairs={{0,7},{1,0},{2,1},{3,2},{4,3},{5,4},{6,5},{7,6},{8,15},{9,8},{10,9... | collective-permute-start | bytes 1376264 | tf_op jit(solution)/shard_map/ppermute | solution.py:23
  22.2 0.0 collective-permute-start.2
  22.2 1.5 %collective-permute-start.6 = (bf16[2,2,4,16,1792]{4,3,2,1,0:T(8,128)(2,1)S(1)}, bf16[2,2,4,16,1792]{4,3,2,1,0:T(8,128)(2,1)S(1)}, u32[]{:S(2)}, u32[]{:S(2)}) collective-permute-start(bf16[2,2,4,16,1792]{4,3,2,1,0:T(8,128)(2,1)S(1)} %collective-permute-done.refs_4_), channel_id=1, source_target_pairs={{0,8},{1,9},{2,10},{3,11},{4,12},{5,13},{6,14},{7,15},{8,0},{9,1},... | collective-permute-start | bytes 2752520 | tf_op jit(solution)/shard_map/ppermute | solution.py:23
  23.7 4.5 %collective-permute-done.1.refs_5_ = bf16[1,2,4,16,1792]{4,3,2,1,0:T(8,128)(2,1)S(1)} collective-permute-done((bf16[1,2,4,16,1792]{4,3,2,1,0:T(8,128)(2,1)S(1)}, bf16[1,2,4,16,1792]{4,3,2,1,0:T(8,128)(2,1)S(1)}, u32[]{:S(2)}, u32[]{:S(2)}) %collective-permute-start.1) | collective-permute-done | bytes 458784 | tf_op jit(solution)/shard_map/ppermute | solution.py:23
  28.2 4.9 %collective-permute-done.2.refs_6_ = bf16[1,2,4,16,1792]{4,3,2,1,0:T(8,128)(2,1)S(1)} collective-permute-done((bf16[1,2,4,16,1792]{4,3,2,1,0:T(8,128)(2,1)S(1)}, bf16[1,2,4,16,1792]{4,3,2,1,0:T(8,128)(2,1)S(1)}, u32[]{:S(2)}, u32[]{:S(2)}) %collective-permute-start.2) | collective-permute-done | bytes 458784 | tf_op jit(solution)/shard_map/ppermute | solution.py:23
  33.1 3.7 %collective-permute-start.3 = (bf16[1,2,4,16,1792]{4,3,2,1,0:T(8,128)(2,1)S(1)}, bf16[1,2,4,16,1792]{4,3,2,1,0:T(8,128)(2,1)S(1)}, u32[]{:S(2)}, u32[]{:S(2)}) collective-permute-start(bf16[1,2,4,16,1792]{4,3,2,1,0:T(8,128)(2,1)S(1)} %get-tuple-element.32), channel_id=1, source_target_pairs={{0,7},{1,0},{2,1},{3,2},{4,3},{5,4},{6,5},{7,6},{8,15},{9,8},{10,9... | collective-permute-start | bytes 1376264 | tf_op jit(solution)/shard_map/ppermute | solution.py:23
  36.8 0.1 pad_maximum_fusion.2
  36.9 2.5 %collective-permute-start.10 = (bf16[2,2,4,16,1792]{4,3,2,1,0:T(8,128)(2,1)S(1)}, bf16[2,2,4,16,1792]{4,3,2,1,0:T(8,128)(2,1)S(1)}, u32[]{:S(2)}, u32[]{:S(2)}) collective-permute-start(bf16[2,2,4,16,1792]{4,3,2,1,0:T(8,128)(2,1)S(1)} %pad_maximum_fusion.2), channel_id=1, source_target_pairs={{0,24},{1,25},{2,26},{3,27},{4,28},{5,29},{6,30},{7,31},{8,16},{9,... | collective-permute-start | bytes 2752520 | tf_op jit(solution)/shard_map/ppermute | solution.py:23
  39.4 9.3 %collective-permute-done.6.refs_8_ = bf16[2,2,4,16,1792]{4,3,2,1,0:T(8,128)(2,1)S(1)} collective-permute-done((bf16[2,2,4,16,1792]{4,3,2,1,0:T(8,128)(2,1)S(1)}, bf16[2,2,4,16,1792]{4,3,2,1,0:T(8,128)(2,1)S(1)}, u32[]{:S(2)}, u32[]{:S(2)}) %collective-permute-start.6) | collective-permute-done | bytes 917536 | tf_op jit(solution)/shard_map/ppermute | solution.py:23
  48.7 2.4 %shard_map.67.refs_9_ = f32[14,8,256]{2,1,0:T(8,128)S(1)} custom-call(s32[1]{0:T(128)} %bitcast.8.late_ref, bf16[4,8,16,1792]{3,2,1,0:T(8,128)(2,1)S(1)} %copy-done, bf16[4,8,16,1792]{3,2,1,0:T(8,128)(2,1)S(1)} %copy-done.3, bf16[4,8,16,1792]{3,2,1,0:T(8,128)(2,1)S(1)} %copy-done.4, bf16[4,8,16,1792]{3,2,1,0:T(8,128)(2,1)S(1)} %copy-done.1, ...), custom_call_target="tpu_custom_call" | custom-call | flops 1 | bytes 1 | tf_op jit(solution)/shard_map/pallas_call | solution.py:164
  51.1 2.1 %collective-permute-start.7 = (f32[14,8,256]{2,1,0:T(8,128)S(1)}, f32[14,8,256]{2,1,0:T(8,128)S(1)}, u32[]{:S(2)}, u32[]{:S(2)}) collective-permute-start(f32[14,8,256]{2,1,0:T(8,128)S(1)} %shard_map.67.refs_9_), channel_id=1, source_target_pairs={{0,8},{1,9},{2,10},{3,11},{4,12},{5,13},{6,14},{7,15},{8,0},{9,1},... | collective-permute-start | bytes 344072 | tf_op jit(solution)/shard_map/ppermute | solution.py:23
  53.3 15.7 %collective-permute-done.10.refs_7_ = bf16[2,2,4,16,1792]{4,3,2,1,0:T(8,128)(2,1)S(1)} collective-permute-done((bf16[2,2,4,16,1792]{4,3,2,1,0:T(8,128)(2,1)S(1)}, bf16[2,2,4,16,1792]{4,3,2,1,0:T(8,128)(2,1)S(1)}, u32[]{:S(2)}, u32[]{:S(2)}) %collective-permute-start.10) | collective-permute-done | bytes 917536 | tf_op jit(solution)/shard_map/ppermute | solution.py:23
  68.9 0.0 collective-permute-done.7.refs_10_
  69.0 2.7 %collective-permute-start.11 = (bf16[2,2,4,16,1792]{4,3,2,1,0:T(8,128)(2,1)S(1)}, bf16[2,2,4,16,1792]{4,3,2,1,0:T(8,128)(2,1)S(1)}, u32[]{:S(2)}, u32[]{:S(2)}) collective-permute-start(bf16[2,2,4,16,1792]{4,3,2,1,0:T(8,128)(2,1)S(1)} %constant_dynamic-update-slice_fusion.refs_4_), channel_id=1, source_target_pairs={{0,24},{1,25},{2,26},{3,27},{4,28},{5,29},{6,30},{7,31},{8,16},{9,... | collective-permute-start | bytes 2752520 | tf_op jit(solution)/shard_map/ppermute | solution.py:23
  71.7 2.6 %collective-permute-start.8 = (bf16[1,2,4,16,1792]{4,3,2,1,0:T(8,128)(2,1)S(1)}, bf16[1,2,4,16,1792]{4,3,2,1,0:T(8,128)(2,1)S(1)}, u32[]{:S(2)}, u32[]{:S(2)}) collective-permute-start(bf16[1,2,4,16,1792]{4,3,2,1,0:T(8,128)(2,1)S(1)} %get-tuple-element.34), channel_id=1, source_target_pairs={{0,7},{1,0},{2,1},{3,2},{4,3},{5,4},{6,5},{7,6},{8,15},{9,8},{10,9... | collective-permute-start | bytes 1376264 | tf_op jit(solution)/shard_map/ppermute | solution.py:23
  74.3 1.1 collective-permute-start.9
  75.4 5.2 %shard_map.68 = (bf16[3,2,4,16,1792]{4,3,2,1,0:T(8,128)(2,1)S(1)}, bf16[2,4,16,1792]{3,2,1,0:T(8,128)(2,1)S(1)}, bf16[2,2,4,16,1792]{4,3,2,1,0:T(8,128)(2,1)S(1)...) custom-call(s32[1]{0:T(128)} %bitcast.8.late_ref, bf16[4,8,16,1792]{3,2,1,0:T(8,128)(2,1)S(1)} %copy-done, ...), custom_call_target="tpu_custom_call" | custom-call | flops 1 | bytes 1 | tf_op jit(solution)/shard_map/pallas_call | solution.py:164
  80.6 0.1 collective-permute-start.17
  80.7 0.6 collective-permute-start.15
  81.3 8.6 %collective-permute-done.9.refs_6_ = bf16[1,2,4,16,1792]{4,3,2,1,0:T(8,128)(2,1)S(1)} collective-permute-done((bf16[1,2,4,16,1792]{4,3,2,1,0:T(8,128)(2,1)S(1)}, bf16[1,2,4,16,1792]{4,3,2,1,0:T(8,128)(2,1)S(1)}, u32[]{:S(2)}, u32[]{:S(2)}) %collective-permute-start.9) | collective-permute-done | bytes 458784 | tf_op jit(solution)/shard_map/ppermute | solution.py:23
  89.9 3.3 %collective-permute-done.11.refs_8_ = bf16[2,2,4,16,1792]{4,3,2,1,0:T(8,128)(2,1)S(1)} collective-permute-done((bf16[2,2,4,16,1792]{4,3,2,1,0:T(8,128)(2,1)S(1)}, bf16[2,2,4,16,1792]{4,3,2,1,0:T(8,128)(2,1)S(1)}, u32[]{:S(2)}, u32[]{:S(2)}) %collective-permute-start.11) | collective-permute-done | bytes 917536 | tf_op jit(solution)/shard_map/ppermute | solution.py:23
  93.2 2.4 %shard_map.69.refs_9_ = f32[14,8,256]{2,1,0:T(8,128)S(1)} custom-call(s32[1]{0:T(128)} %bitcast.late_ref, bf16[4,8,16,1792]{3,2,1,0:T(8,128)(2,1)S(1)} %copy-done, bf16[4,8,16,1792]{3,2,1,0:T(8,128)(2,1)S(1)} %copy-done.3, bf16[4,8,16,1792]{3,2,1,0:T(8,128)(2,1)S(1)} %copy-done.4, bf16[4,8,16,1792]{3,2,1,0:T(8,128)(2,1)S(1)} %copy-done.2, ...), custom_call_target="tpu_custom_call" | custom-call | flops 1 | bytes 1 | tf_op jit(solution)/shard_map/pallas_call | solution.py:164
  95.6 2.8 %collective-permute-start.12 = (f32[14,8,256]{2,1,0:T(8,128)S(1)}, f32[14,8,256]{2,1,0:T(8,128)S(1)}, u32[]{:S(2)}, u32[]{:S(2)}) collective-permute-start(f32[14,8,256]{2,1,0:T(8,128)S(1)} %shard_map.69.refs_9_), channel_id=1, source_target_pairs={{0,24},{1,25},{2,26},{3,27},{4,28},{5,29},{6,30},{7,31},{8,16},{9,... | collective-permute-start | bytes 344072 | tf_op jit(solution)/shard_map/ppermute | solution.py:23
  98.4 3.1 %collective-permute-done.15.refs_2_ = bf16[2,4,16,1792]{3,2,1,0:T(8,128)(2,1)S(1)} collective-permute-done((bf16[2,4,16,1792]{3,2,1,0:T(8,128)(2,1)S(1)}, bf16[2,4,16,1792]{3,2,1,0:T(8,128)(2,1)S(1)}, u32[]{:S(2)}, u32[]{:S(2)}) %collective-permute-start.15) | collective-permute-done | bytes 458784 | tf_op jit(solution)/shard_map/ppermute | solution.py:23
  101.5 1.2 collective-permute-done.12.refs_10_
  102.7 5.2 %shard_map.70 = (bf16[3,2,4,16,1792]{4,3,2,1,0:T(8,128)(2,1)S(1)}, bf16[2,4,16,1792]{3,2,1,0:T(8,128)(2,1)S(1)}, bf16[2,4,16,1792]{3,2,1,0:T(8,128)(2,1)S(1)}, b...) custom-call(s32[1]{0:T(128)} %bitcast.late_ref, ...), custom_call_target="tpu_custom_call" | custom-call | flops 1 | bytes 1 | tf_op jit(solution)/shard_map/pallas_call | solution.py:164
  107.9 4.3 %collective-permute-start.13 = (bf16[2,4,16,1792]{3,2,1,0:T(8,128)(2,1)S(1)}, bf16[2,4,16,1792]{3,2,1,0:T(8,128)(2,1)S(1)}, u32[]{:S(2)}, u32[]{:S(2)}) collective-permute-start(bf16[2,4,16,1792]{3,2,1,0:T(8,128)(2,1)S(1)} %get-tuple-element.41), channel_id=1, source_target_pairs={{0,1},{1,2},{2,3},{3,4},{4,5},{5,6},{6,7},{7,0},{8,9},{9,10},{10,1... | collective-permute-start | bytes 1376264 | tf_op jit(solution)/shard_map/ppermute | solution.py:23
  112.2 0.1 collective-permute-start.20
  112.3 1.6 %collective-permute-start.21 = (bf16[2,4,16,1792]{3,2,1,0:T(8,128)(2,1)S(1)}, bf16[2,4,16,1792]{3,2,1,0:T(8,128)(2,1)S(1)}, u32[]{:S(2)}, u32[]{:S(2)}) collective-permute-start(bf16[2,4,16,1792]{3,2,1,0:T(8,128)(2,1)S(1)} %get-tuple-element.52), channel_id=1, source_target_pairs={{0,1},{1,2},{2,3},{3,4},{4,5},{5,6},{6,7},{7,0},{8,9},{9,10},{10,1... | collective-permute-start | bytes 1376264 | tf_op jit(solution)/shard_map/ppermute | solution.py:23
  113.9 1.5 %collective-permute-start.14 = (bf16[2,4,16,1792]{3,2,1,0:T(8,128)(2,1)S(1)}, bf16[2,4,16,1792]{3,2,1,0:T(8,128)(2,1)S(1)}, u32[]{:S(2)}, u32[]{:S(2)}) collective-permute-start(bf16[2,4,16,1792]{3,2,1,0:T(8,128)(2,1)S(1)} %get-tuple-element.42), channel_id=1, source_target_pairs={{0,24},{1,25},{2,26},{3,27},{4,28},{5,29},{6,30},{7,31},{8,16},{9,... | collective-permute-start | bytes 1376264 | tf_op jit(solution)/shard_map/ppermute | solution.py:23
  115.4 1.3 collective-permute-start.19
  116.8 1.5 %shard_map.73 = (bf16[4,8,16,1792]{3,2,1,0:T(8,128)(2,1)}, bf16[4,8,16,1792]{3,2,1,0:T(8,128)(2,1)}) custom-call(s32[1]{0:T(128)} %bitcast.8.late_ref, bf16[3,2,4,16,1792]{4,3,2,1,0:T(8,128)(2,1)S(1)} %get-tuple-element.50.refs_0_, bf16[2,2,4,16,1792]{4,3,2,1,0:T(8,128)(2,1)S(1)} %collective-permute-done.17.refs_1_), custom_call_target="tpu_custom_call" | custom-call | flops 1 | bytes 1 | tf_op jit(solution)/shard_map/pallas_call | solution.py:164
  118.3 1.2 shard_map.71.refs_4_
  119.5 4.0 %collective-permute-done.20.refs_1_ = bf16[2,4,16,1792]{3,2,1,0:T(8,128)(2,1)S(1)} collective-permute-done((bf16[2,4,16,1792]{3,2,1,0:T(8,128)(2,1)S(1)}, bf16[2,4,16,1792]{3,2,1,0:T(8,128)(2,1)S(1)}, u32[]{:S(2)}, u32[]{:S(2)}) %collective-permute-start.20) | collective-permute-done | bytes 458784 | tf_op jit(solution)/shard_map/ppermute | solution.py:23
  123.5 4.9 %collective-permute-done.21.refs_2_ = bf16[2,4,16,1792]{3,2,1,0:T(8,128)(2,1)S(1)} collective-permute-done((bf16[2,4,16,1792]{3,2,1,0:T(8,128)(2,1)S(1)}, bf16[2,4,16,1792]{3,2,1,0:T(8,128)(2,1)S(1)}, u32[]{:S(2)}, u32[]{:S(2)}) %collective-permute-start.21) | collective-permute-done | bytes 458784 | tf_op jit(solution)/shard_map/ppermute | solution.py:23
  128.4 1.5 %shard_map.74 = (bf16[4,8,16,1792]{3,2,1,0:T(8,128)(2,1)}, bf16[4,8,16,1792]{3,2,1,0:T(8,128)(2,1)}) custom-call(s32[1]{0:T(128)} %bitcast.late_ref, bf16[3,2,4,16,1792]{4,3,2,1,0:T(8,128)(2,1)S(1)} %get-tuple-element.40.refs_0_, bf16[2,4,16,1792]{3,2,1,0:T(8,128)(2,1)S(1)} %collective-permute-done.20.refs_1_, ...), custom_call_target="tpu_custom_call", output_to_operand_aliasing={{0}: (4, {}), {1}: (5, {})} | custom-call | flops 1 | bytes 1 | tf_op jit(solution)/shard_map/pallas_call | solution.py:164
  129.9 5.3 %collective-permute-done.19.refs_3_ = bf16[2,4,16,1792]{3,2,1,0:T(8,128)(2,1)S(1)} collective-permute-done((bf16[2,4,16,1792]{3,2,1,0:T(8,128)(2,1)S(1)}, bf16[2,4,16,1792]{3,2,1,0:T(8,128)(2,1)S(1)}, u32[]{:S(2)}, u32[]{:S(2)}) %collective-permute-start.19) | collective-permute-done | bytes 458784 | tf_op jit(solution)/shard_map/ppermute | solution.py:23
  135.3 1.2 shard_map.72
  (22 shorter events, 0.1 us)
Async XLA Ops:
  2.9 6.3 %copy-start.3 = (bf16[4,8,16,1792]{3,2,1,0:T(8,128)(2,1)S(1)}, bf16[4,8,16,1792]{3,2,1,0:T(8,128)(2,1)}, u32[]{:S(2)}) copy-start(bf16[4,8,16,1792]{3,2,1,0:T(8,128)(2,1)} %refs_1_.7) | copy-start | bytes 5505028
  3.0 15.5 %collective-permute-start = (bf16[2,2,4,16,1792]{4,3,2,1,0:T(8,128)(2,1)S(1)}, bf16[2,2,4,16,1792]{4,3,2,1,0:T(8,128)(2,1)S(1)}, u32[]{:S(2)}, u32[]{:S(2)}) collective-permute-start(bf16[2,2,4,16,1792]{4,3,2,1,0:T(8,128)(2,1)S(1)} %pad_maximum_fusion), channel_id=1, source_target_pairs={{0,7},{1,0},{2,1},{3,2},{4,3},{5,4},{6,5},{7,6},{8,15},{9,8},{10,9... | collective-permute-start | bytes 2752520 | tf_op jit(solution)/shard_map/ppermute | solution.py:23
  7.6 1.7 %copy-start.4 = (bf16[4,8,16,1792]{3,2,1,0:T(8,128)(2,1)S(1)}, bf16[4,8,16,1792]{3,2,1,0:T(8,128)(2,1)}, u32[]{:S(2)}) copy-start(bf16[4,8,16,1792]{3,2,1,0:T(8,128)(2,1)} %refs_2_.7) | copy-start | bytes 5505028
  7.6 29.2 %collective-permute-start.5 = (bf16[2,2,4,16,1792]{4,3,2,1,0:T(8,128)(2,1)S(1)}, bf16[2,2,4,16,1792]{4,3,2,1,0:T(8,128)(2,1)S(1)}, u32[]{:S(2)}, u32[]{:S(2)}) collective-permute-start(bf16[2,2,4,16,1792]{4,3,2,1,0:T(8,128)(2,1)S(1)} %pad_maximum_fusion.1), channel_id=1, source_target_pairs={{0,8},{1,9},{2,10},{3,11},{4,12},{5,13},{6,14},{7,15},{8,0},{9,1},... | collective-permute-start | bytes 2752520 | tf_op jit(solution)/shard_map/ppermute | solution.py:23
  9.3 39.4 %copy-start = (bf16[4,8,16,1792]{3,2,1,0:T(8,128)(2,1)S(1)}, bf16[4,8,16,1792]{3,2,1,0:T(8,128)(2,1)}, u32[]{:S(2)}) copy-start(bf16[4,8,16,1792]{3,2,1,0:T(8,128)(2,1)} %refs_0_.7) | copy-start | bytes 5505028
  9.3 39.4 %copy-start.1 = (bf16[4,8,16,1792]{3,2,1,0:T(8,128)(2,1)S(1)}, bf16[4,8,16,1792]{3,2,1,0:T(8,128)(2,1)}, u32[]{:S(2)}) copy-start(bf16[4,8,16,1792]{3,2,1,0:T(8,128)(2,1)} %refs_3_.7) | copy-start | bytes 5505028
  18.5 9.7 %collective-permute-start.1 = (bf16[1,2,4,16,1792]{4,3,2,1,0:T(8,128)(2,1)S(1)}, bf16[1,2,4,16,1792]{4,3,2,1,0:T(8,128)(2,1)S(1)}, u32[]{:S(2)}, u32[]{:S(2)}) collective-permute-start(bf16[1,2,4,16,1792]{4,3,2,1,0:T(8,128)(2,1)S(1)} %get-tuple-element.30), channel_id=1, source_target_pairs={{0,7},{1,0},{2,1},{3,2},{4,3},{5,4},{6,5},{7,6},{8,15},{9,8},{10,9... | collective-permute-start | bytes 1376264 | tf_op jit(solution)/shard_map/ppermute | solution.py:23
  22.2 10.9 %collective-permute-start.2 = (bf16[1,2,4,16,1792]{4,3,2,1,0:T(8,128)(2,1)S(1)}, bf16[1,2,4,16,1792]{4,3,2,1,0:T(8,128)(2,1)S(1)}, u32[]{:S(2)}, u32[]{:S(2)}) collective-permute-start(bf16[1,2,4,16,1792]{4,3,2,1,0:T(8,128)(2,1)S(1)} %get-tuple-element.31), channel_id=1, source_target_pairs={{0,7},{1,0},{2,1},{3,2},{4,3},{5,4},{6,5},{7,6},{8,15},{9,8},{10,9... | collective-permute-start | bytes 1376264 | tf_op jit(solution)/shard_map/ppermute | solution.py:23
  22.2 26.5 %collective-permute-start.6 = (bf16[2,2,4,16,1792]{4,3,2,1,0:T(8,128)(2,1)S(1)}, bf16[2,2,4,16,1792]{4,3,2,1,0:T(8,128)(2,1)S(1)}, u32[]{:S(2)}, u32[]{:S(2)}) collective-permute-start(bf16[2,2,4,16,1792]{4,3,2,1,0:T(8,128)(2,1)S(1)} %collective-permute-done.refs_4_), channel_id=1, source_target_pairs={{0,8},{1,9},{2,10},{3,11},{4,12},{5,13},{6,14},{7,15},{8,0},{9,1},... | collective-permute-start | bytes 2752520 | tf_op jit(solution)/shard_map/ppermute | solution.py:23
  33.1 20.1 %collective-permute-start.3 = (bf16[1,2,4,16,1792]{4,3,2,1,0:T(8,128)(2,1)S(1)}, bf16[1,2,4,16,1792]{4,3,2,1,0:T(8,128)(2,1)S(1)}, u32[]{:S(2)}, u32[]{:S(2)}) collective-permute-start(bf16[1,2,4,16,1792]{4,3,2,1,0:T(8,128)(2,1)S(1)} %get-tuple-element.32), channel_id=1, source_target_pairs={{0,7},{1,0},{2,1},{3,2},{4,3},{5,4},{6,5},{7,6},{8,15},{9,8},{10,9... | collective-permute-start | bytes 1376264 | tf_op jit(solution)/shard_map/ppermute | solution.py:23
  36.9 32.1 %collective-permute-start.10 = (bf16[2,2,4,16,1792]{4,3,2,1,0:T(8,128)(2,1)S(1)}, bf16[2,2,4,16,1792]{4,3,2,1,0:T(8,128)(2,1)S(1)}, u32[]{:S(2)}, u32[]{:S(2)}) collective-permute-start(bf16[2,2,4,16,1792]{4,3,2,1,0:T(8,128)(2,1)S(1)} %pad_maximum_fusion.2), channel_id=1, source_target_pairs={{0,24},{1,25},{2,26},{3,27},{4,28},{5,29},{6,30},{7,31},{8,16},{9,... | collective-permute-start | bytes 2752520 | tf_op jit(solution)/shard_map/ppermute | solution.py:23
  39.4 13.8 %collective-permute-start.4 = (bf16[1,2,4,16,1792]{4,3,2,1,0:T(8,128)(2,1)S(1)}, bf16[1,2,4,16,1792]{4,3,2,1,0:T(8,128)(2,1)S(1)}, u32[]{:S(2)}, u32[]{:S(2)}) collective-permute-start(bf16[1,2,4,16,1792]{4,3,2,1,0:T(8,128)(2,1)S(1)} %get-tuple-element.33), channel_id=1, source_target_pairs={{0,7},{1,0},{2,1},{3,2},{4,3},{5,4},{6,5},{7,6},{8,15},{9,8},{10,9... | collective-permute-start | bytes 1376264 | tf_op jit(solution)/shard_map/ppermute | solution.py:23
  51.1 17.8 %collective-permute-start.7 = (f32[14,8,256]{2,1,0:T(8,128)S(1)}, f32[14,8,256]{2,1,0:T(8,128)S(1)}, u32[]{:S(2)}, u32[]{:S(2)}) collective-permute-start(f32[14,8,256]{2,1,0:T(8,128)S(1)} %shard_map.67.refs_9_), channel_id=1, source_target_pairs={{0,8},{1,9},{2,10},{3,11},{4,12},{5,13},{6,14},{7,15},{8,0},{9,1},... | collective-permute-start | bytes 344072 | tf_op jit(solution)/shard_map/ppermute | solution.py:23
  69.0 24.2 %collective-permute-start.11 = (bf16[2,2,4,16,1792]{4,3,2,1,0:T(8,128)(2,1)S(1)}, bf16[2,2,4,16,1792]{4,3,2,1,0:T(8,128)(2,1)S(1)}, u32[]{:S(2)}, u32[]{:S(2)}) collective-permute-start(bf16[2,2,4,16,1792]{4,3,2,1,0:T(8,128)(2,1)S(1)} %constant_dynamic-update-slice_fusion.refs_4_), channel_id=1, source_target_pairs={{0,24},{1,25},{2,26},{3,27},{4,28},{5,29},{6,30},{7,31},{8,16},{9,... | collective-permute-start | bytes 2752520 | tf_op jit(solution)/shard_map/ppermute | solution.py:23
  71.7 21.5 %copy-start.2 = (bf16[4,8,16,1792]{3,2,1,0:T(8,128)(2,1)S(1)}, bf16[4,8,16,1792]{3,2,1,0:T(8,128)(2,1)}, u32[]{:S(2)}) copy-start(bf16[4,8,16,1792]{3,2,1,0:T(8,128)(2,1)} %refs_3_.7) | copy-start | bytes 5505028
  71.7 9.6 %collective-permute-start.8 = (bf16[1,2,4,16,1792]{4,3,2,1,0:T(8,128)(2,1)S(1)}, bf16[1,2,4,16,1792]{4,3,2,1,0:T(8,128)(2,1)S(1)}, u32[]{:S(2)}, u32[]{:S(2)}) collective-permute-start(bf16[1,2,4,16,1792]{4,3,2,1,0:T(8,128)(2,1)S(1)} %get-tuple-element.34), channel_id=1, source_target_pairs={{0,7},{1,0},{2,1},{3,2},{4,3},{5,4},{6,5},{7,6},{8,15},{9,8},{10,9... | collective-permute-start | bytes 1376264 | tf_op jit(solution)/shard_map/ppermute | solution.py:23
  74.3 15.6 %collective-permute-start.9 = (bf16[1,2,4,16,1792]{4,3,2,1,0:T(8,128)(2,1)S(1)}, bf16[1,2,4,16,1792]{4,3,2,1,0:T(8,128)(2,1)S(1)}, u32[]{:S(2)}, u32[]{:S(2)}) collective-permute-start(bf16[1,2,4,16,1792]{4,3,2,1,0:T(8,128)(2,1)S(1)} %get-tuple-element.35), channel_id=1, source_target_pairs={{0,7},{1,0},{2,1},{3,2},{4,3},{5,4},{6,5},{7,6},{8,15},{9,8},{10,9... | collective-permute-start | bytes 1376264 | tf_op jit(solution)/shard_map/ppermute | solution.py:23
  80.6 20.9 %collective-permute-start.17 = (bf16[2,2,4,16,1792]{4,3,2,1,0:T(8,128)(2,1)S(1)}, bf16[2,2,4,16,1792]{4,3,2,1,0:T(8,128)(2,1)S(1)}, u32[]{:S(2)}, u32[]{:S(2)}) collective-permute-start(bf16[2,2,4,16,1792]{4,3,2,1,0:T(8,128)(2,1)S(1)} %get-tuple-element.47), channel_id=1, source_target_pairs={{0,1},{1,2},{2,3},{3,4},{4,5},{5,6},{6,7},{7,0},{8,9},{9,10},{10,1... | collective-permute-start | bytes 2752520 | tf_op jit(solution)/shard_map/ppermute | solution.py:23
  80.7 20.8 %collective-permute-start.15 = (bf16[2,4,16,1792]{3,2,1,0:T(8,128)(2,1)S(1)}, bf16[2,4,16,1792]{3,2,1,0:T(8,128)(2,1)S(1)}, u32[]{:S(2)}, u32[]{:S(2)}) collective-permute-start(bf16[2,4,16,1792]{3,2,1,0:T(8,128)(2,1)S(1)} %get-tuple-element.44), channel_id=1, source_target_pairs={{0,8},{1,9},{2,10},{3,11},{4,12},{5,13},{6,14},{7,15},{8,0},{9,1},... | collective-permute-start | bytes 1376264 | tf_op jit(solution)/shard_map/ppermute | solution.py:23
  89.9 11.6 %collective-permute-start.16 = (bf16[2,4,16,1792]{3,2,1,0:T(8,128)(2,1)S(1)}, bf16[2,4,16,1792]{3,2,1,0:T(8,128)(2,1)S(1)}, u32[]{:S(2)}, u32[]{:S(2)}) collective-permute-start(bf16[2,4,16,1792]{3,2,1,0:T(8,128)(2,1)S(1)} %get-tuple-element.46), channel_id=1, source_target_pairs={{0,1},{1,2},{2,3},{3,4},{4,5},{5,6},{6,7},{7,0},{8,9},{9,10},{10,1... | collective-permute-start | bytes 1376264 | tf_op jit(solution)/shard_map/ppermute | solution.py:23
  95.6 7.1 %collective-permute-start.12 = (f32[14,8,256]{2,1,0:T(8,128)S(1)}, f32[14,8,256]{2,1,0:T(8,128)S(1)}, u32[]{:S(2)}, u32[]{:S(2)}) collective-permute-start(f32[14,8,256]{2,1,0:T(8,128)S(1)} %shard_map.69.refs_9_), channel_id=1, source_target_pairs={{0,24},{1,25},{2,26},{3,27},{4,28},{5,29},{6,30},{7,31},{8,16},{9,... | collective-permute-start | bytes 344072 | tf_op jit(solution)/shard_map/ppermute | solution.py:23
  102.7 12.8 %collective-permute-start.18 = (bf16[2,4,16,1792]{3,2,1,0:T(8,128)(2,1)S(1)}, bf16[2,4,16,1792]{3,2,1,0:T(8,128)(2,1)S(1)}, u32[]{:S(2)}, u32[]{:S(2)}) collective-permute-start(bf16[2,4,16,1792]{3,2,1,0:T(8,128)(2,1)S(1)} %get-tuple-element.48), channel_id=1, source_target_pairs={{0,9},{1,10},{2,11},{3,12},{4,13},{5,14},{6,15},{7,8},{8,1},{9,2},... | collective-permute-start | bytes 1376264 | tf_op jit(solution)/shard_map/ppermute | solution.py:23
  107.9 22.0 %collective-permute-start.13 = (bf16[2,4,16,1792]{3,2,1,0:T(8,128)(2,1)S(1)}, bf16[2,4,16,1792]{3,2,1,0:T(8,128)(2,1)S(1)}, u32[]{:S(2)}, u32[]{:S(2)}) collective-permute-start(bf16[2,4,16,1792]{3,2,1,0:T(8,128)(2,1)S(1)} %get-tuple-element.41), channel_id=1, source_target_pairs={{0,1},{1,2},{2,3},{3,4},{4,5},{5,6},{6,7},{7,0},{8,9},{9,10},{10,1... | collective-permute-start | bytes 1376264 | tf_op jit(solution)/shard_map/ppermute | solution.py:23
  112.2 11.3 %collective-permute-start.20 = (bf16[2,4,16,1792]{3,2,1,0:T(8,128)(2,1)S(1)}, bf16[2,4,16,1792]{3,2,1,0:T(8,128)(2,1)S(1)}, u32[]{:S(2)}, u32[]{:S(2)}) collective-permute-start(bf16[2,4,16,1792]{3,2,1,0:T(8,128)(2,1)S(1)} %get-tuple-element.51), channel_id=1, source_target_pairs={{0,1},{1,2},{2,3},{3,4},{4,5},{5,6},{6,7},{7,0},{8,9},{9,10},{10,1... | collective-permute-start | bytes 1376264 | tf_op jit(solution)/shard_map/ppermute | solution.py:23
  112.3 16.1 %collective-permute-start.21 = (bf16[2,4,16,1792]{3,2,1,0:T(8,128)(2,1)S(1)}, bf16[2,4,16,1792]{3,2,1,0:T(8,128)(2,1)S(1)}, u32[]{:S(2)}, u32[]{:S(2)}) collective-permute-start(bf16[2,4,16,1792]{3,2,1,0:T(8,128)(2,1)S(1)} %get-tuple-element.52), channel_id=1, source_target_pairs={{0,1},{1,2},{2,3},{3,4},{4,5},{5,6},{6,7},{7,0},{8,9},{9,10},{10,1... | collective-permute-start | bytes 1376264 | tf_op jit(solution)/shard_map/ppermute | solution.py:23
  113.9 16.0 %collective-permute-start.14 = (bf16[2,4,16,1792]{3,2,1,0:T(8,128)(2,1)S(1)}, bf16[2,4,16,1792]{3,2,1,0:T(8,128)(2,1)S(1)}, u32[]{:S(2)}, u32[]{:S(2)}) collective-permute-start(bf16[2,4,16,1792]{3,2,1,0:T(8,128)(2,1)S(1)} %get-tuple-element.42), channel_id=1, source_target_pairs={{0,24},{1,25},{2,26},{3,27},{4,28},{5,29},{6,30},{7,31},{8,16},{9,... | collective-permute-start | bytes 1376264 | tf_op jit(solution)/shard_map/ppermute | solution.py:23
  115.4 19.8 %collective-permute-start.19 = (bf16[2,4,16,1792]{3,2,1,0:T(8,128)(2,1)S(1)}, bf16[2,4,16,1792]{3,2,1,0:T(8,128)(2,1)S(1)}, u32[]{:S(2)}, u32[]{:S(2)}) collective-permute-start(bf16[2,4,16,1792]{3,2,1,0:T(8,128)(2,1)S(1)} %get-tuple-element.49), channel_id=1, source_target_pairs={{0,25},{1,26},{2,27},{3,28},{4,29},{5,30},{6,31},{7,24},{8,17},{9,... | collective-permute-start | bytes 1376264 | tf_op jit(solution)/shard_map/ppermute | solution.py:23

commit v5 on v4

--- a/solution.py
+++ b/solution.py
@@ -291,7 +291,7 @@
     other0 = moved(stats0, 0, 0)
     row_qg1 = jnp.concatenate([row_of((x,), 1, *row_kv0) for x in qg])
     row_kv1 = rows_of_both(1, other0)
-    corner1 = moved(after(row_qg1, other0, near1), 1, 0)
+    corner1 = moved(after(row_qg1, stats0, near1), 1, 0)
     kept0, row0, pair0, near_b0, corner_b0 = family_grads(
         spot[0], inputs, got0, stats0, other0, True
     )

time: 138 us -> 136 us (0.986)
  starting transfers between devices: 38.3 us -> 34.2 us
  waiting for transfers between devices: 73.9 us -> 75.6 us
    ppermute x22, starting transfers between devices: 38.3 us -> 34.2 us  [moved(): return lax.ppermute(value, AXES, pairs)]
    ppermute x22, waiting for transfers between devices: 73.9 us -> 75.6 us  [moved(): return lax.ppermute(value, AXES, pairs)]
  transfers between devices with their start and end apart: 22 -> 22, of which waited for: 12 -> 13; matrix products, arithmetic and copies ran while one was open for 0% -> 0% of each run, Pallas kernels for 14% -> 15%
where the time goes in v5:
time: 136 us; the launch traced here: 134 us
  waiting for transfers between devices  75.6 us (56%)
  starting transfers between devices  34.2 us (25%)
  Pallas kernels  20.8 us (15%)
  local copies, waits for them, and re-layouts  2.47 us (2%)
    ppermute x22, waiting for transfers between devices, moved(): return lax.ppermute(value, AXES, pairs)  75.6 us
    ppermute x22, starting transfers between devices, moved(): return lax.ppermute(value, AXES, pairs)  34.2 us
    pallas_call x8, Pallas kernels, called(): pl.pallas_call(kernel, grid_spec=pltpu.PrefetchScalarGridSpec(num_scalar_...  20.8 us
  transfers between devices with their start and end apart: 22, of which 13 were waited for; matrix products, arithmetic and copies ran while one was open for 0% of the time, Pallas kernels for 15%

profile of v5, /device:TPU:0, one launch (start us, length us, event | category | flops | bytes accessed | tf_op | source)
XLA Modules:
  0.0 134.0 jit_solution(17928029864204427860)
XLA Ops:
  0.7 2.2 %dynamic-slice_bitcast_fusion = (bf16[1,2,4,16,1792]{4,3,2,1,0:T(8,128)(2,1)S(1)}, bf16[1,2,4,16,1792]{4,3,2,1,0:T(8,128)(2,1)S(1)}, bf16[1,2,4,16,1792]{4,3,2,1...) fusion(bf16[4,8,16,1792]{3,2,1,0:T(8,128)(2,1)} %refs_3_.7, ...), kind=kLoop, calls=%fused_computation.3 | loop fusion | bytes 7340040 | tf_op jit(solution)/shard_map/stack | solution.py:271
  2.9 0.0 copy-start.3
  2.9 0.1 pad_maximum_fusion
  3.0 4.5 %collective-permute-start = (bf16[2,2,4,16,1792]{4,3,2,1,0:T(8,128)(2,1)S(1)}, bf16[2,2,4,16,1792]{4,3,2,1,0:T(8,128)(2,1)S(1)}, u32[]{:S(2)}, u32[]{:S(2)}) collective-permute-start(bf16[2,2,4,16,1792]{4,3,2,1,0:T(8,128)(2,1)S(1)} %pad_maximum_fusion), channel_id=1, source_target_pairs={{0,7},{1,0},{2,1},{3,2},{4,3},{5,4},{6,5},{7,6},{8,15},{9,8},{10,9... | collective-permute-start | bytes 2752520 | tf_op jit(solution)/shard_map/ppermute | solution.py:23
  7.6 0.1 pad_maximum_fusion.1
  7.6 1.6 %collective-permute-start.5 = (bf16[2,2,4,16,1792]{4,3,2,1,0:T(8,128)(2,1)S(1)}, bf16[2,2,4,16,1792]{4,3,2,1,0:T(8,128)(2,1)S(1)}, u32[]{:S(2)}, u32[]{:S(2)}) collective-permute-start(bf16[2,2,4,16,1792]{4,3,2,1,0:T(8,128)(2,1)S(1)} %pad_maximum_fusion.1), channel_id=1, source_target_pairs={{0,8},{1,9},{2,10},{3,11},{4,12},{5,13},{6,14},{7,15},{8,0},{9,1},... | collective-permute-start | bytes 2752520 | tf_op jit(solution)/shard_map/ppermute | solution.py:23
  9.2 0.1 dynamic-slice_bitcast_fusion.5
  9.3 0.0 copy-start
  9.3 0.1 dynamic-slice_bitcast_fusion.2
  9.4 9.1 %collective-permute-done.refs_4_ = bf16[2,2,4,16,1792]{4,3,2,1,0:T(8,128)(2,1)S(1)} collective-permute-done((bf16[2,2,4,16,1792]{4,3,2,1,0:T(8,128)(2,1)S(1)}, bf16[2,2,4,16,1792]{4,3,2,1,0:T(8,128)(2,1)S(1)}, u32[]{:S(2)}, u32[]{:S(2)}) %collective-permute-start) | collective-permute-done | bytes 917536 | tf_op jit(solution)/shard_map/ppermute | solution.py:23
  18.5 3.7 %collective-permute-start.1 = (bf16[1,2,4,16,1792]{4,3,2,1,0:T(8,128)(2,1)S(1)}, bf16[1,2,4,16,1792]{4,3,2,1,0:T(8,128)(2,1)S(1)}, u32[]{:S(2)}, u32[]{:S(2)}) collective-permute-start(bf16[1,2,4,16,1792]{4,3,2,1,0:T(8,128)(2,1)S(1)} %get-tuple-element.30), channel_id=1, source_target_pairs={{0,7},{1,0},{2,1},{3,2},{4,3},{5,4},{6,5},{7,6},{8,15},{9,8},{10,9... | collective-permute-start | bytes 1376264 | tf_op jit(solution)/shard_map/ppermute | solution.py:23
  22.2 0.0 collective-permute-start.2
  22.2 1.5 %collective-permute-start.6 = (bf16[2,2,4,16,1792]{4,3,2,1,0:T(8,128)(2,1)S(1)}, bf16[2,2,4,16,1792]{4,3,2,1,0:T(8,128)(2,1)S(1)}, u32[]{:S(2)}, u32[]{:S(2)}) collective-permute-start(bf16[2,2,4,16,1792]{4,3,2,1,0:T(8,128)(2,1)S(1)} %collective-permute-done.refs_4_), channel_id=1, source_target_pairs={{0,8},{1,9},{2,10},{3,11},{4,12},{5,13},{6,14},{7,15},{8,0},{9,1},... | collective-permute-start | bytes 2752520 | tf_op jit(solution)/shard_map/ppermute | solution.py:23
  23.7 4.5 %collective-permute-done.1.refs_5_ = bf16[1,2,4,16,1792]{4,3,2,1,0:T(8,128)(2,1)S(1)} collective-permute-done((bf16[1,2,4,16,1792]{4,3,2,1,0:T(8,128)(2,1)S(1)}, bf16[1,2,4,16,1792]{4,3,2,1,0:T(8,128)(2,1)S(1)}, u32[]{:S(2)}, u32[]{:S(2)}) %collective-permute-start.1) | collective-permute-done | bytes 458784 | tf_op jit(solution)/shard_map/ppermute | solution.py:23
  28.2 4.9 %collective-permute-done.2.refs_6_ = bf16[1,2,4,16,1792]{4,3,2,1,0:T(8,128)(2,1)S(1)} collective-permute-done((bf16[1,2,4,16,1792]{4,3,2,1,0:T(8,128)(2,1)S(1)}, bf16[1,2,4,16,1792]{4,3,2,1,0:T(8,128)(2,1)S(1)}, u32[]{:S(2)}, u32[]{:S(2)}) %collective-permute-start.2) | collective-permute-done | bytes 458784 | tf_op jit(solution)/shard_map/ppermute | solution.py:23
  33.1 3.7 %collective-permute-start.3 = (bf16[1,2,4,16,1792]{4,3,2,1,0:T(8,128)(2,1)S(1)}, bf16[1,2,4,16,1792]{4,3,2,1,0:T(8,128)(2,1)S(1)}, u32[]{:S(2)}, u32[]{:S(2)}) collective-permute-start(bf16[1,2,4,16,1792]{4,3,2,1,0:T(8,128)(2,1)S(1)} %get-tuple-element.32), channel_id=1, source_target_pairs={{0,7},{1,0},{2,1},{3,2},{4,3},{5,4},{6,5},{7,6},{8,15},{9,8},{10,9... | collective-permute-start | bytes 1376264 | tf_op jit(solution)/shard_map/ppermute | solution.py:23
  36.8 0.1 pad_maximum_fusion.2
  36.9 2.5 %collective-permute-start.10 = (bf16[2,2,4,16,1792]{4,3,2,1,0:T(8,128)(2,1)S(1)}, bf16[2,2,4,16,1792]{4,3,2,1,0:T(8,128)(2,1)S(1)}, u32[]{:S(2)}, u32[]{:S(2)}) collective-permute-start(bf16[2,2,4,16,1792]{4,3,2,1,0:T(8,128)(2,1)S(1)} %pad_maximum_fusion.2), channel_id=1, source_target_pairs={{0,24},{1,25},{2,26},{3,27},{4,28},{5,29},{6,30},{7,31},{8,16},{9,... | collective-permute-start | bytes 2752520 | tf_op jit(solution)/shard_map/ppermute | solution.py:23
  39.4 9.3 %collective-permute-done.6.refs_8_ = bf16[2,2,4,16,1792]{4,3,2,1,0:T(8,128)(2,1)S(1)} collective-permute-done((bf16[2,2,4,16,1792]{4,3,2,1,0:T(8,128)(2,1)S(1)}, bf16[2,2,4,16,1792]{4,3,2,1,0:T(8,128)(2,1)S(1)}, u32[]{:S(2)}, u32[]{:S(2)}) %collective-permute-start.6) | collective-permute-done | bytes 917536 | tf_op jit(solution)/shard_map/ppermute | solution.py:23
  48.7 2.4 %shard_map.67.refs_9_ = f32[14,8,256]{2,1,0:T(8,128)S(1)} custom-call(s32[1]{0:T(128)} %bitcast.8.late_ref, bf16[4,8,16,1792]{3,2,1,0:T(8,128)(2,1)S(1)} %copy-done, bf16[4,8,16,1792]{3,2,1,0:T(8,128)(2,1)S(1)} %copy-done.3, bf16[4,8,16,1792]{3,2,1,0:T(8,128)(2,1)S(1)} %copy-done.4, bf16[4,8,16,1792]{3,2,1,0:T(8,128)(2,1)S(1)} %copy-done.1, ...), custom_call_target="tpu_custom_call" | custom-call | flops 1 | bytes 1 | tf_op jit(solution)/shard_map/pallas_call | solution.py:164
  51.1 2.1 %collective-permute-start.7 = (f32[14,8,256]{2,1,0:T(8,128)S(1)}, f32[14,8,256]{2,1,0:T(8,128)S(1)}, u32[]{:S(2)}, u32[]{:S(2)}) collective-permute-start(f32[14,8,256]{2,1,0:T(8,128)S(1)} %shard_map.67.refs_9_), channel_id=1, source_target_pairs={{0,8},{1,9},{2,10},{3,11},{4,12},{5,13},{6,14},{7,15},{8,0},{9,1},... | collective-permute-start | bytes 344072 | tf_op jit(solution)/shard_map/ppermute | solution.py:23
  53.3 15.7 %collective-permute-done.10.refs_7_ = bf16[2,2,4,16,1792]{4,3,2,1,0:T(8,128)(2,1)S(1)} collective-permute-done((bf16[2,2,4,16,1792]{4,3,2,1,0:T(8,128)(2,1)S(1)}, bf16[2,2,4,16,1792]{4,3,2,1,0:T(8,128)(2,1)S(1)}, u32[]{:S(2)}, u32[]{:S(2)}) %collective-permute-start.10) | collective-permute-done | bytes 917536 | tf_op jit(solution)/shard_map/ppermute | solution.py:23
  68.9 1.4 %collective-permute-start.11 = (bf16[2,2,4,16,1792]{4,3,2,1,0:T(8,128)(2,1)S(1)}, bf16[2,2,4,16,1792]{4,3,2,1,0:T(8,128)(2,1)S(1)}, u32[]{:S(2)}, u32[]{:S(2)}) collective-permute-start(bf16[2,2,4,16,1792]{4,3,2,1,0:T(8,128)(2,1)S(1)} %constant_dynamic-update-slice_fusion.refs_4_), channel_id=1, source_target_pairs={{0,24},{1,25},{2,26},{3,27},{4,28},{5,29},{6,30},{7,31},{8,16},{9,... | collective-permute-start | bytes 2752520 | tf_op jit(solution)/shard_map/ppermute | solution.py:23
  70.4 1.7 %collective-permute-start.8 = (bf16[1,2,4,16,1792]{4,3,2,1,0:T(8,128)(2,1)S(1)}, bf16[1,2,4,16,1792]{4,3,2,1,0:T(8,128)(2,1)S(1)}, u32[]{:S(2)}, u32[]{:S(2)}) collective-permute-start(bf16[1,2,4,16,1792]{4,3,2,1,0:T(8,128)(2,1)S(1)} %get-tuple-element.34), channel_id=1, source_target_pairs={{0,7},{1,0},{2,1},{3,2},{4,3},{5,4},{6,5},{7,6},{8,15},{9,8},{10,9... | collective-permute-start | bytes 1376264 | tf_op jit(solution)/shard_map/ppermute | solution.py:23
  72.1 1.2 collective-permute-start.9
  73.3 5.2 %shard_map.68 = (bf16[3,2,4,16,1792]{4,3,2,1,0:T(8,128)(2,1)S(1)}, bf16[2,4,16,1792]{3,2,1,0:T(8,128)(2,1)S(1)}, bf16[2,2,4,16,1792]{4,3,2,1,0:T(8,128)(2,1)S(1)...) custom-call(s32[1]{0:T(128)} %bitcast.8.late_ref, bf16[4,8,16,1792]{3,2,1,0:T(8,128)(2,1)S(1)} %copy-done, ...), custom_call_target="tpu_custom_call" | custom-call | flops 1 | bytes 1 | tf_op jit(solution)/shard_map/pallas_call | solution.py:164
  78.5 0.1 collective-permute-start.17
  78.6 1.2 collective-permute-start.15
  79.8 7.9 %collective-permute-done.9.refs_6_ = bf16[1,2,4,16,1792]{4,3,2,1,0:T(8,128)(2,1)S(1)} collective-permute-done((bf16[1,2,4,16,1792]{4,3,2,1,0:T(8,128)(2,1)S(1)}, bf16[1,2,4,16,1792]{4,3,2,1,0:T(8,128)(2,1)S(1)}, u32[]{:S(2)}, u32[]{:S(2)}) %collective-permute-start.9) | collective-permute-done | bytes 458784 | tf_op jit(solution)/shard_map/ppermute | solution.py:23
  87.7 5.4 %collective-permute-done.11.refs_8_ = bf16[2,2,4,16,1792]{4,3,2,1,0:T(8,128)(2,1)S(1)} collective-permute-done((bf16[2,2,4,16,1792]{4,3,2,1,0:T(8,128)(2,1)S(1)}, bf16[2,2,4,16,1792]{4,3,2,1,0:T(8,128)(2,1)S(1)}, u32[]{:S(2)}, u32[]{:S(2)}) %collective-permute-start.11) | collective-permute-done | bytes 917536 | tf_op jit(solution)/shard_map/ppermute | solution.py:23
  93.1 2.4 %shard_map.69.refs_9_ = f32[14,8,256]{2,1,0:T(8,128)S(1)} custom-call(s32[1]{0:T(128)} %bitcast.late_ref, bf16[4,8,16,1792]{3,2,1,0:T(8,128)(2,1)S(1)} %copy-done, bf16[4,8,16,1792]{3,2,1,0:T(8,128)(2,1)S(1)} %copy-done.3, bf16[4,8,16,1792]{3,2,1,0:T(8,128)(2,1)S(1)} %copy-done.4, bf16[4,8,16,1792]{3,2,1,0:T(8,128)(2,1)S(1)} %copy-done.2, ...), custom_call_target="tpu_custom_call" | custom-call | flops 1 | bytes 1 | tf_op jit(solution)/shard_map/pallas_call | solution.py:164
  95.6 1.5 %collective-permute-start.12 = (f32[14,8,256]{2,1,0:T(8,128)S(1)}, f32[14,8,256]{2,1,0:T(8,128)S(1)}, u32[]{:S(2)}, u32[]{:S(2)}) collective-permute-start(f32[14,8,256]{2,1,0:T(8,128)S(1)} %shard_map.69.refs_9_), channel_id=1, source_target_pairs={{0,24},{1,25},{2,26},{3,27},{4,28},{5,29},{6,30},{7,31},{8,16},{9,... | collective-permute-start | bytes 344072 | tf_op jit(solution)/shard_map/ppermute | solution.py:23
  97.1 2.6 %collective-permute-done.15.refs_2_ = bf16[2,4,16,1792]{3,2,1,0:T(8,128)(2,1)S(1)} collective-permute-done((bf16[2,4,16,1792]{3,2,1,0:T(8,128)(2,1)S(1)}, bf16[2,4,16,1792]{3,2,1,0:T(8,128)(2,1)S(1)}, u32[]{:S(2)}, u32[]{:S(2)}) %collective-permute-start.15) | collective-permute-done | bytes 458784 | tf_op jit(solution)/shard_map/ppermute | solution.py:23
  99.7 2.4 %collective-permute-done.12.refs_10_ = f32[14,8,256]{2,1,0:T(8,128)S(1)} collective-permute-done((f32[14,8,256]{2,1,0:T(8,128)S(1)}, f32[14,8,256]{2,1,0:T(8,128)S(1)}, u32[]{:S(2)}, u32[]{:S(2)}) %collective-permute-start.12) | collective-permute-done | bytes 114720 | tf_op jit(solution)/shard_map/ppermute | solution.py:23
  102.1 5.2 %shard_map.70 = (bf16[3,2,4,16,1792]{4,3,2,1,0:T(8,128)(2,1)S(1)}, bf16[2,4,16,1792]{3,2,1,0:T(8,128)(2,1)S(1)}, bf16[2,4,16,1792]{3,2,1,0:T(8,128)(2,1)S(1)}, b...) custom-call(s32[1]{0:T(128)} %bitcast.late_ref, ...), custom_call_target="tpu_custom_call" | custom-call | flops 1 | bytes 1 | tf_op jit(solution)/shard_map/pallas_call | solution.py:164
  107.3 3.4 %collective-permute-start.13 = (bf16[2,4,16,1792]{3,2,1,0:T(8,128)(2,1)S(1)}, bf16[2,4,16,1792]{3,2,1,0:T(8,128)(2,1)S(1)}, u32[]{:S(2)}, u32[]{:S(2)}) collective-permute-start(bf16[2,4,16,1792]{3,2,1,0:T(8,128)(2,1)S(1)} %get-tuple-element.41), channel_id=1, source_target_pairs={{0,1},{1,2},{2,3},{3,4},{4,5},{5,6},{6,7},{7,0},{8,9},{9,10},{10,1... | collective-permute-start | bytes 1376264 | tf_op jit(solution)/shard_map/ppermute | solution.py:23
  110.7 0.1 collective-permute-start.20
  110.8 1.6 %collective-permute-start.21 = (bf16[2,4,16,1792]{3,2,1,0:T(8,128)(2,1)S(1)}, bf16[2,4,16,1792]{3,2,1,0:T(8,128)(2,1)S(1)}, u32[]{:S(2)}, u32[]{:S(2)}) collective-permute-start(bf16[2,4,16,1792]{3,2,1,0:T(8,128)(2,1)S(1)} %get-tuple-element.52), channel_id=1, source_target_pairs={{0,1},{1,2},{2,3},{3,4},{4,5},{5,6},{6,7},{7,0},{8,9},{9,10},{10,1... | collective-permute-start | bytes 1376264 | tf_op jit(solution)/shard_map/ppermute | solution.py:23
  112.4 0.5 collective-permute-start.14
  112.9 0.1 collective-permute-done.18.refs_3_
  113.0 1.9 %collective-permute-start.19 = (bf16[2,4,16,1792]{3,2,1,0:T(8,128)(2,1)S(1)}, bf16[2,4,16,1792]{3,2,1,0:T(8,128)(2,1)S(1)}, u32[]{:S(2)}, u32[]{:S(2)}) collective-permute-start(bf16[2,4,16,1792]{3,2,1,0:T(8,128)(2,1)S(1)} %get-tuple-element.49), channel_id=1, source_target_pairs={{0,25},{1,26},{2,27},{3,28},{4,29},{5,30},{6,31},{7,24},{8,17},{9,... | collective-permute-start | bytes 1376264 | tf_op jit(solution)/shard_map/ppermute | solution.py:23
  114.9 1.5 %shard_map.73 = (bf16[4,8,16,1792]{3,2,1,0:T(8,128)(2,1)}, bf16[4,8,16,1792]{3,2,1,0:T(8,128)(2,1)}) custom-call(s32[1]{0:T(128)} %bitcast.8.late_ref, bf16[3,2,4,16,1792]{4,3,2,1,0:T(8,128)(2,1)S(1)} %get-tuple-element.50.refs_0_, bf16[2,2,4,16,1792]{4,3,2,1,0:T(8,128)(2,1)S(1)} %collective-permute-done.17.refs_1_), custom_call_target="tpu_custom_call" | custom-call | flops 1 | bytes 1 | tf_op jit(solution)/shard_map/pallas_call | solution.py:164
  116.4 1.2 shard_map.71.refs_4_
  117.7 5.3 %collective-permute-done.20.refs_1_ = bf16[2,4,16,1792]{3,2,1,0:T(8,128)(2,1)S(1)} collective-permute-done((bf16[2,4,16,1792]{3,2,1,0:T(8,128)(2,1)S(1)}, bf16[2,4,16,1792]{3,2,1,0:T(8,128)(2,1)S(1)}, u32[]{:S(2)}, u32[]{:S(2)}) %collective-permute-start.20) | collective-permute-done | bytes 458784 | tf_op jit(solution)/shard_map/ppermute | solution.py:23
  122.9 4.9 %collective-permute-done.21.refs_2_ = bf16[2,4,16,1792]{3,2,1,0:T(8,128)(2,1)S(1)} collective-permute-done((bf16[2,4,16,1792]{3,2,1,0:T(8,128)(2,1)S(1)}, bf16[2,4,16,1792]{3,2,1,0:T(8,128)(2,1)S(1)}, u32[]{:S(2)}, u32[]{:S(2)}) %collective-permute-start.21) | collective-permute-done | bytes 458784 | tf_op jit(solution)/shard_map/ppermute | solution.py:23
  127.9 1.5 %shard_map.74 = (bf16[4,8,16,1792]{3,2,1,0:T(8,128)(2,1)}, bf16[4,8,16,1792]{3,2,1,0:T(8,128)(2,1)}) custom-call(s32[1]{0:T(128)} %bitcast.late_ref, bf16[3,2,4,16,1792]{4,3,2,1,0:T(8,128)(2,1)S(1)} %get-tuple-element.40.refs_0_, bf16[2,4,16,1792]{3,2,1,0:T(8,128)(2,1)S(1)} %collective-permute-done.20.refs_1_, ...), custom_call_target="tpu_custom_call", output_to_operand_aliasing={{0}: (4, {}), {1}: (5, {})} | custom-call | flops 1 | bytes 1 | tf_op jit(solution)/shard_map/pallas_call | solution.py:164
  129.4 3.4 %collective-permute-done.19.refs_3_ = bf16[2,4,16,1792]{3,2,1,0:T(8,128)(2,1)S(1)} collective-permute-done((bf16[2,4,16,1792]{3,2,1,0:T(8,128)(2,1)S(1)}, bf16[2,4,16,1792]{3,2,1,0:T(8,128)(2,1)S(1)}, u32[]{:S(2)}, u32[]{:S(2)}) %collective-permute-start.19) | collective-permute-done | bytes 458784 | tf_op jit(solution)/shard_map/ppermute | solution.py:23
  132.8 1.2 shard_map.72
  (22 shorter events, 0.1 us)
Async XLA Ops:
  2.9 6.3 %copy-start.3 = (bf16[4,8,16,1792]{3,2,1,0:T(8,128)(2,1)S(1)}, bf16[4,8,16,1792]{3,2,1,0:T(8,128)(2,1)}, u32[]{:S(2)}) copy-start(bf16[4,8,16,1792]{3,2,1,0:T(8,128)(2,1)} %refs_1_.7) | copy-start | bytes 5505028
  3.0 15.5 %collective-permute-start = (bf16[2,2,4,16,1792]{4,3,2,1,0:T(8,128)(2,1)S(1)}, bf16[2,2,4,16,1792]{4,3,2,1,0:T(8,128)(2,1)S(1)}, u32[]{:S(2)}, u32[]{:S(2)}) collective-permute-start(bf16[2,2,4,16,1792]{4,3,2,1,0:T(8,128)(2,1)S(1)} %pad_maximum_fusion), channel_id=1, source_target_pairs={{0,7},{1,0},{2,1},{3,2},{4,3},{5,4},{6,5},{7,6},{8,15},{9,8},{10,9... | collective-permute-start | bytes 2752520 | tf_op jit(solution)/shard_map/ppermute | solution.py:23
  7.6 1.7 %copy-start.4 = (bf16[4,8,16,1792]{3,2,1,0:T(8,128)(2,1)S(1)}, bf16[4,8,16,1792]{3,2,1,0:T(8,128)(2,1)}, u32[]{:S(2)}) copy-start(bf16[4,8,16,1792]{3,2,1,0:T(8,128)(2,1)} %refs_2_.7) | copy-start | bytes 5505028
  7.6 29.2 %collective-permute-start.5 = (bf16[2,2,4,16,1792]{4,3,2,1,0:T(8,128)(2,1)S(1)}, bf16[2,2,4,16,1792]{4,3,2,1,0:T(8,128)(2,1)S(1)}, u32[]{:S(2)}, u32[]{:S(2)}) collective-permute-start(bf16[2,2,4,16,1792]{4,3,2,1,0:T(8,128)(2,1)S(1)} %pad_maximum_fusion.1), channel_id=1, source_target_pairs={{0,8},{1,9},{2,10},{3,11},{4,12},{5,13},{6,14},{7,15},{8,0},{9,1},... | collective-permute-start | bytes 2752520 | tf_op jit(solution)/shard_map/ppermute | solution.py:23
  9.3 39.4 %copy-start = (bf16[4,8,16,1792]{3,2,1,0:T(8,128)(2,1)S(1)}, bf16[4,8,16,1792]{3,2,1,0:T(8,128)(2,1)}, u32[]{:S(2)}) copy-start(bf16[4,8,16,1792]{3,2,1,0:T(8,128)(2,1)} %refs_0_.7) | copy-start | bytes 5505028
  9.3 39.4 %copy-start.1 = (bf16[4,8,16,1792]{3,2,1,0:T(8,128)(2,1)S(1)}, bf16[4,8,16,1792]{3,2,1,0:T(8,128)(2,1)}, u32[]{:S(2)}) copy-start(bf16[4,8,16,1792]{3,2,1,0:T(8,128)(2,1)} %refs_3_.7) | copy-start | bytes 5505028
  18.5 9.7 %collective-permute-start.1 = (bf16[1,2,4,16,1792]{4,3,2,1,0:T(8,128)(2,1)S(1)}, bf16[1,2,4,16,1792]{4,3,2,1,0:T(8,128)(2,1)S(1)}, u32[]{:S(2)}, u32[]{:S(2)}) collective-permute-start(bf16[1,2,4,16,1792]{4,3,2,1,0:T(8,128)(2,1)S(1)} %get-tuple-element.30), channel_id=1, source_target_pairs={{0,7},{1,0},{2,1},{3,2},{4,3},{5,4},{6,5},{7,6},{8,15},{9,8},{10,9... | collective-permute-start | bytes 1376264 | tf_op jit(solution)/shard_map/ppermute | solution.py:23
  22.2 10.9 %collective-permute-start.2 = (bf16[1,2,4,16,1792]{4,3,2,1,0:T(8,128)(2,1)S(1)}, bf16[1,2,4,16,1792]{4,3,2,1,0:T(8,128)(2,1)S(1)}, u32[]{:S(2)}, u32[]{:S(2)}) collective-permute-start(bf16[1,2,4,16,1792]{4,3,2,1,0:T(8,128)(2,1)S(1)} %get-tuple-element.31), channel_id=1, source_target_pairs={{0,7},{1,0},{2,1},{3,2},{4,3},{5,4},{6,5},{7,6},{8,15},{9,8},{10,9... | collective-permute-start | bytes 1376264 | tf_op jit(solution)/shard_map/ppermute | solution.py:23
  22.2 26.5 %collective-permute-start.6 = (bf16[2,2,4,16,1792]{4,3,2,1,0:T(8,128)(2,1)S(1)}, bf16[2,2,4,16,1792]{4,3,2,1,0:T(8,128)(2,1)S(1)}, u32[]{:S(2)}, u32[]{:S(2)}) collective-permute-start(bf16[2,2,4,16,1792]{4,3,2,1,0:T(8,128)(2,1)S(1)} %collective-permute-done.refs_4_), channel_id=1, source_target_pairs={{0,8},{1,9},{2,10},{3,11},{4,12},{5,13},{6,14},{7,15},{8,0},{9,1},... | collective-permute-start | bytes 2752520 | tf_op jit(solution)/shard_map/ppermute | solution.py:23
  33.1 20.1 %collective-permute-start.3 = (bf16[1,2,4,16,1792]{4,3,2,1,0:T(8,128)(2,1)S(1)}, bf16[1,2,4,16,1792]{4,3,2,1,0:T(8,128)(2,1)S(1)}, u32[]{:S(2)}, u32[]{:S(2)}) collective-permute-start(bf16[1,2,4,16,1792]{4,3,2,1,0:T(8,128)(2,1)S(1)} %get-tuple-element.32), channel_id=1, source_target_pairs={{0,7},{1,0},{2,1},{3,2},{4,3},{5,4},{6,5},{7,6},{8,15},{9,8},{10,9... | collective-permute-start | bytes 1376264 | tf_op jit(solution)/shard_map/ppermute | solution.py:23
  36.9 32.1 %collective-permute-start.10 = (bf16[2,2,4,16,1792]{4,3,2,1,0:T(8,128)(2,1)S(1)}, bf16[2,2,4,16,1792]{4,3,2,1,0:T(8,128)(2,1)S(1)}, u32[]{:S(2)}, u32[]{:S(2)}) collective-permute-start(bf16[2,2,4,16,1792]{4,3,2,1,0:T(8,128)(2,1)S(1)} %pad_maximum_fusion.2), channel_id=1, source_target_pairs={{0,24},{1,25},{2,26},{3,27},{4,28},{5,29},{6,30},{7,31},{8,16},{9,... | collective-permute-start | bytes 2752520 | tf_op jit(solution)/shard_map/ppermute | solution.py:23
  39.4 13.8 %collective-permute-start.4 = (bf16[1,2,4,16,1792]{4,3,2,1,0:T(8,128)(2,1)S(1)}, bf16[1,2,4,16,1792]{4,3,2,1,0:T(8,128)(2,1)S(1)}, u32[]{:S(2)}, u32[]{:S(2)}) collective-permute-start(bf16[1,2,4,16,1792]{4,3,2,1,0:T(8,128)(2,1)S(1)} %get-tuple-element.33), channel_id=1, source_target_pairs={{0,7},{1,0},{2,1},{3,2},{4,3},{5,4},{6,5},{7,6},{8,15},{9,8},{10,9... | collective-permute-start | bytes 1376264 | tf_op jit(solution)/shard_map/ppermute | solution.py:23
  51.1 19.2 %collective-permute-start.7 = (f32[14,8,256]{2,1,0:T(8,128)S(1)}, f32[14,8,256]{2,1,0:T(8,128)S(1)}, u32[]{:S(2)}, u32[]{:S(2)}) collective-permute-start(f32[14,8,256]{2,1,0:T(8,128)S(1)} %shard_map.67.refs_9_), channel_id=1, source_target_pairs={{0,8},{1,9},{2,10},{3,11},{4,12},{5,13},{6,14},{7,15},{8,0},{9,1},... | collective-permute-start | bytes 344072 | tf_op jit(solution)/shard_map/ppermute | solution.py:23
  68.9 24.2 %collective-permute-start.11 = (bf16[2,2,4,16,1792]{4,3,2,1,0:T(8,128)(2,1)S(1)}, bf16[2,2,4,16,1792]{4,3,2,1,0:T(8,128)(2,1)S(1)}, u32[]{:S(2)}, u32[]{:S(2)}) collective-permute-start(bf16[2,2,4,16,1792]{4,3,2,1,0:T(8,128)(2,1)S(1)} %constant_dynamic-update-slice_fusion.refs_4_), channel_id=1, source_target_pairs={{0,24},{1,25},{2,26},{3,27},{4,28},{5,29},{6,30},{7,31},{8,16},{9,... | collective-permute-start | bytes 2752520 | tf_op jit(solution)/shard_map/ppermute | solution.py:23
  70.4 22.8 %copy-start.2 = (bf16[4,8,16,1792]{3,2,1,0:T(8,128)(2,1)S(1)}, bf16[4,8,16,1792]{3,2,1,0:T(8,128)(2,1)}, u32[]{:S(2)}) copy-start(bf16[4,8,16,1792]{3,2,1,0:T(8,128)(2,1)} %refs_3_.7) | copy-start | bytes 5505028
  70.4 9.4 %collective-permute-start.8 = (bf16[1,2,4,16,1792]{4,3,2,1,0:T(8,128)(2,1)S(1)}, bf16[1,2,4,16,1792]{4,3,2,1,0:T(8,128)(2,1)S(1)}, u32[]{:S(2)}, u32[]{:S(2)}) collective-permute-start(bf16[1,2,4,16,1792]{4,3,2,1,0:T(8,128)(2,1)S(1)} %get-tuple-element.34), channel_id=1, source_target_pairs={{0,7},{1,0},{2,1},{3,2},{4,3},{5,4},{6,5},{7,6},{8,15},{9,8},{10,9... | collective-permute-start | bytes 1376264 | tf_op jit(solution)/shard_map/ppermute | solution.py:23
  72.1 15.6 %collective-permute-start.9 = (bf16[1,2,4,16,1792]{4,3,2,1,0:T(8,128)(2,1)S(1)}, bf16[1,2,4,16,1792]{4,3,2,1,0:T(8,128)(2,1)S(1)}, u32[]{:S(2)}, u32[]{:S(2)}) collective-permute-start(bf16[1,2,4,16,1792]{4,3,2,1,0:T(8,128)(2,1)S(1)} %get-tuple-element.35), channel_id=1, source_target_pairs={{0,7},{1,0},{2,1},{3,2},{4,3},{5,4},{6,5},{7,6},{8,15},{9,8},{10,9... | collective-permute-start | bytes 1376264 | tf_op jit(solution)/shard_map/ppermute | solution.py:23
  78.5 21.2 %collective-permute-start.17 = (bf16[2,2,4,16,1792]{4,3,2,1,0:T(8,128)(2,1)S(1)}, bf16[2,2,4,16,1792]{4,3,2,1,0:T(8,128)(2,1)S(1)}, u32[]{:S(2)}, u32[]{:S(2)}) collective-permute-start(bf16[2,2,4,16,1792]{4,3,2,1,0:T(8,128)(2,1)S(1)} %get-tuple-element.47), channel_id=1, source_target_pairs={{0,1},{1,2},{2,3},{3,4},{4,5},{5,6},{6,7},{7,0},{8,9},{9,10},{10,1... | collective-permute-start | bytes 2752520 | tf_op jit(solution)/shard_map/ppermute | solution.py:23
  78.6 21.1 %collective-permute-start.15 = (bf16[2,4,16,1792]{3,2,1,0:T(8,128)(2,1)S(1)}, bf16[2,4,16,1792]{3,2,1,0:T(8,128)(2,1)S(1)}, u32[]{:S(2)}, u32[]{:S(2)}) collective-permute-start(bf16[2,4,16,1792]{3,2,1,0:T(8,128)(2,1)S(1)} %get-tuple-element.44), channel_id=1, source_target_pairs={{0,8},{1,9},{2,10},{3,11},{4,12},{5,13},{6,14},{7,15},{8,0},{9,1},... | collective-permute-start | bytes 1376264 | tf_op jit(solution)/shard_map/ppermute | solution.py:23
  87.7 12.0 %collective-permute-start.16 = (bf16[2,4,16,1792]{3,2,1,0:T(8,128)(2,1)S(1)}, bf16[2,4,16,1792]{3,2,1,0:T(8,128)(2,1)S(1)}, u32[]{:S(2)}, u32[]{:S(2)}) collective-permute-start(bf16[2,4,16,1792]{3,2,1,0:T(8,128)(2,1)S(1)} %get-tuple-element.46), channel_id=1, source_target_pairs={{0,1},{1,2},{2,3},{3,4},{4,5},{5,6},{6,7},{7,0},{8,9},{9,10},{10,1... | collective-permute-start | bytes 1376264 | tf_op jit(solution)/shard_map/ppermute | solution.py:23
  95.6 6.5 %collective-permute-start.12 = (f32[14,8,256]{2,1,0:T(8,128)S(1)}, f32[14,8,256]{2,1,0:T(8,128)S(1)}, u32[]{:S(2)}, u32[]{:S(2)}) collective-permute-start(f32[14,8,256]{2,1,0:T(8,128)S(1)} %shard_map.69.refs_9_), channel_id=1, source_target_pairs={{0,24},{1,25},{2,26},{3,27},{4,28},{5,29},{6,30},{7,31},{8,16},{9,... | collective-permute-start | bytes 344072 | tf_op jit(solution)/shard_map/ppermute | solution.py:23
  102.1 10.9 %collective-permute-start.18 = (bf16[2,4,16,1792]{3,2,1,0:T(8,128)(2,1)S(1)}, bf16[2,4,16,1792]{3,2,1,0:T(8,128)(2,1)S(1)}, u32[]{:S(2)}, u32[]{:S(2)}) collective-permute-start(bf16[2,4,16,1792]{3,2,1,0:T(8,128)(2,1)S(1)} %get-tuple-element.48), channel_id=1, source_target_pairs={{0,9},{1,10},{2,11},{3,12},{4,13},{5,14},{6,15},{7,8},{8,1},{9,2},... | collective-permute-start | bytes 1376264 | tf_op jit(solution)/shard_map/ppermute | solution.py:23
  107.3 22.0 %collective-permute-start.13 = (bf16[2,4,16,1792]{3,2,1,0:T(8,128)(2,1)S(1)}, bf16[2,4,16,1792]{3,2,1,0:T(8,128)(2,1)S(1)}, u32[]{:S(2)}, u32[]{:S(2)}) collective-permute-start(bf16[2,4,16,1792]{3,2,1,0:T(8,128)(2,1)S(1)} %get-tuple-element.41), channel_id=1, source_target_pairs={{0,1},{1,2},{2,3},{3,4},{4,5},{5,6},{6,7},{7,0},{8,9},{9,10},{10,1... | collective-permute-start | bytes 1376264 | tf_op jit(solution)/shard_map/ppermute | solution.py:23
  110.7 12.2 %collective-permute-start.20 = (bf16[2,4,16,1792]{3,2,1,0:T(8,128)(2,1)S(1)}, bf16[2,4,16,1792]{3,2,1,0:T(8,128)(2,1)S(1)}, u32[]{:S(2)}, u32[]{:S(2)}) collective-permute-start(bf16[2,4,16,1792]{3,2,1,0:T(8,128)(2,1)S(1)} %get-tuple-element.51), channel_id=1, source_target_pairs={{0,1},{1,2},{2,3},{3,4},{4,5},{5,6},{6,7},{7,0},{8,9},{9,10},{10,1... | collective-permute-start | bytes 1376264 | tf_op jit(solution)/shard_map/ppermute | solution.py:23
  110.8 17.1 %collective-permute-start.21 = (bf16[2,4,16,1792]{3,2,1,0:T(8,128)(2,1)S(1)}, bf16[2,4,16,1792]{3,2,1,0:T(8,128)(2,1)S(1)}, u32[]{:S(2)}, u32[]{:S(2)}) collective-permute-start(bf16[2,4,16,1792]{3,2,1,0:T(8,128)(2,1)S(1)} %get-tuple-element.52), channel_id=1, source_target_pairs={{0,1},{1,2},{2,3},{3,4},{4,5},{5,6},{6,7},{7,0},{8,9},{9,10},{10,1... | collective-permute-start | bytes 1376264 | tf_op jit(solution)/shard_map/ppermute | solution.py:23
  112.4 17.0 %collective-permute-start.14 = (bf16[2,4,16,1792]{3,2,1,0:T(8,128)(2,1)S(1)}, bf16[2,4,16,1792]{3,2,1,0:T(8,128)(2,1)S(1)}, u32[]{:S(2)}, u32[]{:S(2)}) collective-permute-start(bf16[2,4,16,1792]{3,2,1,0:T(8,128)(2,1)S(1)} %get-tuple-element.42), channel_id=1, source_target_pairs={{0,24},{1,25},{2,26},{3,27},{4,28},{5,29},{6,30},{7,31},{8,16},{9,... | collective-permute-start | bytes 1376264 | tf_op jit(solution)/shard_map/ppermute | solution.py:23
  113.0 19.8 %collective-permute-start.19 = (bf16[2,4,16,1792]{3,2,1,0:T(8,128)(2,1)S(1)}, bf16[2,4,16,1792]{3,2,1,0:T(8,128)(2,1)S(1)}, u32[]{:S(2)}, u32[]{:S(2)}) collective-permute-start(bf16[2,4,16,1792]{3,2,1,0:T(8,128)(2,1)S(1)} %get-tuple-element.49), channel_id=1, source_target_pairs={{0,25},{1,26},{2,27},{3,28},{4,29},{5,30},{6,31},{7,24},{8,17},{9,... | collective-permute-start | bytes 1376264 | tf_op jit(solution)/shard_map/ppermute | solution.py:23
